TPU v7x, 32 devices: a whole 2x2x4 slice. The times are simulated.
32 devices in a mesh: groups: 2 (over x), blk: 16 (over z, y, core).
Axes of the slice: x: 2, y: 2, z: 4, core: 2. Of those that a mesh axis runs over, the one named last changes fastest.
Arguments:
- projections: bfloat16 [2, 512, 8192], P(None, ('groups', 'blk')), parts along dimension 1, may hold values from -12 to 12
- images: bfloat16 [64, 8192], P(('groups', 'blk')), parts along dimension 0, may hold values from -16 to 16, as said below
- ctf_group: int32 [64], P(('groups', 'blk')), parts along dimension 0, may hold values from 0 to 15
- shift_offsets: int32 [64, 9, 2], P(('groups', 'blk')), parts along dimension 0, may hold values from -8 to 8
- shell_limit: int32 [64], P(('groups', 'blk')), parts along dimension 0, may hold values from 16 to 63
- ctf_table: float32 [32, 4096], P('groups'), parts along dimension 0, may hold values from -1 to 1
- noise_weight: float32 [32, 4096], P('groups'), parts along dimension 0, may hold values from 0.25 to 4
Outputs:
- slices: float32 [2, 512, 8192], P(None, ('groups', 'blk')), parts along dimension 1
- best_posterior: float32 [64], P(('groups', 'blk')), parts along dimension 0
- log_total: float32 [64], P(('groups', 'blk')), parts along dimension 0
There are 2 independent parts, one for each index of `groups`. A program takes and returns all parts, laid end to end along the dimension named above; each array names one. Nothing has to cross between parts.
Inputs may be any that keep to these rules, and one draw needn't show every extreme that they name: `images`: image coefficients.
All inputs are finite; a program needn't handle non-finite values.
Results may differ from a plain program's by a relative error of at most 0.006.
Values may be sent and summed in bfloat16 or wider, within the bound.
No kernel may reach another device: no remote copies, remote signals or barrier semaphores. Data moves between devices by JAX's collectives and lax.ppermute only.
A program may use at most 128 MiB of HBM per device.

v0:
```python
import math

import jax
import jax.numpy as jnp
from jax import lax
from jax.sharding import PartitionSpec as P

KY = 64
IMG = 256


def combined_all(value, axis, join):
    pieces = jax.tree.map(lambda part: lax.all_gather(part, axis), value)
    head = jax.tree.map(lambda part: part[0], pieces)
    tail = jax.tree.map(lambda part: part[1:], pieces)
    so_far, _ = lax.scan(lambda so_far, section: (join(so_far, section), None), head, tail)
    return so_far


def frequencies(half_width):
    positions = jnp.arange(half_width, dtype=jnp.int32)
    return (positions // KY, positions % KY - KY // 2)


def shift_factors(offsets, half_width):
    row_count = offsets.shape[0]
    shift_count = offsets.shape[1]
    row_freq = jnp.arange(half_width // KY, dtype=jnp.int32)
    col_freq = jnp.arange(KY, dtype=jnp.int32) - KY // 2
    turns_x = row_freq[None, None, :] * offsets[:, :, 0:1] % IMG
    turns_y = col_freq[None, None, :] * offsets[:, :, 1:2] % IMG
    angle_x = turns_x.astype(jnp.float32) * (2.0 * math.pi / IMG)
    angle_y = turns_y.astype(jnp.float32) * (2.0 * math.pi / IMG)
    cosine_x = jnp.cos(angle_x)[:, :, :, None]
    sine_x = jnp.sin(angle_x)[:, :, :, None]
    cosine_y = jnp.cos(angle_y)[:, :, None, :]
    sine_y = jnp.sin(angle_y)[:, :, None, :]
    cosine = cosine_x * cosine_y - sine_x * sine_y
    sine_part = sine_x * cosine_y + cosine_x * sine_y
    return (
        cosine.reshape(row_count, shift_count, half_width),
        sine_part.reshape(row_count, shift_count, half_width),
    )


def particle_terms(image_rows, ctf_rows, weight_rows, offsets, limits, freq_x, freq_y):
    half_width = image_rows.shape[1] // 2
    image_real = image_rows[:, :half_width].astype(jnp.float32)
    image_imag = image_rows[:, half_width:].astype(jnp.float32)
    radius_sq = freq_x * freq_x + freq_y * freq_y
    inside = (radius_sq[None, :] < (limits * limits)[:, None]).astype(jnp.float32)
    masked_weight = inside * weight_rows
    ctf_weight = masked_weight * ctf_rows
    norm_term = jnp.sum(masked_weight * (image_real * image_real + image_imag * image_imag), axis=1)
    quad_weight = ctf_weight * ctf_rows
    cosine, sine_part = shift_factors(offsets, half_width)
    shift_real = image_real[:, None, :] * cosine + image_imag[:, None, :] * sine_part
    shift_imag = image_imag[:, None, :] * cosine - image_real[:, None, :] * sine_part
    weighted = jnp.concatenate(
        [ctf_weight[:, None, :] * shift_real, ctf_weight[:, None, :] * shift_imag], axis=2
    ).astype(jnp.bfloat16)
    return (weighted, norm_term, quad_weight)


def combine_lse(first, second):
    score_top = jnp.maximum(first[0], second[0])
    exp_total = first[1] * jnp.exp(first[0] - score_top) + second[1] * jnp.exp(
        second[0] - score_top
    )
    return (score_top, exp_total)


def block_shape(row_count):
    return 64 if row_count % 64 == 0 else row_count


def split_rows(members, block_rows):
    return tuple(
        (
            member.reshape((member.shape[0] // block_rows, block_rows) + member.shape[1:])
            for member in members
        )
    )


def local(projections, images, ctf_group, shift_offsets, shell_limit, ctf_table, noise_weight):
    batch_count, orient_dev, full_width = projections.shape
    half_width = full_width // 2
    candidates = batch_count * orient_dev
    flat_proj = projections.reshape(candidates, full_width)
    proj_real = flat_proj[:, :half_width].astype(jnp.float32)
    proj_imag = flat_proj[:, half_width:].astype(jnp.float32)
    proj_power = proj_real * proj_real + proj_imag * proj_imag
    freq_x, freq_y = frequencies(half_width)
    score_scale = 0.5 / math.sqrt(half_width)
    group_count = ctf_table.shape[0]
    particles_dev = images.shape[0]

    def block_terms(members):
        image_rows, groups, offsets, limits = members
        one_hot = (groups[:, None] == jnp.arange(group_count, dtype=jnp.int32)[None, :]).astype(
            jnp.float32
        )
        ctf_rows = jnp.dot(
            one_hot, ctf_table, precision=lax.Precision.HIGHEST, preferred_element_type=jnp.float32
        )
        weight_rows = jnp.dot(
            one_hot,
            noise_weight,
            precision=lax.Precision.HIGHEST,
            preferred_element_type=jnp.float32,
        )
        return particle_terms(image_rows, ctf_rows, weight_rows, offsets, limits, freq_x, freq_y)

    def score_block(members):
        weighted, norm_term, quad_weight = block_terms(members)
        cross_term = lax.dot_general(
            weighted, flat_proj, (((2,), (1,)), ((), ())), preferred_element_type=jnp.float32
        )
        quad_term = lax.dot_general(
            quad_weight,
            proj_power,
            (((1,), (1,)), ((), ())),
            precision=lax.Precision.HIGHEST,
            preferred_element_type=jnp.float32,
        )
        return -(norm_term[:, None, None] - 2.0 * cross_term + quad_term[:, None, :]) * score_scale

    members = (
        lax.all_gather(images, "blk", axis=0, tiled=True),
        lax.all_gather(ctf_group, "blk", axis=0, tiled=True),
        lax.all_gather(shift_offsets, "blk", axis=0, tiled=True),
        lax.all_gather(shell_limit, "blk", axis=0, tiled=True),
    )
    row_count = members[0].shape[0]
    block_rows = block_shape(row_count)
    blocks = lax.map(score_block, split_rows(members, block_rows))
    scores = blocks.reshape((row_count,) + blocks.shape[2:])
    local_top = jnp.max(scores, axis=(1, 2))
    local_total = jnp.sum(jnp.exp(scores - local_top[:, None, None]), axis=(1, 2))
    score_top, exp_total = combined_all((local_top, local_total), "blk", combine_lse)
    log_total = score_top + jnp.log(exp_total)
    pieces = (
        lax.all_gather(images, "blk", axis=0, tiled=True),
        lax.all_gather(ctf_group, "blk", axis=0, tiled=True),
        lax.all_gather(shift_offsets, "blk", axis=0, tiled=True),
        lax.all_gather(shell_limit, "blk", axis=0, tiled=True),
    )
    row_count = pieces[0].shape[0]
    block_rows = block_shape(row_count)

    def add_block(carry, packed):
        member_block, score_block_values, log_block = packed
        weighted = block_terms(member_block)[0]
        posterior = jnp.exp(score_block_values - log_block[:, None, None]).astype(jnp.bfloat16)
        contrib = lax.dot_general(
            posterior, weighted, (((0, 1), (0, 1)), ((), ())), preferred_element_type=jnp.float32
        )
        return (carry + contrib, None)

    zero_slices = jnp.zeros((candidates, full_width), jnp.float32)
    packed_scores = split_rows((scores, log_total), block_rows)
    summed, unused_out = lax.scan(
        add_block, zero_slices, (split_rows(pieces, block_rows), packed_scores[0], packed_scores[1])
    )
    slices = (summed * (candidates / particles_dev)).reshape(batch_count, orient_dev, full_width)
    own_start = lax.axis_index("blk") * particles_dev
    own_top = lax.dynamic_slice_in_dim(score_top, own_start, particles_dev, 0)
    own_log = lax.dynamic_slice_in_dim(log_total, own_start, particles_dev, 0)
    best_posterior = jnp.exp(own_top - own_log)
    return (slices, best_posterior, own_log)


def solution(mesh):
    in_specs = (
        P(None, ("groups", "blk"), None),
        P(("groups", "blk"), None),
        P(("groups", "blk")),
        P(("groups", "blk"), None, None),
        P(("groups", "blk")),
        P("groups", None),
        P("groups", None),
    )
    out_specs = (P(None, ("groups", "blk"), None), P(("groups", "blk")), P(("groups", "blk")))
    return jax.shard_map(local, mesh=mesh, in_specs=in_specs, out_specs=out_specs, check_vma=False)
```

profile of v0, /device:TPU:0, one launch (start us, length us, event | category | flops | bytes accessed | tf_op | source)
XLA Modules:
  0.0 127.0 jit_solution(18370479021721928491)
XLA Ops:
  0.6 0.0 copy-start
  0.6 23.6 %all_gather.31 = s32[32,9,2]{1,2,0:T(2,128)S(1)} all-gather(s32[2,9,2]{1,2,0:T(2,128)} %param.12), channel_id=1, replica_groups=mesh['groups'=2,'blk'=16] {'blk'}, dimensions={0}, use_global_device_ids=true | all-gather | bytes 2448 | tf_op jit(solution)/shard_map/all_gather | solution.py:146
  24.2 0.1 copy.14
  24.3 0.1 copy.13
  24.4 1.2 fusion.32
  25.6 7.2 %multiply_subtract_fusion = (f32[32,9,64,64]{3,2,0,1:T(8,128)}, f32[32,9,64,64]{3,2,0,1:T(8,128)}) fusion(f32[32,9,64]{2,0,1:T(8,128)S(1)} %get-tuple-element.134, f32[32,9,64]{2,0,1:T(8,128)S(1)} %get-tuple-element.140, f32[32,9,64]{2,0,1:T(8,128)S(1)} %get-tuple-element.133, f32[32,9,64]{2,0,1:T(8,128)S(1)} %get-tuple-element.141), kind=kLoop, calls=%fused_computation.8 | loop fusion | flops 7077888 | bytes 9732096 | tf_op jit(solution)/shard_map/while/body/eval_jaxpr/sub | solution.py:38
  32.8 8.3 %add.127 = f32[32,9,4096]{2,0,1:T(8,128)} reshape(f32[32,9,64,64]{3,2,0,1:T(8,128)} %get-tuple-element.126) | data formatting | bytes 9437184 | tf_op jit(solution)/shard_map/while/body/eval_jaxpr/add | solution.py:39
  41.1 0.0 copy-start.4
  41.1 0.0 copy-start.7
  41.1 0.0 copy-start.5
  41.1 0.0 copy-start.6
  41.1 0.0 copy-start.2
  41.1 8.4 %sub.78 = f32[32,9,4096]{2,0,1:T(8,128)} reshape(f32[32,9,64,64]{3,2,0,1:T(8,128)} %get-tuple-element.125) | data formatting | bytes 9437184 | tf_op jit(solution)/shard_map/while/body/eval_jaxpr/sub | solution.py:38
  49.5 0.0 copy-done.4
  49.5 18.8 %all-gather.2 = bf16[16,2,8192]{2,1,0:T(2,128)(2,1)S(1)} all-gather(bf16[1,2,8192]{2,1,0:T(2,128)(2,1)S(1)} %bitcast.43), channel_id=1, replica_groups=mesh['groups'=2,'blk'=16] {'blk'}, dimensions={0}, use_global_device_ids=true | all-gather | bytes 557056 | tf_op jit(solution)/shard_map/all_gather | solution.py:144
  68.3 0.2 reshape.156
  68.5 0.9 slice_convert_fusion.1
  69.4 0.0 copy-done.7
  69.4 0.6 dynamic-slice.6
  70.7 0.0 copy-done.5
  70.7 0.2 dynamic-update-slice
  70.9 0.0 copy-done.6
  70.9 0.2 dynamic-update-slice.1
  71.1 9.5 %all-reduce.4 = (s32[32]{0:T(128)S(1)}, s32[32]{0:T(128)S(1)}) all-reduce(s32[32]{0:T(128)S(1)} %dynamic-update-slice, s32[32]{0:T(128)S(1)} %dynamic-update-slice.1), channel_id=1, replica_groups=mesh['groups'=2,'blk'=16] {'blk'}, use_global_device_ids=true, to_apply=%add | all-reduce | flops 64 | bytes 512
  80.6 0.0 copy-done.2
  80.6 0.4 fusion.46
  81.0 0.0 copy-done
  81.1 0.6 multiply_reduce_fusion
  81.7 0.0 copy-start.3
  81.7 4.7 %multiply_convert_fusion.1 = (bf16[32,9,4096]{2,0,1:T(8,128)(2,1)S(1)}, bf16[32,9,4096]{2,0,1:T(8,128)(2,1)S(1)}) fusion(f32[32,9,4096]{2,0,1:T(8,128)} %add.127, f32[32,9,4096]{2,0,1:T(8,128)} %sub.78, f32[32,4096]{1,0:T(8,128)} %get-tuple-element.130, f32[32,4096]{1,0:T(8,128)S(1)} %get-tuple-element.129, f32[32,4096]{1,0:T(8,128)S(1)} %get-tuple-element.128), kind=kLoop, calls=%fused_computation.13 | loop fusion | flops 11796480 | bytes 15728640 | tf_op jit(solution)/shard_map/convert
  86.3 0.0 copy-start.1
  86.4 0.0 copy-done.3
  86.4 0.6 fusion.12
  87.0 3.5 %fusion.53 = (f32[32]{0:T(128)S(1)}, f32[32,9,32]{0,2,1:T(8,128)S(1)}) fusion(f32[32,32]{0,1:T(8,128)S(1)} %fusion.12, bf16[32,8192,1]{1,0,2:T(8,128)(2,1)S(1)} %bitcast.40, bf16[32,9,4096]{2,0,1:T(8,128)(2,1)S(1)} %get-tuple-element.124, bf16[32,9,4096]{2,0,1:T(8,128)(2,1)S(1)} %get-tuple-element.123, f32[32]{0:T(128)S(1)} %get-tuple-element.127), kind=kOutput, calls=%fused_computation.82 | convolution fusion | flops 160487392 | bytes 5284096 | tf_op jit(solution)/shard_map/while/body/eval_jaxpr/dot_general | solution.py:117
  90.5 0.0 copy-done.1
  91.2 0.2 dynamic-update-slice.2
  91.4 0.1 exponential_reduce_fusion
  91.5 0.2 dynamic-update-slice.3
  91.7 30.1 %all-reduce.5 = (f32[512]{0:T(512)S(1)}, f32[512]{0:T(512)S(1)}) all-reduce(f32[512]{0:T(512)S(1)} %dynamic-update-slice.2, f32[512]{0:T(512)S(1)} %dynamic-update-slice.3), channel_id=2, replica_groups=mesh['groups'=2,'blk'=16] {'blk'}, use_global_device_ids=true, to_apply=%add.2 | all-reduce | flops 1024 | bytes 8192
  121.8 0.1 slice.54
  121.9 0.1 reshape.141
  122.0 0.1 slice.55
  122.0 0.1 reshape.142
  122.1 0.6 while.2
  122.7 3.6 %fusion.5 = f32[32,8192]{1,0:T(8,128)} fusion(bf16[32,9,4096]{2,0,1:T(8,128)(2,1)} %copy-done.1, bf16[32,9,4096]{2,0,1:T(8,128)(2,1)S(1)} %get-tuple-element.123, f32[32,9,32]{0,2,1:T(8,128)S(1)} %get-tuple-element.139, f32[32]{0:T(128)S(1)} %log_add_fusion), kind=kOutput, calls=%fused_computation.10 | convolution fusion | flops 160712704 | bytes 5804160 | tf_op jit(solution)/shard_map/while/body/eval_jaxpr/dot_general | solution.py:156
  126.4 0.6 subtract_exponential_fusion
  (26 shorter events, 0.5 us)
Async XLA Ops:
  0.6 80.4 %copy-start = (f32[16,4096]{1,0:T(8,128)S(1)}, f32[16,4096]{1,0:T(8,128)}, u32[]{:S(2)}) copy-start(f32[16,4096]{1,0:T(8,128)} %param.15) | copy-start | bytes 786436
  41.1 8.4 %copy-start.4 = (bf16[2,8192]{1,0:T(2,128)(2,1)S(1)}, bf16[2,8192]{1,0:T(2,128)(2,1)}, u32[]{:S(2)}) copy-start(bf16[2,8192]{1,0:T(2,128)(2,1)} %param.10) | copy-start | bytes 98308
  41.1 28.3 %copy-start.7 = (u32[32]{0:T(128)S(1)}, u32[32]{0:T(128)}, u32[]{:S(2)}) copy-start(u32[32]{0:T(128)} %constant.138) | copy-start | bytes 388
  41.1 29.5 %copy-start.5 = (s32[2]{0:T(128)S(1)}, s32[2]{0:T(128)}, u32[]{:S(2)}) copy-start(s32[2]{0:T(128)} %param.13) | copy-start | bytes 28
  41.1 29.8 %copy-start.6 = (s32[2]{0:T(128)S(1)}, s32[2]{0:T(128)}, u32[]{:S(2)}) copy-start(s32[2]{0:T(128)} %param.11) | copy-start | bytes 28
  41.1 39.5 %copy-start.2 = (f32[16,4096]{1,0:T(8,128)S(1)}, f32[16,4096]{1,0:T(8,128)}, u32[]{:S(2)}) copy-start(f32[16,4096]{1,0:T(8,128)} %param.14) | copy-start | bytes 786436
  81.7 4.7 %copy-start.3 = (bf16[2,16,8192]{2,1,0:T(8,128)(2,1)S(1)}, bf16[2,16,8192]{2,1,0:T(8,128)(2,1)}, u32[]{:S(2)}) copy-start(bf16[2,16,8192]{2,1,0:T(8,128)(2,1)} %param.9) | copy-start | bytes 1572868
  86.3 4.2 %copy-start.1 = (bf16[32,9,4096]{2,0,1:T(8,128)(2,1)}, bf16[32,9,4096]{2,0,1:T(8,128)(2,1)S(1)}, u32[]{:S(2)}) copy-start(bf16[32,9,4096]{2,0,1:T(8,128)(2,1)S(1)} %get-tuple-element.124) | copy-start | bytes 7077892
where the time goes:
time: 127 us
  blocking collectives  81.9 us (64%)
  local copies, waits for them, and re-layouts  18.9 us (15%)
  other arithmetic  15 us (12%)
  matrix products  8.79 us (7%)
  between operations  2.1 us (2%)
    unnamed x2, blocking collectives  39.5 us
    all_gather x1, blocking collectives, local(): lax.all_gather(shift_offsets, 'blk', axis=0, tiled=True)  23.6 us
    all_gather x1, blocking collectives, local(): lax.all_gather(images, 'blk', axis=0, tiled=True)  18.8 us
    sub x1, local copies, waits for them, and re-layouts, shift_factors(): cosine = cosine_x * cosine_y - sine_x * sine_y  8.36 us
    add x1, local copies, waits for them, and re-layouts, shift_factors(): sine_part = sine_x * cosine_y + cosine_x * sine_y  8.32 us
    sub x1, other arithmetic, shift_factors(): cosine = cosine_x * cosine_y - sine_x * sine_y  7.17 us
    another operation x1, other arithmetic  4.66 us
    dot_general x1, matrix products, add_block(): lax.dot_general(posterior, weighted, (((0, 1), (0, 1)), ((), ())), prefer...  3.63 us

commit v1 on v0

v1 whole, which is shorter than its diff:
```python
import functools
import math

import jax
import jax.numpy as jnp
from jax import lax
from jax.experimental import pallas as pl
from jax.experimental.pallas import tpu as pltpu
from jax.sharding import PartitionSpec as P

KY = 64
IMG = 256
LANES = 128
ROWS = 16
LIMIT_AT = 1
X_AT = 16
Y_AT = 48

VMEM = pl.BlockSpec(memory_space=pltpu.VMEM)
SMEM = pl.BlockSpec(memory_space=pltpu.SMEM)
NT = (((1,), (1,)), ((), ()))


def sin_cos(turns):
    quarter = IMG // 4
    wrapped = (turns + quarter // 2) & (IMG - 1)
    quadrant = wrapped >> int(math.log2(quarter))
    angle = (wrapped - quadrant * quarter - quarter // 2).astype(jnp.float32) * (
        2.0 * math.pi / IMG
    )
    square = angle * angle
    even = 1.0 + square * (
        -1.0 / 2 + square * (1.0 / 24 + square * (-1.0 / 720 + square * (1.0 / 40320)))
    )
    odd = angle * (
        1.0
        + square
        * (-1.0 / 6 + square * (1.0 / 120 + square * (-1.0 / 5040 + square * (1.0 / 362880))))
    )
    swapped = (quadrant & 1) == 1
    cosine = jnp.where(swapped, odd, even)
    sine = jnp.where(swapped, even, odd)
    cosine = jnp.where((quadrant == 1) | (quadrant == 2), -cosine, cosine)
    sine = jnp.where(quadrant >= 2, -sine, sine)
    return cosine, sine


def split_halves(value):
    high = value.astype(jnp.bfloat16)
    return high, (value - high.astype(jnp.float32)).astype(jnp.bfloat16)


def power_kernel(own_ref, other_ref, both_ref, high_ref, low_ref):
    rows, full = own_ref.shape
    half = full // 2
    for place, ref in enumerate((own_ref, other_ref)):
        at = pl.ds(place * rows, rows)
        both_ref[at, :] = ref[...]
        real = ref[:, :half].astype(jnp.float32)
        imag = ref[:, half:].astype(jnp.float32)
        high, low = split_halves(real * real + imag * imag)
        high_ref[at, :] = high
        low_ref[at, :] = low


def score_kernel(
    pieces_count,
    shifts,
    order_ref,
    *refs,
):
    pieces = refs[:pieces_count]
    both_ref, high_ref, low_ref, ctf_ref, noise_ref = refs[pieces_count : pieces_count + 5]
    weighted_ref, exps_ref, stats_ref = refs[pieces_count + 5 : pieces_count + 8]
    image_ref, real_ref, imag_ref, cross_ref, square_ref = refs[pieces_count + 8 :]
    half = ctf_ref.shape[1]
    full = 2 * half
    groups = ctf_ref.shape[0]
    candidates = both_ref.shape[0]
    particles = image_ref.shape[0]
    per_device = pieces[0].shape[1]
    scale = 0.5 / math.sqrt(half)
    place = 0
    for piece in pieces:
        for row in range(piece.shape[0]):
            start = order_ref[place] * per_device
            values = piece[row].astype(jnp.float32)
            for sub in range(per_device):
                image_ref[pl.ds(start + sub, 1), :] = values[sub : sub + 1]
            place += 1

    lane = lax.broadcasted_iota(jnp.int32, (ROWS, LANES), 1)
    block_rows = shifts * ROWS

    def block(index, carry):
        rows = pl.ds(pl.multiple_of(index * ROWS, ROWS), ROWS)
        first = pl.multiple_of(index * block_rows, ROWS)
        numbers = image_ref[rows, full:]
        one_hot = (
            numbers[:, :1].astype(jnp.int32)
            == lax.broadcasted_iota(jnp.int32, (ROWS, groups), 1)
        ).astype(jnp.float32)
        ctf = jnp.dot(
            one_hot,
            ctf_ref[...],
            precision=lax.Precision.HIGHEST,
            preferred_element_type=jnp.float32,
        )
        noise = jnp.dot(
            one_hot,
            noise_ref[...],
            precision=lax.Precision.HIGHEST,
            preferred_element_type=jnp.float32,
        )
        limit = numbers[:, LIMIT_AT : LIMIT_AT + 1].astype(jnp.int32)
        position = lax.broadcasted_iota(jnp.int32, (1, half), 1)
        freq_x = position // KY
        freq_y = position % KY - KY // 2
        weight = jnp.where(freq_x * freq_x + freq_y * freq_y < limit * limit, noise, 0.0)
        ctf_weight = weight * ctf
        real = image_ref[rows, :half]
        imag = image_ref[rows, half:full]
        norm = jnp.sum(weight * (real * real + imag * imag), axis=1, keepdims=True)
        real_ref[...] = ctf_weight * real
        imag_ref[...] = ctf_weight * imag
        quad_high, quad_low = split_halves(ctf_weight * ctf)
        quad_weight = jnp.concatenate([quad_high, quad_low], axis=0)
        quad = lax.dot_general(
            quad_weight, high_ref[...], NT, preferred_element_type=jnp.float32
        ) + lax.dot_general(quad_weight, low_ref[...], NT, preferred_element_type=jnp.float32)
        quad = quad[:ROWS] + quad[ROWS:]

        numbers_int = numbers.astype(jnp.int32)
        step_cos, step_sin = sin_cos(numbers_int * (LANES // KY))
        for shift in range(shifts):
            turns = (
                (lane // KY) * numbers_int[:, X_AT + shift : X_AT + shift + 1]
                + (lane % KY - KY // 2) * numbers_int[:, Y_AT + shift : Y_AT + shift + 1]
            )
            cosine, sine = sin_cos(turns)
            turn_cos = step_cos[:, X_AT + shift : X_AT + shift + 1]
            turn_sin = step_sin[:, X_AT + shift : X_AT + shift + 1]
            cosine_before = cosine * turn_cos + sine * turn_sin
            sine_before = sine * turn_cos - cosine * turn_sin
            double = jnp.broadcast_to(2.0 * turn_cos, (ROWS, LANES))
            out_rows = pl.ds(first + shift * ROWS, ROWS)
            for chunk in range(half // LANES):
                at = pl.ds(chunk * LANES, LANES)
                real = real_ref[:, at]
                imag = imag_ref[:, at]
                weighted_ref[out_rows, at] = (real * cosine + imag * sine).astype(jnp.bfloat16)
                weighted_ref[out_rows, pl.ds(half + chunk * LANES, LANES)] = (
                    imag * cosine - real * sine
                ).astype(jnp.bfloat16)
                cosine, cosine_before = double * cosine - cosine_before, cosine
                sine, sine_before = double * sine - sine_before, sine

        cross_ref[...] = lax.dot_general(
            weighted_ref[pl.ds(first, block_rows), :],
            both_ref[...],
            NT,
            preferred_element_type=jnp.float32,
        )
        base = norm + quad
        scores = [
            -(base - 2.0 * cross_ref[pl.ds(shift * ROWS, ROWS), :]) * scale
            for shift in range(shifts)
        ]
        top = jnp.max(functools.reduce(jnp.maximum, scores), axis=1, keepdims=True)
        exps = [jnp.exp(score - top) for score in scores]
        total = jnp.sum(functools.reduce(jnp.add, exps), axis=1, keepdims=True)
        top_wide = jnp.broadcast_to(top, (ROWS, LANES - candidates))
        total_wide = jnp.broadcast_to(total, (ROWS, LANES - candidates))
        spare = lax.broadcasted_iota(jnp.int32, top_wide.shape, 1)
        tail = jnp.where(spare == 0, top_wide, total_wide)
        for shift in range(shifts):
            square_ref[pl.ds(shift * ROWS, ROWS), :] = jnp.concatenate(
                [exps[shift], tail], axis=1
            )
        turned = square_ref[...].T
        exps_ref[index] = turned[:candidates, :block_rows]
        for target in range(stats_ref.shape[0]):
            stats_ref[target, index] = turned[candidates : candidates + 2, :block_rows]
        return carry

    lax.fori_loop(0, particles // ROWS, block, 0)


def slice_kernel(
    scale,
    own_ref,
    stats_ref,
    mine_ref,
    exps_ref,
    weighted_ref,
    keep_ref,
    send_ref,
    best_ref,
    log_ref,
    posterior_ref,
):
    blocks, candidates, block_rows = exps_ref.shape
    half_rows = candidates // 2
    per_device = best_ref.shape[0]
    for block in range(blocks):
        tops = stats_ref[:, block, 0, :]
        top = jnp.max(tops, axis=0, keepdims=True)
        total = jnp.sum(stats_ref[:, block, 1, :] * jnp.exp(tops - top), axis=0, keepdims=True)
        log_total = top + jnp.log(total)
        factor = jnp.exp(mine_ref[0, block, 0:1, :] - log_total)
        posterior_ref[block] = (exps_ref[block] * factor).astype(jnp.bfloat16)
        best = jnp.exp(top - log_total)
        column = lax.broadcasted_iota(jnp.int32, (1, block_rows), 1)
        for row in range(per_device):
            particle = own_ref[0] * per_device + row

            @pl.when(particle // ROWS == block)
            def _():
                chosen = column == particle % ROWS
                best_ref[row] = jnp.sum(jnp.where(chosen, best, 0.0))
                log_ref[row] = jnp.sum(jnp.where(chosen, log_total, 0.0))

    width = 1024
    for start in range(0, weighted_ref.shape[1], width):
        at = pl.ds(start, width)
        summed = jnp.zeros((candidates, width), jnp.float32)
        for block in range(blocks):
            summed = summed + jnp.dot(
                posterior_ref[block],
                weighted_ref[pl.ds(block * block_rows, block_rows), at],
                preferred_element_type=jnp.float32,
            )
        summed = summed * scale
        keep_ref[:, at] = summed[:half_rows]
        send_ref[:, at] = summed[half_rows:].astype(send_ref.dtype)


def local(
    axis_size, projections, images, ctf_group, shift_offsets, shell_limit, ctf_table, noise_weight
):
    batch_count, orient_dev, full = projections.shape
    half = full // 2
    own_rows = batch_count * orient_dev
    candidates = 2 * own_rows
    per_device = images.shape[0]
    shifts = shift_offsets.shape[1]
    chips = axis_size // 2
    particles = chips * per_device
    blocks = particles // ROWS
    block_rows = shifts * ROWS
    chip = lax.axis_index("blk") // 2
    params = pltpu.CompilerParams(vmem_limit_bytes=48 * 1024 * 1024)

    def swap(value, mask):
        return lax.ppermute(value, "blk", [(i, i ^ mask) for i in range(axis_size)])

    offsets = shift_offsets.astype(jnp.bfloat16)

    def at_column(value, column):
        return jnp.pad(value, ((0, 0), (column, LANES - column - value.shape[1])))

    numbers = (
        at_column(ctf_group[:, None].astype(jnp.bfloat16), 0)
        + at_column(shell_limit[:, None].astype(jnp.bfloat16), LIMIT_AT)
        + at_column(offsets[:, :, 0], X_AT)
        + at_column(offsets[:, :, 1], Y_AT)
    )
    packed = jnp.concatenate([images, numbers], axis=1)[None]
    if chips <= 8:
        pair = jnp.concatenate([packed, swap(packed, 2)], axis=0) if chips > 1 else packed
        pieces = [pair] + [swap(pair, mask) for mask in range(4, axis_size, 4)]
        order = jnp.arange(chips, dtype=jnp.int32) ^ chip
    else:
        same_core = [[2 * c + core for c in range(chips)] for core in range(2)]
        pieces = [
            lax.all_gather(packed, "blk", axis=0, tiled=True, axis_index_groups=same_core)
        ]
        order = jnp.arange(chips, dtype=jnp.int32)

    flat = projections.reshape(own_rows, full)
    other = swap(flat, 1)
    both, high, low = pl.pallas_call(
        power_kernel,
        out_shape=(
            jax.ShapeDtypeStruct((candidates, full), jnp.bfloat16),
            jax.ShapeDtypeStruct((candidates, half), jnp.bfloat16),
            jax.ShapeDtypeStruct((candidates, half), jnp.bfloat16),
        ),
        in_specs=[VMEM] * 2,
        out_specs=(VMEM,) * 3,
        compiler_params=params,
        cost_estimate=pl.CostEstimate(
            flops=8 * candidates * full, bytes_accessed=4 * candidates * full, transcendentals=0
        ),
        name="power",
    )(flat, other)

    weighted, exps, stats = pl.pallas_call(
        functools.partial(score_kernel, len(pieces), shifts),
        out_shape=(
            jax.ShapeDtypeStruct((blocks * block_rows, full), jnp.bfloat16),
            jax.ShapeDtypeStruct((blocks, candidates, block_rows), jnp.float32),
            jax.ShapeDtypeStruct((chips, blocks, 2, block_rows), jnp.float32),
        ),
        in_specs=[SMEM] + [VMEM] * (len(pieces) + 5),
        out_specs=(VMEM,) * 3,
        scratch_shapes=[
            pltpu.VMEM((particles, full + LANES), jnp.float32),
            pltpu.VMEM((ROWS, half), jnp.float32),
            pltpu.VMEM((ROWS, half), jnp.float32),
            pltpu.VMEM((block_rows, candidates), jnp.float32),
            pltpu.VMEM((-(-block_rows // LANES) * LANES, LANES), jnp.float32),
        ],
        compiler_params=params,
        name="scores",
    )(order, *pieces, both, high, low, ctf_table, noise_weight)

    same_core = [[2 * c + core for c in range(chips)] for core in range(2)]
    gathered = lax.all_to_all(stats, "blk", 0, 0, axis_index_groups=same_core)

    keep, send, best_posterior, log_total = pl.pallas_call(
        functools.partial(slice_kernel, own_rows / per_device),
        out_shape=(
            jax.ShapeDtypeStruct((own_rows, full), jnp.float32),
            jax.ShapeDtypeStruct((own_rows, full), jnp.float32),
            jax.ShapeDtypeStruct((per_device,), jnp.float32),
            jax.ShapeDtypeStruct((per_device,), jnp.float32),
        ),
        in_specs=[SMEM] + [VMEM] * 4,
        out_specs=(VMEM, VMEM, SMEM, SMEM),
        scratch_shapes=[pltpu.VMEM((blocks, candidates, block_rows), jnp.bfloat16)],
        compiler_params=params,
        name="slices",
    )(chip.reshape(1).astype(jnp.int32), gathered, stats, exps, weighted)

    slices = (keep + swap(send, 1)).reshape(batch_count, orient_dev, full)
    return (slices, best_posterior, log_total)


def solution(mesh):
    in_specs = (
        P(None, ("groups", "blk"), None),
        P(("groups", "blk"), None),
        P(("groups", "blk")),
        P(("groups", "blk"), None, None),
        P(("groups", "blk")),
        P("groups", None),
        P("groups", None),
    )
    out_specs = (P(None, ("groups", "blk"), None), P(("groups", "blk")), P(("groups", "blk")))
    return jax.shard_map(
        functools.partial(local, mesh.shape["blk"]),
        mesh=mesh,
        in_specs=in_specs,
        out_specs=out_specs,
        check_vma=False,
    )
```

time: 127 us -> 39.4 us (0.31)
  blocking collectives: 81.9 us -> 10.7 us
  local copies, waits for them, and re-layouts: 18.9 us -> 3.17 us
  other arithmetic: 15 us -> 4.08 us
  matrix products: 8.79 us -> 0 us
  starting transfers between devices: 0 us -> 7.92 us
  waiting for transfers between devices: 0 us -> 7.74 us
  Pallas kernels: 0 us -> 4.74 us
  between operations: 2.1 us -> 0.68 us
    all_gather x2 -> x0, blocking collectives: 42.4 us -> none  [the longest x1 23.6 us: local(): lax.all_gather(shift_offsets, 'blk', axis=0, tiled=True)]
    unnamed x2 -> x0, blocking collectives: 39.5 us -> none
    all_to_all x0 -> x1, blocking collectives: none -> 10.7 us  [local(): gathered = lax.all_to_all(stats, 'blk', 0, 0, axis_index_groups=same_core)]
    dot_general x5 -> x0, matrix products: 8.79 us -> none  [the longest x1 3.63 us: add_block(): lax.dot_general(posterior, weighted, (((0, 1), (0, 1)), ((), ())), prefer...]
    sub x1 -> x0, local copies, waits for them, and re-layouts: 8.36 us -> none  [shift_factors(): cosine = cosine_x * cosine_y - sine_x * sine_y]
    add x1 -> x0, local copies, waits for them, and re-layouts: 8.32 us -> none  [shift_factors(): sine_part = sine_x * cosine_y + cosine_x * sine_y]
    ppermute x0 -> x6, starting transfers between devices: none -> 7.92 us  [swap(): return lax.ppermute(value, 'blk', [(i, i ^ mask) for i in range(axis_size)])]
    ppermute x0 -> x6, waiting for transfers between devices: none -> 7.74 us  [swap(): return lax.ppermute(value, 'blk', [(i, i ^ mask) for i in range(axis_size)])]
  transfers between devices with their start and end apart: 0 -> 6, of which waited for: 0 -> 4; matrix products, arithmetic and copies ran while one was open for 0% -> 0% of each run, Pallas kernels for 0% -> 1%
where the time goes in v1:
time: 39.4 us; the launch traced here: 39.1 us
  blocking collectives  10.7 us (27%)
  starting transfers between devices  7.92 us (20%)
  waiting for transfers between devices  7.74 us (20%)
  Pallas kernels  4.74 us (12%)
  other arithmetic  4.08 us (10%)
  local copies, waits for them, and re-layouts  3.17 us (8%)
  between operations  0.68 us (2%)
    all_to_all x1, blocking collectives, local(): gathered = lax.all_to_all(stats, 'blk', 0, 0, axis_index_groups=same_core)  10.7 us
    ppermute x6, starting transfers between devices, swap(): return lax.ppermute(value, 'blk', [(i, i ^ mask) for i in range(axis_size)])  7.92 us
    ppermute x6, waiting for transfers between devices, swap(): return lax.ppermute(value, 'blk', [(i, i ^ mask) for i in range(axis_size)])  7.74 us
    pallas_call x1, Pallas kernels, local(): pl.pallas_call(functools.partial(score_kernel, len(pieces), shifts), out_...  3.57 us
    unnamed x7, local copies, waits for them, and re-layouts  2.95 us
    add x1, other arithmetic, local(): slices = (keep + swap(send, 1)).reshape(batch_count, orient_dev, full)  1.12 us
    pallas_call x1, Pallas kernels, local(): pl.pallas_call(functools.partial(slice_kernel, own_rows / per_device), ou...  0.83 us
    broadcast_in_dim x1, other arithmetic, local(): packed = jnp.concatenate([images, numbers], axis=1)[None]  0.79 us
  transfers between devices with their start and end apart: 6, of which 4 were waited for; matrix products, arithmetic and copies ran while one was open for 0% of the time, Pallas kernels for 1%

profile of v1, /device:TPU:0, one launch (start us, length us, event | category | flops | bytes accessed | tf_op | source)
XLA Modules:
  0.0 39.1 jit_solution(10087281807035910930)
XLA Ops:
  0.6 0.7 %convert_bitcast_fusion.1 = bf16[2,1]{0,1:T(2,128)(2,1)S(1)} fusion(s32[2]{0:T(128)} %param.9), kind=kLoop, calls=%fused_computation.6 | loop fusion | flops 2 | bytes 12 | tf_op jit(solution)/shard_map/convert_element_type | solution.py:263
  1.3 0.1 copy.12
  1.4 0.7 %convert_bitcast_fusion = bf16[2,1]{0,1:T(2,128)(2,1)S(1)} fusion(s32[2]{0:T(128)} %param.11), kind=kLoop, calls=%fused_computation.5 | loop fusion | flops 2 | bytes 12 | tf_op jit(solution)/shard_map/convert_element_type | solution.py:264
  2.1 0.1 copy.13
  2.2 0.7 %convert_element_type.27 = bf16[2,9,2]{1,2,0:T(2,128)(2,1)S(1)} convert(s32[2,9,2]{1,2,0:T(2,128)} %param.10) | non-fusion elementwise | flops 36 | bytes 216 | tf_op jit(solution)/shard_map/convert_element_type | solution.py:257
  2.9 0.1 pad_add_fusion
  2.9 0.8 %maximum_bitcast_fusion = bf16[1,2,8320]{2,1,0:T(2,128)(2,1)S(1)} fusion(bf16[2,128]{1,0:T(2,128)(2,1)S(1)} %pad_add_fusion, bf16[2,8192]{1,0:T(2,128)(2,1)} %param.8), kind=kLoop, calls=%fused_computation.1 | loop fusion | flops 66560 | bytes 66560 | tf_op jit(solution)/shard_map/broadcast_in_dim | solution.py:268
  3.7 3.0 %collective-permute-start = (bf16[1,2,8320]{2,1,0:T(2,128)(2,1)S(1)}, bf16[1,2,8320]{2,1,0:T(2,128)(2,1)S(1)}, u32[]{:S(2)}, u32[]{:S(2)}) collective-permute-start(bf16[1,2,8320]{2,1,0:T(2,128)(2,1)S(1)} %maximum_bitcast_fusion), channel_id=1, source_target_pairs={{0,2},{1,3},{2,0},{3,1},{4,6},{5,7},{6,4},{7,5},{8,10},{9,11},{10,... | collective-permute-start | bytes 99848 | tf_op jit(solution)/shard_map/ppermute | solution.py:255
  6.8 0.0 collective-permute-start.4
  6.8 1.9 %collective-permute-done = bf16[1,2,8320]{2,1,0:T(2,128)(2,1)S(1)} collective-permute-done((bf16[1,2,8320]{2,1,0:T(2,128)(2,1)S(1)}, bf16[1,2,8320]{2,1,0:T(2,128)(2,1)S(1)}, u32[]{:S(2)}, u32[]{:S(2)}) %collective-permute-start) | collective-permute-done | bytes 33312 | tf_op jit(solution)/shard_map/ppermute | solution.py:255
  8.7 0.1 pad_maximum_fusion.refs_0_
  8.8 4.2 %collective-permute-start.3 = (bf16[2,2,8320]{2,1,0:T(2,128)(2,1)S(1)}, bf16[2,2,8320]{2,1,0:T(2,128)(2,1)S(1)}, u32[]{:S(2)}, u32[]{:S(2)}) collective-permute-start(bf16[2,2,8320]{2,1,0:T(2,128)(2,1)S(1)} %pad_maximum_fusion.refs_0_), channel_id=1, source_target_pairs={{0,12},{1,13},{2,14},{3,15},{4,8},{5,9},{6,10},{7,11},{8,4},{9,5},... | collective-permute-start | bytes 199688 | tf_op jit(solution)/shard_map/ppermute | solution.py:255
  12.9 0.0 collective-permute-start.2
  12.9 0.6 %collective-permute-start.1 = (bf16[2,2,8320]{2,1,0:T(2,128)(2,1)S(1)}, bf16[2,2,8320]{2,1,0:T(2,128)(2,1)S(1)}, u32[]{:S(2)}, u32[]{:S(2)}) collective-permute-start(bf16[2,2,8320]{2,1,0:T(2,128)(2,1)S(1)} %pad_maximum_fusion.refs_0_), channel_id=1, source_target_pairs={{0,4},{1,5},{2,6},{3,7},{4,0},{5,1},{6,2},{7,3},{8,12},{9,13},{10,... | collective-permute-start | bytes 199688 | tf_op jit(solution)/shard_map/ppermute | solution.py:255
  13.6 0.0 collective-permute-done.4.other_ref
  13.6 0.0 copy-start
  13.6 1.0 %copy-done = bf16[2,16,8192]{2,1,0:T(8,128)(2,1)S(1)} copy-done((bf16[2,16,8192]{2,1,0:T(8,128)(2,1)S(1)}, bf16[2,16,8192]{2,1,0:T(8,128)(2,1)}, u32[]{:S(2)}) %copy-start) | copy-done | bytes 524312
  14.6 0.3 power.1
  15.0 0.4 %collective-permute-done.3.refs_3_ = bf16[2,2,8320]{2,1,0:T(2,128)(2,1)S(1)} collective-permute-done((bf16[2,2,8320]{2,1,0:T(2,128)(2,1)S(1)}, bf16[2,2,8320]{2,1,0:T(2,128)(2,1)S(1)}, u32[]{:S(2)}, u32[]{:S(2)}) %collective-permute-start.3) | collective-permute-done | bytes 66592 | tf_op jit(solution)/shard_map/ppermute | solution.py:255
  15.4 2.8 %collective-permute-done.2.refs_2_ = bf16[2,2,8320]{2,1,0:T(2,128)(2,1)S(1)} collective-permute-done((bf16[2,2,8320]{2,1,0:T(2,128)(2,1)S(1)}, bf16[2,2,8320]{2,1,0:T(2,128)(2,1)S(1)}, u32[]{:S(2)}, u32[]{:S(2)}) %collective-permute-start.2) | collective-permute-done | bytes 66592 | tf_op jit(solution)/shard_map/ppermute | solution.py:255
  18.2 0.0 collective-permute-done.1.refs_1_
  18.2 0.0 copy-start.1
  18.2 0.9 %copy-done.1 = f32[16,4096]{1,0:T(8,128)S(1)} copy-done((f32[16,4096]{1,0:T(8,128)S(1)}, f32[16,4096]{1,0:T(8,128)}, u32[]{:S(2)}) %copy-start.1) | copy-done | bytes 262168
  19.1 0.0 copy-start.2
  19.1 0.9 %copy-done.2 = f32[16,4096]{1,0:T(8,128)S(1)} copy-done((f32[16,4096]{1,0:T(8,128)S(1)}, f32[16,4096]{1,0:T(8,128)}, u32[]{:S(2)}) %copy-start.2) | copy-done | bytes 262168
  20.1 3.6 %scores.1 = (bf16[144,8192]{1,0:T(8,128)(2,1)S(1)}, f32[1,64,144]{2,1,0:T(8,128)S(1)}, f32[8,1,2,144]{3,2,1,0:T(2,128)S(1)}) custom-call(s32[8]{0:T(128)S(1)} %iota_xor_fusion.order_ref, bf16[2,2,8320]{2,1,0:T(2,128)(2,1)S(1)} %pad_maximum_fusion.refs_0_, bf16[2,2,8320]{2,1,0:T(2,128)(2,1)S(1)} %collective-permute-done.1.refs_1_, ...), custom_call_target="tpu_custom_call" | custom-call | tf_op jit(solution)/shard_map/scores/pallas_call | solution.py:298
  23.6 10.7 %all_to_all.5.stats_ref = f32[8,1,2,144]{3,2,1,0:T(2,128)S(1)} all-to-all(f32[8,1,2,144]{3,2,1,0:T(2,128)S(1)} %get-tuple-element.16.mine_ref), channel_id=1, replica_groups={{0,2,4,6,8,10,12,14},{1,3,5,7,9,11,13,15},{16,18,20,22,24,26,28,30},{17..., dimensions={0} | all-to-all | bytes 18432 | tf_op jit(solution)/shard_map/all_to_all | solution.py:319
  34.4 0.8 %slices.1 = (f32[32,8192]{1,0:T(8,128)S(1)}, f32[32,8192]{1,0:T(8,128)S(1)}, f32[2]{0:T(128)}, f32[2]{0:T(128)}) custom-call(s32[1]{0:T(128)} %bitcast.own_ref, f32[8,1,2,144]{3,2,1,0:T(2,128)S(1)} %all_to_all.5.stats_ref, f32[8,1,2,144]{3,2,1,0:T(2,128)S(1)} %get-tuple-element.16.mine_ref, f32[1,64,144]{2,1,0:T(8,128)S(1)} %get-tuple-element.17.exps_ref, ...), custom_call_target="tpu_custom_call" | custom-call | tf_op jit(solution)/shard_map/slices/pallas_call | solution.py:321
  35.2 0.1 collective-permute-start.5
  35.3 2.6 %collective-permute-done.5 = f32[32,8192]{1,0:T(8,128)S(1)} collective-permute-done((f32[32,8192]{1,0:T(8,128)S(1)}, f32[32,8192]{1,0:T(8,128)S(1)}, u32[]{:S(2)}, u32[]{:S(2)}) %collective-permute-start.5) | collective-permute-done | bytes 1048608 | tf_op jit(solution)/shard_map/ppermute | solution.py:255
  38.0 1.1 %add.24 = f32[32,8192]{1,0:T(8,128)} add(f32[32,8192]{1,0:T(8,128)S(1)} %get-tuple-element.19, f32[32,8192]{1,0:T(8,128)S(1)} %collective-permute-done.5) | non-fusion elementwise | flops 262144 | bytes 3145728 | tf_op jit(solution)/shard_map/add | solution.py:336
  (3 shorter events, 0.0 us)
Async XLA Ops:
  3.7 4.9 %collective-permute-start = (bf16[1,2,8320]{2,1,0:T(2,128)(2,1)S(1)}, bf16[1,2,8320]{2,1,0:T(2,128)(2,1)S(1)}, u32[]{:S(2)}, u32[]{:S(2)}) collective-permute-start(bf16[1,2,8320]{2,1,0:T(2,128)(2,1)S(1)} %maximum_bitcast_fusion), channel_id=1, source_target_pairs={{0,2},{1,3},{2,0},{3,1},{4,6},{5,7},{6,4},{7,5},{8,10},{9,11},{10,... | collective-permute-start | bytes 99848 | tf_op jit(solution)/shard_map/ppermute | solution.py:255
  6.8 6.8 %collective-permute-start.4 = (bf16[32,8192]{1,0:T(8,128)(2,1)}, bf16[32,8192]{1,0:T(8,128)(2,1)S(1)}, u32[]{:S(2)}, u32[]{:S(2)}) collective-permute-start(bf16[32,8192]{1,0:T(8,128)(2,1)} %bitcast.13), channel_id=1, source_target_pairs={{0,1},{1,0},{2,3},{3,2},{4,5},{5,4},{6,7},{7,6},{8,9},{9,8},{10,11... | collective-permute-start | bytes 1572872 | tf_op jit(solution)/shard_map/ppermute | solution.py:255
  8.8 6.6 %collective-permute-start.3 = (bf16[2,2,8320]{2,1,0:T(2,128)(2,1)S(1)}, bf16[2,2,8320]{2,1,0:T(2,128)(2,1)S(1)}, u32[]{:S(2)}, u32[]{:S(2)}) collective-permute-start(bf16[2,2,8320]{2,1,0:T(2,128)(2,1)S(1)} %pad_maximum_fusion.refs_0_), channel_id=1, source_target_pairs={{0,12},{1,13},{2,14},{3,15},{4,8},{5,9},{6,10},{7,11},{8,4},{9,5},... | collective-permute-start | bytes 199688 | tf_op jit(solution)/shard_map/ppermute | solution.py:255
  12.9 5.2 %collective-permute-start.2 = (bf16[2,2,8320]{2,1,0:T(2,128)(2,1)S(1)}, bf16[2,2,8320]{2,1,0:T(2,128)(2,1)S(1)}, u32[]{:S(2)}, u32[]{:S(2)}) collective-permute-start(bf16[2,2,8320]{2,1,0:T(2,128)(2,1)S(1)} %pad_maximum_fusion.refs_0_), channel_id=1, source_target_pairs={{0,8},{1,9},{2,10},{3,11},{4,12},{5,13},{6,14},{7,15},{8,0},{9,1},... | collective-permute-start | bytes 199688 | tf_op jit(solution)/shard_map/ppermute | solution.py:255
  12.9 5.2 %collective-permute-start.1 = (bf16[2,2,8320]{2,1,0:T(2,128)(2,1)S(1)}, bf16[2,2,8320]{2,1,0:T(2,128)(2,1)S(1)}, u32[]{:S(2)}, u32[]{:S(2)}) collective-permute-start(bf16[2,2,8320]{2,1,0:T(2,128)(2,1)S(1)} %pad_maximum_fusion.refs_0_), channel_id=1, source_target_pairs={{0,4},{1,5},{2,6},{3,7},{4,0},{5,1},{6,2},{7,3},{8,12},{9,13},{10,... | collective-permute-start | bytes 199688 | tf_op jit(solution)/shard_map/ppermute | solution.py:255
  13.6 1.0 %copy-start = (bf16[2,16,8192]{2,1,0:T(8,128)(2,1)S(1)}, bf16[2,16,8192]{2,1,0:T(8,128)(2,1)}, u32[]{:S(2)}) copy-start(bf16[2,16,8192]{2,1,0:T(8,128)(2,1)} %param.7) | copy-start | bytes 1572868
  18.2 1.0 %copy-start.1 = (f32[16,4096]{1,0:T(8,128)S(1)}, f32[16,4096]{1,0:T(8,128)}, u32[]{:S(2)}) copy-start(f32[16,4096]{1,0:T(8,128)} %refs_7_.1) | copy-start | bytes 786436
  19.1 0.9 %copy-start.2 = (f32[16,4096]{1,0:T(8,128)S(1)}, f32[16,4096]{1,0:T(8,128)}, u32[]{:S(2)}) copy-start(f32[16,4096]{1,0:T(8,128)} %refs_8_.1) | copy-start | bytes 786436
  35.2 2.7 %collective-permute-start.5 = (f32[32,8192]{1,0:T(8,128)S(1)}, f32[32,8192]{1,0:T(8,128)S(1)}, u32[]{:S(2)}, u32[]{:S(2)}) collective-permute-start(f32[32,8192]{1,0:T(8,128)S(1)} %get-tuple-element.20), channel_id=1, source_target_pairs={{0,1},{1,0},{2,3},{3,2},{4,5},{5,4},{6,7},{7,6},{8,9},{9,8},{10,11... | collective-permute-start | bytes 3145736 | tf_op jit(solution)/shard_map/ppermute | solution.py:255

commit v2 on v1

--- a/solution.py
+++ b/solution.py
@@ -17,6 +17,7 @@
 Y_AT = 48
 
 VMEM = pl.BlockSpec(memory_space=pltpu.VMEM)
+HBM = pl.BlockSpec(memory_space=pltpu.HBM)
 SMEM = pl.BlockSpec(memory_space=pltpu.SMEM)
 NT = (((1,), (1,)), ((), ()))
 
@@ -50,32 +51,88 @@
     return high, (value - high.astype(jnp.float32)).astype(jnp.bfloat16)
 
 
-def power_kernel(own_ref, other_ref, both_ref, high_ref, low_ref):
-    rows, full = own_ref.shape
+def pack_kernel(images_hbm, group_hbm, limit_hbm, offsets_hbm, packed_ref, group, limit, offsets, sems):
+    per_device, full = images_hbm.shape
+    shifts = offsets_hbm.shape[2]
+    copies = [
+        pltpu.make_async_copy(images_hbm, packed_ref.at[0, :, pl.ds(0, full)], sems.at[0]),
+        pltpu.make_async_copy(group_hbm, group, sems.at[1]),
+        pltpu.make_async_copy(limit_hbm, limit, sems.at[2]),
+        pltpu.make_async_copy(offsets_hbm, offsets, sems.at[3]),
+    ]
+    for copy in copies:
+        copy.start()
+    for copy in copies[1:]:
+        copy.wait()
+    row = lax.broadcasted_iota(jnp.int32, (per_device, LANES), 0)
+    lane = lax.broadcasted_iota(jnp.int32, (per_device, LANES), 1)
+    numbers = jnp.zeros((per_device, LANES), jnp.int32)
+    for particle in range(per_device):
+        line = jnp.zeros((per_device, LANES), jnp.int32)
+        line = jnp.where(lane == 0, group[particle], line)
+        line = jnp.where(lane == LIMIT_AT, limit[particle], line)
+        for shift in range(shifts):
+            line = jnp.where(lane == X_AT + shift, offsets[particle, 0, shift], line)
+            line = jnp.where(lane == Y_AT + shift, offsets[particle, 1, shift], line)
+        numbers = jnp.where(row == particle, line, numbers)
+    packed_ref[0, :, pl.ds(full, LANES)] = numbers.astype(jnp.float32).astype(jnp.bfloat16)
+    copies[0].wait()
+
+
+def split_thirds(value):
+    high = value.astype(jnp.bfloat16)
+    rest = value - high.astype(jnp.float32)
+    middle = rest.astype(jnp.bfloat16)
+    return high, middle, (rest - middle.astype(jnp.float32)).astype(jnp.bfloat16)
+
+
+def power_kernel(
+    own_hbm,
+    other_ref,
+    ctf_hbm,
+    noise_hbm,
+    both_ref,
+    high_ref,
+    low_ref,
+    table_ref,
+    ctf_ref,
+    noise_ref,
+    sems,
+):
+    rows, full = other_ref.shape
     half = full // 2
-    for place, ref in enumerate((own_ref, other_ref)):
+    groups = ctf_ref.shape[0]
+    copies = [
+        pltpu.make_async_copy(own_hbm, both_ref.at[pl.ds(0, rows)], sems.at[0]),
+        pltpu.make_async_copy(ctf_hbm, ctf_ref, sems.at[1]),
+        pltpu.make_async_copy(noise_hbm, noise_ref, sems.at[2]),
+    ]
+    for copy in copies:
+        copy.start()
+    both_ref[pl.ds(rows, rows), :] = other_ref[...]
+    for place in (1, 0):
         at = pl.ds(place * rows, rows)
-        both_ref[at, :] = ref[...]
-        real = ref[:, :half].astype(jnp.float32)
-        imag = ref[:, half:].astype(jnp.float32)
+        if place == 0:
+            copies[0].wait()
+        real = both_ref[at, :half].astype(jnp.float32)
+        imag = both_ref[at, half:].astype(jnp.float32)
         high, low = split_halves(real * real + imag * imag)
         high_ref[at, :] = high
         low_ref[at, :] = low
-
-
-def score_kernel(
-    pieces_count,
-    shifts,
-    order_ref,
-    *refs,
-):
+    for place, ref in enumerate((ctf_ref, noise_ref)):
+        copies[1 + place].wait()
+        for third, part in enumerate(split_thirds(ref[...])):
+            table_ref[pl.ds(third * groups, groups), pl.ds(place * half, half)] = part
+
+
+def score_kernel(pieces_count, shifts, by_distance, place_ref, *refs):
     pieces = refs[:pieces_count]
-    both_ref, high_ref, low_ref, ctf_ref, noise_ref = refs[pieces_count : pieces_count + 5]
-    weighted_ref, exps_ref, stats_ref = refs[pieces_count + 5 : pieces_count + 8]
+    both_ref, high_ref, low_ref, table_ref = refs[pieces_count : pieces_count + 4]
+    weighted_ref, exps_ref, exps_other_ref, stats_ref = refs[pieces_count + 4 : pieces_count + 8]
     image_ref, real_ref, imag_ref, cross_ref, square_ref = refs[pieces_count + 8 :]
-    half = ctf_ref.shape[1]
-    full = 2 * half
-    groups = ctf_ref.shape[0]
+    full = both_ref.shape[1]
+    half = full // 2
+    groups = table_ref.shape[0] // 3
     candidates = both_ref.shape[0]
     particles = image_ref.shape[0]
     per_device = pieces[0].shape[1]
@@ -83,7 +140,8 @@
     place = 0
     for piece in pieces:
         for row in range(piece.shape[0]):
-            start = order_ref[place] * per_device
+            source = place_ref[0] ^ place if by_distance else place
+            start = source * per_device
             values = piece[row].astype(jnp.float32)
             for sub in range(per_device):
                 image_ref[pl.ds(start + sub, 1), :] = values[sub : sub + 1]
@@ -96,22 +154,11 @@
         rows = pl.ds(pl.multiple_of(index * ROWS, ROWS), ROWS)
         first = pl.multiple_of(index * block_rows, ROWS)
         numbers = image_ref[rows, full:]
-        one_hot = (
-            numbers[:, :1].astype(jnp.int32)
-            == lax.broadcasted_iota(jnp.int32, (ROWS, groups), 1)
-        ).astype(jnp.float32)
-        ctf = jnp.dot(
-            one_hot,
-            ctf_ref[...],
-            precision=lax.Precision.HIGHEST,
-            preferred_element_type=jnp.float32,
-        )
-        noise = jnp.dot(
-            one_hot,
-            noise_ref[...],
-            precision=lax.Precision.HIGHEST,
-            preferred_element_type=jnp.float32,
-        )
+        column = lax.broadcasted_iota(jnp.int32, (ROWS, 3 * groups), 1) % groups
+        one_hot = (numbers[:, :1].astype(jnp.int32) == column).astype(jnp.bfloat16)
+        tables = jnp.dot(one_hot, table_ref[...], preferred_element_type=jnp.float32)
+        ctf = tables[:, :half]
+        noise = tables[:, half:]
         limit = numbers[:, LIMIT_AT : LIMIT_AT + 1].astype(jnp.int32)
         position = lax.broadcasted_iota(jnp.int32, (1, half), 1)
         freq_x = position // KY
@@ -178,7 +225,8 @@
                 [exps[shift], tail], axis=1
             )
         turned = square_ref[...].T
-        exps_ref[index] = turned[:candidates, :block_rows]
+        exps_ref[index] = turned[: candidates // 2, :block_rows]
+        exps_other_ref[index] = turned[candidates // 2 : candidates, :block_rows]
         for target in range(stats_ref.shape[0]):
             stats_ref[target, index] = turned[candidates : candidates + 2, :block_rows]
         return carry
@@ -188,51 +236,65 @@
 
 def slice_kernel(
     scale,
-    own_ref,
+    place_ref,
     stats_ref,
-    mine_ref,
-    exps_ref,
-    weighted_ref,
-    keep_ref,
-    send_ref,
+    exps_own_ref,
+    exps_other_ref,
+    weighted_own_ref,
+    weighted_other_ref,
+    out_hbm,
     best_ref,
     log_ref,
     posterior_ref,
+    summed_ref,
+    sems,
 ):
-    blocks, candidates, block_rows = exps_ref.shape
-    half_rows = candidates // 2
+    blocks, rows, block_rows = exps_own_ref.shape
+    chips = stats_ref.shape[0]
     per_device = best_ref.shape[0]
-    for block in range(blocks):
-        tops = stats_ref[:, block, 0, :]
-        top = jnp.max(tops, axis=0, keepdims=True)
-        total = jnp.sum(stats_ref[:, block, 1, :] * jnp.exp(tops - top), axis=0, keepdims=True)
-        log_total = top + jnp.log(total)
-        factor = jnp.exp(mine_ref[0, block, 0:1, :] - log_total)
-        posterior_ref[block] = (exps_ref[block] * factor).astype(jnp.bfloat16)
-        best = jnp.exp(top - log_total)
-        column = lax.broadcasted_iota(jnp.int32, (1, block_rows), 1)
-        for row in range(per_device):
-            particle = own_ref[0] * per_device + row
-
-            @pl.when(particle // ROWS == block)
-            def _():
-                chosen = column == particle % ROWS
-                best_ref[row] = jnp.sum(jnp.where(chosen, best, 0.0))
-                log_ref[row] = jnp.sum(jnp.where(chosen, log_total, 0.0))
+    full = out_hbm.shape[1]
+    for side, exps_ref in enumerate((exps_own_ref, exps_other_ref)):
+        core = place_ref[1] if side == 0 else 1 - place_ref[1]
+        for block in range(blocks):
+            tops = [stats_ref[source, core, block, 0:1, :] for source in range(chips)]
+            totals = [stats_ref[source, core, block, 1:2, :] for source in range(chips)]
+            top = functools.reduce(jnp.maximum, tops)
+            total = functools.reduce(
+                jnp.add, [part * jnp.exp(high - top) for high, part in zip(tops, totals)]
+            )
+            log_total = top + jnp.log(total)
+            factor = jnp.exp(stats_ref[place_ref[0], core, block, 0:1, :] - log_total)
+            posterior_ref[side, block] = (exps_ref[block] * factor).astype(jnp.bfloat16)
+            if side == 0:
+                best = jnp.exp(top - log_total)
+                column = lax.broadcasted_iota(jnp.int32, (1, block_rows), 1)
+                for row in range(per_device):
+                    particle = place_ref[0] * per_device + row
+
+                    @pl.when(particle // ROWS == block)
+                    def _():
+                        chosen = column == particle % ROWS
+                        best_ref[row] = jnp.sum(jnp.where(chosen, best, 0.0))
+                        log_ref[row] = jnp.sum(jnp.where(chosen, log_total, 0.0))
 
     width = 1024
-    for start in range(0, weighted_ref.shape[1], width):
+    copies = []
+    for number, start in enumerate(range(0, full, width)):
         at = pl.ds(start, width)
-        summed = jnp.zeros((candidates, width), jnp.float32)
-        for block in range(blocks):
-            summed = summed + jnp.dot(
-                posterior_ref[block],
-                weighted_ref[pl.ds(block * block_rows, block_rows), at],
-                preferred_element_type=jnp.float32,
-            )
-        summed = summed * scale
-        keep_ref[:, at] = summed[:half_rows]
-        send_ref[:, at] = summed[half_rows:].astype(send_ref.dtype)
+        summed = jnp.zeros((rows, width), jnp.float32)
+        for side, weighted_ref in enumerate((weighted_own_ref, weighted_other_ref)):
+            for block in range(blocks):
+                summed = summed + jnp.dot(
+                    posterior_ref[side, block],
+                    weighted_ref[pl.ds(block * block_rows, block_rows), at],
+                    preferred_element_type=jnp.float32,
+                )
+        summed_ref[:, at] = summed * scale
+        copy = pltpu.make_async_copy(summed_ref.at[:, at], out_hbm.at[:, at], sems.at[number])
+        copy.start()
+        copies.append(copy)
+    for copy in copies:
+        copy.wait()
 
 
 def local(
@@ -248,62 +310,73 @@
     particles = chips * per_device
     blocks = particles // ROWS
     block_rows = shifts * ROWS
-    chip = lax.axis_index("blk") // 2
-    params = pltpu.CompilerParams(vmem_limit_bytes=48 * 1024 * 1024)
+    index = lax.axis_index("blk")
+    place = jnp.stack([index >> 1, index & 1])
+    megabytes = 12 + -(-2 * blocks * block_rows * full * 2 // 2**20)
+    params = pltpu.CompilerParams(vmem_limit_bytes=megabytes * 2**20)
 
     def swap(value, mask):
         return lax.ppermute(value, "blk", [(i, i ^ mask) for i in range(axis_size)])
 
-    offsets = shift_offsets.astype(jnp.bfloat16)
-
-    def at_column(value, column):
-        return jnp.pad(value, ((0, 0), (column, LANES - column - value.shape[1])))
-
-    numbers = (
-        at_column(ctf_group[:, None].astype(jnp.bfloat16), 0)
-        + at_column(shell_limit[:, None].astype(jnp.bfloat16), LIMIT_AT)
-        + at_column(offsets[:, :, 0], X_AT)
-        + at_column(offsets[:, :, 1], Y_AT)
-    )
-    packed = jnp.concatenate([images, numbers], axis=1)[None]
-    if chips <= 8:
+    packed = pl.pallas_call(
+        pack_kernel,
+        out_shape=jax.ShapeDtypeStruct((1, per_device, full + LANES), jnp.bfloat16),
+        in_specs=[HBM] * 4,
+        out_specs=VMEM,
+        scratch_shapes=[
+            pltpu.SMEM((per_device,), jnp.int32),
+            pltpu.SMEM((per_device,), jnp.int32),
+            pltpu.SMEM((per_device, 2, shifts), jnp.int32),
+            pltpu.SemaphoreType.DMA((4,)),
+        ],
+        compiler_params=pltpu.CompilerParams(vmem_limit_bytes=60 * 2**20),
+        name="pack",
+    )(images, ctf_group, shell_limit, shift_offsets.transpose(0, 2, 1))
+    by_distance = chips <= 8
+    if by_distance:
         pair = jnp.concatenate([packed, swap(packed, 2)], axis=0) if chips > 1 else packed
         pieces = [pair] + [swap(pair, mask) for mask in range(4, axis_size, 4)]
-        order = jnp.arange(chips, dtype=jnp.int32) ^ chip
     else:
         same_core = [[2 * c + core for c in range(chips)] for core in range(2)]
         pieces = [
             lax.all_gather(packed, "blk", axis=0, tiled=True, axis_index_groups=same_core)
         ]
-        order = jnp.arange(chips, dtype=jnp.int32)
 
     flat = projections.reshape(own_rows, full)
     other = swap(flat, 1)
-    both, high, low = pl.pallas_call(
+    groups = ctf_table.shape[0]
+    both, high, low, tables = pl.pallas_call(
         power_kernel,
         out_shape=(
             jax.ShapeDtypeStruct((candidates, full), jnp.bfloat16),
             jax.ShapeDtypeStruct((candidates, half), jnp.bfloat16),
             jax.ShapeDtypeStruct((candidates, half), jnp.bfloat16),
+            jax.ShapeDtypeStruct((3 * groups, full), jnp.bfloat16),
         ),
-        in_specs=[VMEM] * 2,
-        out_specs=(VMEM,) * 3,
+        in_specs=[HBM, VMEM, HBM, HBM],
+        out_specs=(VMEM,) * 4,
+        scratch_shapes=[
+            pltpu.VMEM((groups, half), jnp.float32),
+            pltpu.VMEM((groups, half), jnp.float32),
+            pltpu.SemaphoreType.DMA((3,)),
+        ],
         compiler_params=params,
         cost_estimate=pl.CostEstimate(
             flops=8 * candidates * full, bytes_accessed=4 * candidates * full, transcendentals=0
         ),
         name="power",
-    )(flat, other)
-
-    weighted, exps, stats = pl.pallas_call(
-        functools.partial(score_kernel, len(pieces), shifts),
+    )(flat, other, ctf_table, noise_weight)
+
+    weighted, exps, exps_other, stats = pl.pallas_call(
+        functools.partial(score_kernel, len(pieces), shifts, by_distance),
         out_shape=(
             jax.ShapeDtypeStruct((blocks * block_rows, full), jnp.bfloat16),
-            jax.ShapeDtypeStruct((blocks, candidates, block_rows), jnp.float32),
-            jax.ShapeDtypeStruct((chips, blocks, 2, block_rows), jnp.float32),
+            jax.ShapeDtypeStruct((blocks, own_rows, block_rows), jnp.float32),
+            jax.ShapeDtypeStruct((blocks, own_rows, block_rows), jnp.float32),
+            jax.ShapeDtypeStruct((axis_size, blocks, 2, block_rows), jnp.float32),
         ),
-        in_specs=[SMEM] + [VMEM] * (len(pieces) + 5),
-        out_specs=(VMEM,) * 3,
+        in_specs=[SMEM] + [VMEM] * (len(pieces) + 4),
+        out_specs=(VMEM,) * 4,
         scratch_shapes=[
             pltpu.VMEM((particles, full + LANES), jnp.float32),
             pltpu.VMEM((ROWS, half), jnp.float32),
@@ -313,28 +386,31 @@
         ],
         compiler_params=params,
         name="scores",
-    )(order, *pieces, both, high, low, ctf_table, noise_weight)
-
-    same_core = [[2 * c + core for c in range(chips)] for core in range(2)]
-    gathered = lax.all_to_all(stats, "blk", 0, 0, axis_index_groups=same_core)
-
-    keep, send, best_posterior, log_total = pl.pallas_call(
+    )(place, *pieces, both, high, low, tables)
+
+    weighted_other = swap(weighted, 1)
+    exps_in = swap(exps_other, 1)
+    gathered = lax.all_to_all(stats, "blk", 0, 0)
+    gathered = gathered.reshape((chips, 2) + gathered.shape[1:])
+
+    slices, best_posterior, log_total = pl.pallas_call(
         functools.partial(slice_kernel, own_rows / per_device),
         out_shape=(
-            jax.ShapeDtypeStruct((own_rows, full), jnp.float32),
             jax.ShapeDtypeStruct((own_rows, full), jnp.float32),
             jax.ShapeDtypeStruct((per_device,), jnp.float32),
             jax.ShapeDtypeStruct((per_device,), jnp.float32),
         ),
-        in_specs=[SMEM] + [VMEM] * 4,
-        out_specs=(VMEM, VMEM, SMEM, SMEM),
-        scratch_shapes=[pltpu.VMEM((blocks, candidates, block_rows), jnp.bfloat16)],
+        in_specs=[SMEM] + [VMEM] * 5,
+        out_specs=(HBM, SMEM, SMEM),
+        scratch_shapes=[
+            pltpu.VMEM((2, blocks, own_rows, block_rows), jnp.bfloat16),
+            pltpu.VMEM((own_rows, full), jnp.float32),
+            pltpu.SemaphoreType.DMA((full // 1024,)),
+        ],
         compiler_params=params,
         name="slices",
-    )(chip.reshape(1).astype(jnp.int32), gathered, stats, exps, weighted)
-
-    slices = (keep + swap(send, 1)).reshape(batch_count, orient_dev, full)
-    return (slices, best_posterior, log_total)
+    )(place, gathered, exps, exps_in, weighted, weighted_other)
+    return (slices.reshape(batch_count, orient_dev, full), best_posterior, log_total)
 
 
 def solution(mesh):

time: 39.4 us -> 38 us (0.964)
  blocking collectives: 10.7 us -> 0 us
  starting transfers between devices: 7.92 us -> 13.6 us
  Pallas kernels: 4.74 us -> 10.1 us
  other arithmetic: 4.08 us -> 0.94 us
  waiting for transfers between devices: 7.74 us -> 9.18 us
    all_to_all x1 -> x0, blocking collectives: 10.7 us -> none  [local(): gathered = lax.all_to_all(stats, 'blk', 0, 0, axis_index_groups=same_core)]
    all_to_all x0 -> x1, starting transfers between devices: none -> 5.37 us  [local(): gathered = lax.all_to_all(stats, 'blk', 0, 0)]
    all_to_all x0 -> x1, waiting for transfers between devices: none -> 5.36 us  [local(): gathered = lax.all_to_all(stats, 'blk', 0, 0)]
    ppermute x6 -> x7, waiting for transfers between devices: 7.74 us -> 3.83 us  [swap(): return lax.ppermute(value, 'blk', [(i, i ^ mask) for i in range(axis_size)])]
    pallas_call x1, Pallas kernels: 0.83 us -> 4.03 us  [local(): pl.pallas_call(functools.partial(slice_kernel, own_rows / per_device), ou...]
    convert_element_type x3 -> x0, other arithmetic: 2 us -> none  [the longest x1 0.68 us: local(): offsets = shift_offsets.astype(jnp.bfloat16)]
    pallas_call x1 -> x2, Pallas kernels: 3.57 us -> 5.42 us  [the longest x1 3.91 us: local(): pl.pallas_call(functools.partial(score_kernel, len(pieces), shifts, by_di...]
    add x2 -> x0, other arithmetic: 1.2 us -> none  [the longest x1 1.12 us: local(): slices = (keep + swap(send, 1)).reshape(batch_count, orient_dev, full)]
  transfers between devices with their start and end apart: 6 -> 8, of which waited for: 4 -> 4; matrix products, arithmetic and copies ran while one was open for 0% -> 3% of each run, Pallas kernels for 1% -> 2%
where the time goes in v2:
time: 38 us; the launch traced here: 37.5 us
  starting transfers between devices  13.6 us (36%)
  Pallas kernels  10.1 us (27%)
  waiting for transfers between devices  9.18 us (24%)
  local copies, waits for them, and re-layouts  2.94 us (8%)
  other arithmetic  0.94 us (2%)
  between operations  0.68 us (2%)
    ppermute x7, starting transfers between devices, swap(): return lax.ppermute(value, 'blk', [(i, i ^ mask) for i in range(axis_size)])  8.26 us
    all_to_all x1, starting transfers between devices, local(): gathered = lax.all_to_all(stats, 'blk', 0, 0)  5.37 us
    all_to_all x1, waiting for transfers between devices, local(): gathered = lax.all_to_all(stats, 'blk', 0, 0)  5.36 us
    pallas_call x1, Pallas kernels, local(): pl.pallas_call(functools.partial(slice_kernel, own_rows / per_device), ou...  4.03 us
    pallas_call x1, Pallas kernels, local(): pl.pallas_call(functools.partial(score_kernel, len(pieces), shifts, by_di...  3.91 us
    ppermute x7, waiting for transfers between devices, swap(): return lax.ppermute(value, 'blk', [(i, i ^ mask) for i in range(axis_size)])  3.83 us
    unnamed x6, local copies, waits for them, and re-layouts  2.94 us
    pallas_call x1, Pallas kernels, local(): pl.pallas_call(pack_kernel, out_shape=jax.ShapeDtypeStruct((1, per_device...  1.51 us
  transfers between devices with their start and end apart: 8, of which 4 were waited for; matrix products, arithmetic and copies ran while one was open for 3% of the time, Pallas kernels for 2%

profile of v2, /device:TPU:0, one launch (start us, length us, event | category | flops | bytes accessed | tf_op | source)
XLA Modules:
  0.0 37.5 jit_solution(4740785739969753248)
XLA Ops:
  0.6 1.5 %pack.1 = bf16[1,2,8320]{2,1,0:T(2,128)(2,1)} custom-call(bf16[2,8192]{1,0:T(2,128)(2,1)} %images_hbm.1, s32[2]{0:T(128)} %group_hbm.1, s32[2]{0:T(128)} %limit_hbm.1, s32[2,2,9]{2,1,0:T(2,128)} %bitcast.9), custom_call_target="tpu_custom_call" | custom-call | tf_op jit(solution)/shard_map/pack/pallas_call | solution.py:321
  2.1 3.0 %collective-permute-start = (bf16[1,2,8320]{2,1,0:T(2,128)(2,1)}, bf16[1,2,8320]{2,1,0:T(2,128)(2,1)S(1)}, u32[]{:S(2)}, u32[]{:S(2)}) collective-permute-start(bf16[1,2,8320]{2,1,0:T(2,128)(2,1)} %pack.1), channel_id=1, source_target_pairs={{0,2},{1,3},{2,0},{3,1},{4,6},{5,7},{6,4},{7,5},{8,10},{9,11},{10,... | collective-permute-start | bytes 99848 | tf_op jit(solution)/shard_map/ppermute | solution.py:319
  5.2 0.0 collective-permute-start.4
  5.2 2.1 %collective-permute-done = bf16[1,2,8320]{2,1,0:T(2,128)(2,1)S(1)} collective-permute-done((bf16[1,2,8320]{2,1,0:T(2,128)(2,1)}, bf16[1,2,8320]{2,1,0:T(2,128)(2,1)S(1)}, u32[]{:S(2)}, u32[]{:S(2)}) %collective-permute-start) | collective-permute-done | bytes 33312 | tf_op jit(solution)/shard_map/ppermute | solution.py:319
  7.3 0.9 %pad_maximum_fusion.refs_0_ = bf16[2,2,8320]{2,1,0:T(2,128)(2,1)S(1)} fusion(bf16[1,2,8320]{2,1,0:T(2,128)(2,1)S(1)} %collective-permute-done, bf16[1,2,8320]{2,1,0:T(2,128)(2,1)} %pack.1), kind=kLoop, calls=%fused_computation | loop fusion | flops 33280 | bytes 133120 | tf_op jit(solution)/shard_map/concatenate | solution.py:337
  8.2 4.2 %collective-permute-start.3 = (bf16[2,2,8320]{2,1,0:T(2,128)(2,1)S(1)}, bf16[2,2,8320]{2,1,0:T(2,128)(2,1)S(1)}, u32[]{:S(2)}, u32[]{:S(2)}) collective-permute-start(bf16[2,2,8320]{2,1,0:T(2,128)(2,1)S(1)} %pad_maximum_fusion.refs_0_), channel_id=1, source_target_pairs={{0,12},{1,13},{2,14},{3,15},{4,8},{5,9},{6,10},{7,11},{8,4},{9,5},... | collective-permute-start | bytes 199688 | tf_op jit(solution)/shard_map/ppermute | solution.py:319
  12.3 0.0 collective-permute-start.2
  12.3 0.6 %collective-permute-start.1 = (bf16[2,2,8320]{2,1,0:T(2,128)(2,1)S(1)}, bf16[2,2,8320]{2,1,0:T(2,128)(2,1)S(1)}, u32[]{:S(2)}, u32[]{:S(2)}) collective-permute-start(bf16[2,2,8320]{2,1,0:T(2,128)(2,1)S(1)} %pad_maximum_fusion.refs_0_), channel_id=1, source_target_pairs={{0,4},{1,5},{2,6},{3,7},{4,0},{5,1},{6,2},{7,3},{8,12},{9,13},{10,... | collective-permute-start | bytes 199688 | tf_op jit(solution)/shard_map/ppermute | solution.py:319
  13.0 0.1 pad_add_fusion.place_ref
  13.0 0.0 collective-permute-done.4.other_ref
  13.0 0.0 copy-start
  13.0 1.0 %copy-done = bf16[2,16,8192]{2,1,0:T(8,128)(2,1)S(1)} copy-done((bf16[2,16,8192]{2,1,0:T(8,128)(2,1)S(1)}, bf16[2,16,8192]{2,1,0:T(8,128)(2,1)}, u32[]{:S(2)}) %copy-start) | copy-done | bytes 524312
  14.1 0.0 copy-start.1
  14.1 0.9 %copy-done.1 = f32[16,4096]{1,0:T(8,128)S(1)} copy-done((f32[16,4096]{1,0:T(8,128)S(1)}, f32[16,4096]{1,0:T(8,128)}, u32[]{:S(2)}) %copy-start.1) | copy-done | bytes 262168
  15.0 0.0 copy-start.2
  15.0 0.9 %copy-done.2 = f32[16,4096]{1,0:T(8,128)S(1)} copy-done((f32[16,4096]{1,0:T(8,128)S(1)}, f32[16,4096]{1,0:T(8,128)}, u32[]{:S(2)}) %copy-start.2) | copy-done | bytes 262168
  16.0 0.7 %power.1 = (bf16[64,8192]{1,0:T(8,128)(2,1)S(1)}, bf16[64,4096]{1,0:T(8,128)(2,1)S(1)}, bf16[64,4096]{1,0:T(8,128)(2,1)S(1)}, bf16[48,8192]{1,0:T(8,128)(2,1)S(1)}) custom-call(bf16[32,8192]{1,0:T(8,128)(2,1)S(1)} %bitcast.7, bf16[32,8192]{1,0:T(8,128)(2,1)S(1)} %collective-permute-done.4.other_ref, f32[16,4096]{1,0:T(8,128)S(1)} %copy-done.1, ...), custom_call_target="tpu_custom_call" | custom-call | flops 4194304 | bytes 2097152 | tf_op jit(solution)/shard_map/power/pallas_call | solution.py:348
  16.7 0.0 collective-permute-done.3.refs_3_
  16.7 0.8 %collective-permute-done.2.refs_2_ = bf16[2,2,8320]{2,1,0:T(2,128)(2,1)S(1)} collective-permute-done((bf16[2,2,8320]{2,1,0:T(2,128)(2,1)S(1)}, bf16[2,2,8320]{2,1,0:T(2,128)(2,1)S(1)}, u32[]{:S(2)}, u32[]{:S(2)}) %collective-permute-start.2) | collective-permute-done | bytes 66592 | tf_op jit(solution)/shard_map/ppermute | solution.py:319
  17.5 0.0 collective-permute-done.1.refs_1_
  17.5 3.9 %scores.1 = (bf16[144,8192]{1,0:T(8,128)(2,1)S(1)}, f32[1,32,144]{2,1,0:T(8,128)S(1)}, f32[1,32,144]{2,1,0:T(8,128)S(1)}, f32[16,1,2,144]{3,2,1,0:T(2,128)}) custom-call(s32[2]{0:T(128)S(1)} %pad_add_fusion.place_ref, bf16[2,2,8320]{2,1,0:T(2,128)(2,1)S(1)} %pad_maximum_fusion.refs_0_, bf16[2,2,8320]{2,1,0:T(2,128)(2,1)S(1)} %collective-permute-done.1.refs_1_, ...), custom_call_target="tpu_custom_call" | custom-call | tf_op jit(solution)/shard_map/scores/pallas_call | solution.py:370
  21.5 0.0 collective-permute-start.6
  21.5 5.4 %all-to-all-start = ((f32[16,1,2,144]{3,2,1,0:T(2,128)}), f32[16,1,2,144]{3,2,1,0:T(2,128)S(1)}, u32[]{:S(2)}, u32[]{:S(2)}) async-start(f32[16,1,2,144]{3,2,1,0:T(2,128)} %get-tuple-element.18), calls=%async_computation | async-start | bytes 65536 | tf_op jit(solution)/shard_map/all_to_all | solution.py:393
  26.8 0.4 %collective-permute-start.5 = (f32[1,32,144]{2,1,0:T(8,128)S(1)}, f32[1,32,144]{2,1,0:T(8,128)S(1)}, u32[]{:S(2)}, u32[]{:S(2)}) collective-permute-start(f32[1,32,144]{2,1,0:T(8,128)S(1)} %get-tuple-element.20), channel_id=1, source_target_pairs={{0,1},{1,0},{2,3},{3,2},{4,5},{5,4},{6,7},{7,6},{8,9},{9,8},{10,11... | collective-permute-start | bytes 55304 | tf_op jit(solution)/shard_map/ppermute | solution.py:319
  27.3 0.9 %collective-permute-done.5.exps_other_ref = f32[1,32,144]{2,1,0:T(8,128)S(1)} collective-permute-done((f32[1,32,144]{2,1,0:T(8,128)S(1)}, f32[1,32,144]{2,1,0:T(8,128)S(1)}, u32[]{:S(2)}, u32[]{:S(2)}) %collective-permute-start.5) | collective-permute-done | bytes 18464 | tf_op jit(solution)/shard_map/ppermute | solution.py:319
  28.1 5.4 %all-to-all-done = f32[16,1,2,144]{3,2,1,0:T(2,128)S(1)} async-done(((f32[16,1,2,144]{3,2,1,0:T(2,128)}), f32[16,1,2,144]{3,2,1,0:T(2,128)S(1)}, u32[]{:S(2)}, u32[]{:S(2)}) %all-to-all-start) | async-done | bytes 18464 | tf_op jit(solution)/shard_map/all_to_all | solution.py:393
  33.5 0.0 collective-permute-done.6.weighted_other_ref
  33.5 4.0 %slices.1 = (f32[32,8192]{1,0:T(8,128)}, f32[2]{0:T(128)}, f32[2]{0:T(128)}) custom-call(s32[2]{0:T(128)S(1)} %pad_add_fusion.place_ref, f32[8,2,1,2,144]{4,3,2,1,0:T(2,128)S(1)} %bitcast.8, f32[1,32,144]{2,1,0:T(8,128)S(1)} %get-tuple-element.19.exps_own_ref, f32[1,32,144]{2,1,0:T(8,128)S(1)} %collective-permute-done.5.exps_other_ref, ...), custom_call_target="tpu_custom_call" | custom-call | tf_op jit(solution)/shard_map/slices/pallas_call | solution.py:396
Async XLA Ops:
  2.1 5.1 %collective-permute-start = (bf16[1,2,8320]{2,1,0:T(2,128)(2,1)}, bf16[1,2,8320]{2,1,0:T(2,128)(2,1)S(1)}, u32[]{:S(2)}, u32[]{:S(2)}) collective-permute-start(bf16[1,2,8320]{2,1,0:T(2,128)(2,1)} %pack.1), channel_id=1, source_target_pairs={{0,2},{1,3},{2,0},{3,1},{4,6},{5,7},{6,4},{7,5},{8,10},{9,11},{10,... | collective-permute-start | bytes 99848 | tf_op jit(solution)/shard_map/ppermute | solution.py:319
  5.2 7.9 %collective-permute-start.4 = (bf16[32,8192]{1,0:T(8,128)(2,1)}, bf16[32,8192]{1,0:T(8,128)(2,1)S(1)}, u32[]{:S(2)}, u32[]{:S(2)}) collective-permute-start(bf16[32,8192]{1,0:T(8,128)(2,1)} %bitcast.6), channel_id=1, source_target_pairs={{0,1},{1,0},{2,3},{3,2},{4,5},{5,4},{6,7},{7,6},{8,9},{9,8},{10,11... | collective-permute-start | bytes 1572872 | tf_op jit(solution)/shard_map/ppermute | solution.py:319
  8.2 8.5 %collective-permute-start.3 = (bf16[2,2,8320]{2,1,0:T(2,128)(2,1)S(1)}, bf16[2,2,8320]{2,1,0:T(2,128)(2,1)S(1)}, u32[]{:S(2)}, u32[]{:S(2)}) collective-permute-start(bf16[2,2,8320]{2,1,0:T(2,128)(2,1)S(1)} %pad_maximum_fusion.refs_0_), channel_id=1, source_target_pairs={{0,12},{1,13},{2,14},{3,15},{4,8},{5,9},{6,10},{7,11},{8,4},{9,5},... | collective-permute-start | bytes 199688 | tf_op jit(solution)/shard_map/ppermute | solution.py:319
  12.3 5.2 %collective-permute-start.2 = (bf16[2,2,8320]{2,1,0:T(2,128)(2,1)S(1)}, bf16[2,2,8320]{2,1,0:T(2,128)(2,1)S(1)}, u32[]{:S(2)}, u32[]{:S(2)}) collective-permute-start(bf16[2,2,8320]{2,1,0:T(2,128)(2,1)S(1)} %pad_maximum_fusion.refs_0_), channel_id=1, source_target_pairs={{0,8},{1,9},{2,10},{3,11},{4,12},{5,13},{6,14},{7,15},{8,0},{9,1},... | collective-permute-start | bytes 199688 | tf_op jit(solution)/shard_map/ppermute | solution.py:319
  12.3 5.2 %collective-permute-start.1 = (bf16[2,2,8320]{2,1,0:T(2,128)(2,1)S(1)}, bf16[2,2,8320]{2,1,0:T(2,128)(2,1)S(1)}, u32[]{:S(2)}, u32[]{:S(2)}) collective-permute-start(bf16[2,2,8320]{2,1,0:T(2,128)(2,1)S(1)} %pad_maximum_fusion.refs_0_), channel_id=1, source_target_pairs={{0,4},{1,5},{2,6},{3,7},{4,0},{5,1},{6,2},{7,3},{8,12},{9,13},{10,... | collective-permute-start | bytes 199688 | tf_op jit(solution)/shard_map/ppermute | solution.py:319
  13.0 1.0 %copy-start = (bf16[2,16,8192]{2,1,0:T(8,128)(2,1)S(1)}, bf16[2,16,8192]{2,1,0:T(8,128)(2,1)}, u32[]{:S(2)}) copy-start(bf16[2,16,8192]{2,1,0:T(8,128)(2,1)} %param.7) | copy-start | bytes 1572868
  14.1 0.9 %copy-start.1 = (f32[16,4096]{1,0:T(8,128)S(1)}, f32[16,4096]{1,0:T(8,128)}, u32[]{:S(2)}) copy-start(f32[16,4096]{1,0:T(8,128)} %ctf_hbm.1) | copy-start | bytes 786436
  15.0 0.9 %copy-start.2 = (f32[16,4096]{1,0:T(8,128)S(1)}, f32[16,4096]{1,0:T(8,128)}, u32[]{:S(2)}) copy-start(f32[16,4096]{1,0:T(8,128)} %noise_hbm.1) | copy-start | bytes 786436
  21.5 12.0 %collective-permute-start.6 = (bf16[144,8192]{1,0:T(8,128)(2,1)S(1)}, bf16[144,8192]{1,0:T(8,128)(2,1)}, u32[]{:S(2)}, u32[]{:S(2)}) collective-permute-start(bf16[144,8192]{1,0:T(8,128)(2,1)S(1)} %get-tuple-element.21.weighted_own_ref), channel_id=1, source_target_pairs={{0,1},{1,0},{2,3},{3,2},{4,5},{5,4},{6,7},{7,6},{8,9},{9,8},{10,11... | collective-permute-start | bytes 7077896 | tf_op jit(solution)/shard_map/ppermute | solution.py:319
  21.5 12.0 %all-to-all-start = ((f32[16,1,2,144]{3,2,1,0:T(2,128)}), f32[16,1,2,144]{3,2,1,0:T(2,128)S(1)}, u32[]{:S(2)}, u32[]{:S(2)}) async-start(f32[16,1,2,144]{3,2,1,0:T(2,128)} %get-tuple-element.18), calls=%async_computation | async-start | bytes 65536 | tf_op jit(solution)/shard_map/all_to_all | solution.py:393
  26.8 1.3 %collective-permute-start.5 = (f32[1,32,144]{2,1,0:T(8,128)S(1)}, f32[1,32,144]{2,1,0:T(8,128)S(1)}, u32[]{:S(2)}, u32[]{:S(2)}) collective-permute-start(f32[1,32,144]{2,1,0:T(8,128)S(1)} %get-tuple-element.20), channel_id=1, source_target_pairs={{0,1},{1,0},{2,3},{3,2},{4,5},{5,4},{6,7},{7,6},{8,9},{9,8},{10,11... | collective-permute-start | bytes 55304 | tf_op jit(solution)/shard_map/ppermute | solution.py:319

commit v3 on v2

--- a/solution.py
+++ b/solution.py
@@ -18,7 +18,6 @@
 
 VMEM = pl.BlockSpec(memory_space=pltpu.VMEM)
 HBM = pl.BlockSpec(memory_space=pltpu.HBM)
-SMEM = pl.BlockSpec(memory_space=pltpu.SMEM)
 NT = (((1,), (1,)), ((), ()))
 
 
@@ -125,7 +124,7 @@
             table_ref[pl.ds(third * groups, groups), pl.ds(place * half, half)] = part
 
 
-def score_kernel(pieces_count, shifts, by_distance, place_ref, *refs):
+def score_kernel(pieces_count, shifts, by_distance, *refs):
     pieces = refs[:pieces_count]
     both_ref, high_ref, low_ref, table_ref = refs[pieces_count : pieces_count + 4]
     weighted_ref, exps_ref, exps_other_ref, stats_ref = refs[pieces_count + 4 : pieces_count + 8]
@@ -137,10 +136,11 @@
     particles = image_ref.shape[0]
     per_device = pieces[0].shape[1]
     scale = 0.5 / math.sqrt(half)
+    chip = lax.axis_index("blk") >> 1
     place = 0
     for piece in pieces:
         for row in range(piece.shape[0]):
-            source = place_ref[0] ^ place if by_distance else place
+            source = chip ^ place if by_distance else place
             start = source * per_device
             values = piece[row].astype(jnp.float32)
             for sub in range(per_device):
@@ -216,19 +216,16 @@
         top = jnp.max(functools.reduce(jnp.maximum, scores), axis=1, keepdims=True)
         exps = [jnp.exp(score - top) for score in scores]
         total = jnp.sum(functools.reduce(jnp.add, exps), axis=1, keepdims=True)
-        top_wide = jnp.broadcast_to(top, (ROWS, LANES - candidates))
-        total_wide = jnp.broadcast_to(total, (ROWS, LANES - candidates))
-        spare = lax.broadcasted_iota(jnp.int32, top_wide.shape, 1)
-        tail = jnp.where(spare == 0, top_wide, total_wide)
         for shift in range(shifts):
-            square_ref[pl.ds(shift * ROWS, ROWS), :] = jnp.concatenate(
-                [exps[shift], tail], axis=1
-            )
+            square_ref[pl.ds(shift * ROWS, ROWS), :candidates] = exps[shift]
         turned = square_ref[...].T
         exps_ref[index] = turned[: candidates // 2, :block_rows]
         exps_other_ref[index] = turned[candidates // 2 : candidates, :block_rows]
+        row = lax.broadcasted_iota(jnp.int32, (ROWS, LANES), 0)
+        both_stats = jnp.where(lane == row, top, jnp.where(lane == row + ROWS, total, 0.0))
+        line = jnp.sum(both_stats, axis=0, keepdims=True)
         for target in range(stats_ref.shape[0]):
-            stats_ref[target, index] = turned[candidates : candidates + 2, :block_rows]
+            stats_ref[target, pl.ds(index, 1), :] = line
         return carry
 
     lax.fori_loop(0, particles // ROWS, block, 0)
@@ -236,49 +233,65 @@
 
 def slice_kernel(
     scale,
-    place_ref,
     stats_ref,
     exps_own_ref,
     exps_other_ref,
     weighted_own_ref,
     weighted_other_ref,
     out_hbm,
+    best_hbm,
+    log_hbm,
     best_ref,
     log_ref,
     posterior_ref,
     summed_ref,
     sems,
+    number_sems,
 ):
     blocks, rows, block_rows = exps_own_ref.shape
     chips = stats_ref.shape[0]
     per_device = best_ref.shape[0]
     full = out_hbm.shape[1]
+    index = lax.axis_index("blk")
+    chip = index >> 1
+    lane = lax.broadcasted_iota(jnp.int32, (1, LANES), 1)
     for side, exps_ref in enumerate((exps_own_ref, exps_other_ref)):
-        core = place_ref[1] if side == 0 else 1 - place_ref[1]
+        core = (index & 1) ^ side
         for block in range(blocks):
-            tops = [stats_ref[source, core, block, 0:1, :] for source in range(chips)]
-            totals = [stats_ref[source, core, block, 1:2, :] for source in range(chips)]
-            top = functools.reduce(jnp.maximum, tops)
+            at = pl.ds(block, 1)
+            lines = [stats_ref[source, core, at, :] for source in range(chips)]
+            top = functools.reduce(jnp.maximum, lines)
             total = functools.reduce(
-                jnp.add, [part * jnp.exp(high - top) for high, part in zip(tops, totals)]
+                jnp.add,
+                [pltpu.roll(line, LANES - ROWS, 1) * jnp.exp(line - top) for line in lines],
             )
             log_total = top + jnp.log(total)
-            factor = jnp.exp(stats_ref[place_ref[0], core, block, 0:1, :] - log_total)
+            factor = jnp.exp(stats_ref[chip, core, at, :] - log_total)
+            factor = jnp.where(lane < ROWS, factor, 0.0)
+            filled = ROWS
+            while filled < LANES:
+                factor = factor + pltpu.roll(factor, filled, 1)
+                filled *= 2
+            factor = jnp.concatenate([factor] * -(-block_rows // LANES), axis=1)[:, :block_rows]
             posterior_ref[side, block] = (exps_ref[block] * factor).astype(jnp.bfloat16)
             if side == 0:
                 best = jnp.exp(top - log_total)
-                column = lax.broadcasted_iota(jnp.int32, (1, block_rows), 1)
                 for row in range(per_device):
-                    particle = place_ref[0] * per_device + row
+                    particle = chip * per_device + row
 
                     @pl.when(particle // ROWS == block)
                     def _():
-                        chosen = column == particle % ROWS
+                        chosen = lane == particle % ROWS
                         best_ref[row] = jnp.sum(jnp.where(chosen, best, 0.0))
                         log_ref[row] = jnp.sum(jnp.where(chosen, log_total, 0.0))
 
     width = 1024
-    copies = []
+    copies = [
+        pltpu.make_async_copy(best_ref, best_hbm, number_sems.at[0]),
+        pltpu.make_async_copy(log_ref, log_hbm, number_sems.at[1]),
+    ]
+    for copy in copies:
+        copy.start()
     for number, start in enumerate(range(0, full, width)):
         at = pl.ds(start, width)
         summed = jnp.zeros((rows, width), jnp.float32)
@@ -310,8 +323,6 @@
     particles = chips * per_device
     blocks = particles // ROWS
     block_rows = shifts * ROWS
-    index = lax.axis_index("blk")
-    place = jnp.stack([index >> 1, index & 1])
     megabytes = 12 + -(-2 * blocks * block_rows * full * 2 // 2**20)
     params = pltpu.CompilerParams(vmem_limit_bytes=megabytes * 2**20)
 
@@ -373,9 +384,9 @@
             jax.ShapeDtypeStruct((blocks * block_rows, full), jnp.bfloat16),
             jax.ShapeDtypeStruct((blocks, own_rows, block_rows), jnp.float32),
             jax.ShapeDtypeStruct((blocks, own_rows, block_rows), jnp.float32),
-            jax.ShapeDtypeStruct((axis_size, blocks, 2, block_rows), jnp.float32),
+            jax.ShapeDtypeStruct((axis_size, blocks, LANES), jnp.float32),
         ),
-        in_specs=[SMEM] + [VMEM] * (len(pieces) + 4),
+        in_specs=[VMEM] * (len(pieces) + 4),
         out_specs=(VMEM,) * 4,
         scratch_shapes=[
             pltpu.VMEM((particles, full + LANES), jnp.float32),
@@ -386,7 +397,7 @@
         ],
         compiler_params=params,
         name="scores",
-    )(place, *pieces, both, high, low, tables)
+    )(*pieces, both, high, low, tables)
 
     weighted_other = swap(weighted, 1)
     exps_in = swap(exps_other, 1)
@@ -400,16 +411,19 @@
             jax.ShapeDtypeStruct((per_device,), jnp.float32),
             jax.ShapeDtypeStruct((per_device,), jnp.float32),
         ),
-        in_specs=[SMEM] + [VMEM] * 5,
-        out_specs=(HBM, SMEM, SMEM),
+        in_specs=[VMEM] * 5,
+        out_specs=(HBM, HBM, HBM),
         scratch_shapes=[
+            pltpu.SMEM((per_device,), jnp.float32),
+            pltpu.SMEM((per_device,), jnp.float32),
             pltpu.VMEM((2, blocks, own_rows, block_rows), jnp.bfloat16),
             pltpu.VMEM((own_rows, full), jnp.float32),
             pltpu.SemaphoreType.DMA((full // 1024,)),
+            pltpu.SemaphoreType.DMA((2,)),
         ],
         compiler_params=params,
         name="slices",
-    )(place, gathered, exps, exps_in, weighted, weighted_other)
+    )(gathered, exps, exps_in, weighted, weighted_other)
     return (slices.reshape(batch_count, orient_dev, full), best_posterior, log_total)
 
 

time: 38 us -> 34.8 us (0.916)
  blocking collectives: 0 us -> 11.4 us
  waiting for transfers between devices: 9.18 us -> 3.04 us
  starting transfers between devices: 13.6 us -> 8.41 us
  Pallas kernels: 10.1 us -> 7.1 us
    all_to_all x0 -> x1, blocking collectives: none -> 11.4 us  [local(): gathered = lax.all_to_all(stats, 'blk', 0, 0)]
    all_to_all x1 -> x0, starting transfers between devices: 5.37 us -> none  [local(): gathered = lax.all_to_all(stats, 'blk', 0, 0)]
    all_to_all x1 -> x0, waiting for transfers between devices: 5.36 us -> none  [local(): gathered = lax.all_to_all(stats, 'blk', 0, 0)]
    pallas_call x1, Pallas kernels: 4.03 us -> 2.36 us  [local(): pl.pallas_call(functools.partial(slice_kernel, own_rows / per_device), ou...]
    pallas_call x1, Pallas kernels: 3.91 us -> 2.54 us  [local(): pl.pallas_call(functools.partial(score_kernel, len(pieces), shifts, by_di...]
    ppermute x7, waiting for transfers between devices: 3.83 us -> 3.04 us  [swap(): return lax.ppermute(value, 'blk', [(i, i ^ mask) for i in range(axis_size)])]
  transfers between devices with their start and end apart: 8 -> 7, of which waited for: 4 -> 2; matrix products, arithmetic and copies ran while one was open for 3% -> 2% of each run, Pallas kernels for 2% -> 2%
where the time goes in v3:
time: 34.8 us; the launch traced here: 34.4 us
  blocking collectives  11.4 us (33%)
  starting transfers between devices  8.41 us (24%)
  Pallas kernels  7.1 us (20%)
  waiting for transfers between devices  3.04 us (9%)
  local copies, waits for them, and re-layouts  2.94 us (8%)
  other arithmetic  0.86 us (2%)
  between operations  0.68 us (2%)
    all_to_all x1, blocking collectives, local(): gathered = lax.all_to_all(stats, 'blk', 0, 0)  11.4 us
    ppermute x7, starting transfers between devices, swap(): return lax.ppermute(value, 'blk', [(i, i ^ mask) for i in range(axis_size)])  8.41 us
    ppermute x7, waiting for transfers between devices, swap(): return lax.ppermute(value, 'blk', [(i, i ^ mask) for i in range(axis_size)])  3.04 us
    unnamed x6, local copies, waits for them, and re-layouts  2.94 us
    pallas_call x1, Pallas kernels, local(): pl.pallas_call(functools.partial(score_kernel, len(pieces), shifts, by_di...  2.54 us
    pallas_call x1, Pallas kernels, local(): pl.pallas_call(functools.partial(slice_kernel, own_rows / per_device), ou...  2.36 us
    pallas_call x1, Pallas kernels, local(): pl.pallas_call(pack_kernel, out_shape=jax.ShapeDtypeStruct((1, per_device...  1.51 us
    concatenate x1, other arithmetic, local(): jnp.concatenate([packed, swap(packed, 2)], axis=0)  0.86 us
  transfers between devices with their start and end apart: 7, of which 2 were waited for; matrix products, arithmetic and copies ran while one was open for 2% of the time, Pallas kernels for 2%

profile of v3, /device:TPU:0, one launch (start us, length us, event | category | flops | bytes accessed | tf_op | source)
XLA Modules:
  0.0 34.4 jit_solution(7185077074497887796)
XLA Ops:
  0.6 1.5 %pack.1 = bf16[1,2,8320]{2,1,0:T(2,128)(2,1)} custom-call(bf16[2,8192]{1,0:T(2,128)(2,1)} %images_hbm.1, s32[2]{0:T(128)} %group_hbm.1, s32[2]{0:T(128)} %limit_hbm.1, s32[2,2,9]{2,1,0:T(2,128)} %bitcast.7), custom_call_target="tpu_custom_call" | custom-call | tf_op jit(solution)/shard_map/pack/pallas_call | solution.py:332
  2.1 3.0 %collective-permute-start = (bf16[1,2,8320]{2,1,0:T(2,128)(2,1)}, bf16[1,2,8320]{2,1,0:T(2,128)(2,1)S(1)}, u32[]{:S(2)}, u32[]{:S(2)}) collective-permute-start(bf16[1,2,8320]{2,1,0:T(2,128)(2,1)} %pack.1), channel_id=1, source_target_pairs={{0,2},{1,3},{2,0},{3,1},{4,6},{5,7},{6,4},{7,5},{8,10},{9,11},{10,... | collective-permute-start | bytes 99848 | tf_op jit(solution)/shard_map/ppermute | solution.py:330
  5.2 0.0 collective-permute-start.4
  5.2 2.1 %collective-permute-done = bf16[1,2,8320]{2,1,0:T(2,128)(2,1)S(1)} collective-permute-done((bf16[1,2,8320]{2,1,0:T(2,128)(2,1)}, bf16[1,2,8320]{2,1,0:T(2,128)(2,1)S(1)}, u32[]{:S(2)}, u32[]{:S(2)}) %collective-permute-start) | collective-permute-done | bytes 33312 | tf_op jit(solution)/shard_map/ppermute | solution.py:330
  7.3 0.9 %pad_maximum_fusion.refs_0_ = bf16[2,2,8320]{2,1,0:T(2,128)(2,1)S(1)} fusion(bf16[1,2,8320]{2,1,0:T(2,128)(2,1)S(1)} %collective-permute-done, bf16[1,2,8320]{2,1,0:T(2,128)(2,1)} %pack.1), kind=kLoop, calls=%fused_computation | loop fusion | flops 33280 | bytes 133120 | tf_op jit(solution)/shard_map/concatenate | solution.py:348
  8.1 4.2 %collective-permute-start.3 = (bf16[2,2,8320]{2,1,0:T(2,128)(2,1)S(1)}, bf16[2,2,8320]{2,1,0:T(2,128)(2,1)S(1)}, u32[]{:S(2)}, u32[]{:S(2)}) collective-permute-start(bf16[2,2,8320]{2,1,0:T(2,128)(2,1)S(1)} %pad_maximum_fusion.refs_0_), channel_id=1, source_target_pairs={{0,12},{1,13},{2,14},{3,15},{4,8},{5,9},{6,10},{7,11},{8,4},{9,5},... | collective-permute-start | bytes 199688 | tf_op jit(solution)/shard_map/ppermute | solution.py:330
  12.3 0.0 collective-permute-start.2
  12.3 0.6 %collective-permute-start.1 = (bf16[2,2,8320]{2,1,0:T(2,128)(2,1)S(1)}, bf16[2,2,8320]{2,1,0:T(2,128)(2,1)S(1)}, u32[]{:S(2)}, u32[]{:S(2)}) collective-permute-start(bf16[2,2,8320]{2,1,0:T(2,128)(2,1)S(1)} %pad_maximum_fusion.refs_0_), channel_id=1, source_target_pairs={{0,4},{1,5},{2,6},{3,7},{4,0},{5,1},{6,2},{7,3},{8,12},{9,13},{10,... | collective-permute-start | bytes 199688 | tf_op jit(solution)/shard_map/ppermute | solution.py:330
  13.0 0.0 collective-permute-done.4.other_ref
  13.0 0.0 copy-start
  13.0 1.0 %copy-done = bf16[2,16,8192]{2,1,0:T(8,128)(2,1)S(1)} copy-done((bf16[2,16,8192]{2,1,0:T(8,128)(2,1)S(1)}, bf16[2,16,8192]{2,1,0:T(8,128)(2,1)}, u32[]{:S(2)}) %copy-start) | copy-done | bytes 524312
  14.0 0.0 copy-start.1
  14.0 0.9 %copy-done.1 = f32[16,4096]{1,0:T(8,128)S(1)} copy-done((f32[16,4096]{1,0:T(8,128)S(1)}, f32[16,4096]{1,0:T(8,128)}, u32[]{:S(2)}) %copy-start.1) | copy-done | bytes 262168
  15.0 0.0 copy-start.2
  15.0 0.9 %copy-done.2 = f32[16,4096]{1,0:T(8,128)S(1)} copy-done((f32[16,4096]{1,0:T(8,128)S(1)}, f32[16,4096]{1,0:T(8,128)}, u32[]{:S(2)}) %copy-start.2) | copy-done | bytes 262168
  15.9 0.7 %power.1 = (bf16[64,8192]{1,0:T(8,128)(2,1)S(1)}, bf16[64,4096]{1,0:T(8,128)(2,1)S(1)}, bf16[64,4096]{1,0:T(8,128)(2,1)S(1)}, bf16[48,8192]{1,0:T(8,128)(2,1)S(1)}) custom-call(bf16[32,8192]{1,0:T(8,128)(2,1)S(1)} %bitcast.5, bf16[32,8192]{1,0:T(8,128)(2,1)S(1)} %collective-permute-done.4.other_ref, f32[16,4096]{1,0:T(8,128)S(1)} %copy-done.1, ...), custom_call_target="tpu_custom_call" | custom-call | flops 4194304 | bytes 2097152 | tf_op jit(solution)/shard_map/power/pallas_call | solution.py:359
  16.6 0.0 collective-permute-done.3.refs_3_
  16.6 0.9 %collective-permute-done.2.refs_2_ = bf16[2,2,8320]{2,1,0:T(2,128)(2,1)S(1)} collective-permute-done((bf16[2,2,8320]{2,1,0:T(2,128)(2,1)S(1)}, bf16[2,2,8320]{2,1,0:T(2,128)(2,1)S(1)}, u32[]{:S(2)}, u32[]{:S(2)}) %collective-permute-start.2) | collective-permute-done | bytes 66592 | tf_op jit(solution)/shard_map/ppermute | solution.py:330
  17.5 0.0 collective-permute-done.1.refs_1_
  17.5 2.5 %scores.1 = (bf16[144,8192]{1,0:T(8,128)(2,1)S(1)}, f32[1,32,144]{2,1,0:T(8,128)S(1)}, f32[1,32,144]{2,1,0:T(8,128)S(1)}, f32[16,1,128]{2,1,0:T(1,128)S(1)}) custom-call(bf16[2,2,8320]{2,1,0:T(2,128)(2,1)S(1)} %pad_maximum_fusion.refs_0_, bf16[2,2,8320]{2,1,0:T(2,128)(2,1)S(1)} %collective-permute-done.1.refs_1_, ...), custom_call_target="tpu_custom_call" | custom-call | tf_op jit(solution)/shard_map/scores/pallas_call | solution.py:381
  20.1 0.1 collective-permute-start.6
  20.2 0.5 %collective-permute-start.5 = (f32[1,32,144]{2,1,0:T(8,128)S(1)}, f32[1,32,144]{2,1,0:T(8,128)S(1)}, u32[]{:S(2)}, u32[]{:S(2)}) collective-permute-start(f32[1,32,144]{2,1,0:T(8,128)S(1)} %get-tuple-element.20), channel_id=1, source_target_pairs={{0,1},{1,0},{2,3},{3,2},{4,5},{5,4},{6,7},{7,6},{8,9},{9,8},{10,11... | collective-permute-start | bytes 55304 | tf_op jit(solution)/shard_map/ppermute | solution.py:330
  20.7 11.4 %all_to_all.5 = f32[16,1,128]{2,1,0:T(1,128)S(1)} all-to-all(f32[16,1,128]{2,1,0:T(1,128)S(1)} %get-tuple-element.18), channel_id=1, replica_groups=mesh['groups'=2,'blk'=16] {'blk'}, dimensions={0} | all-to-all | bytes 16384 | tf_op jit(solution)/shard_map/all_to_all | solution.py:404
  32.0 0.0 collective-permute-done.5.exps_other_ref
  32.0 0.0 collective-permute-done.6.weighted_other_ref
  32.0 2.4 %slices.1 = (f32[32,8192]{1,0:T(8,128)}, f32[2]{0:T(128)}, f32[2]{0:T(128)}) custom-call(f32[8,2,1,128]{3,2,1,0:T(1,128)S(1)} %bitcast.6, f32[1,32,144]{2,1,0:T(8,128)S(1)} %get-tuple-element.19.exps_own_ref, f32[1,32,144]{2,1,0:T(8,128)S(1)} %collective-permute-done.5.exps_other_ref, bf16[144,8192]{1,0:T(8,128)(2,1)S(1)} %get-tuple-element.21.weighted_own_ref, ...), custom_call_target="tpu_custom_call" | custom-call | tf_op jit(solution)/shard_map/slices/pallas_call | solution.py:407
Async XLA Ops:
  2.1 5.1 %collective-permute-start = (bf16[1,2,8320]{2,1,0:T(2,128)(2,1)}, bf16[1,2,8320]{2,1,0:T(2,128)(2,1)S(1)}, u32[]{:S(2)}, u32[]{:S(2)}) collective-permute-start(bf16[1,2,8320]{2,1,0:T(2,128)(2,1)} %pack.1), channel_id=1, source_target_pairs={{0,2},{1,3},{2,0},{3,1},{4,6},{5,7},{6,4},{7,5},{8,10},{9,11},{10,... | collective-permute-start | bytes 99848 | tf_op jit(solution)/shard_map/ppermute | solution.py:330
  5.2 7.8 %collective-permute-start.4 = (bf16[32,8192]{1,0:T(8,128)(2,1)}, bf16[32,8192]{1,0:T(8,128)(2,1)S(1)}, u32[]{:S(2)}, u32[]{:S(2)}) collective-permute-start(bf16[32,8192]{1,0:T(8,128)(2,1)} %bitcast.4), channel_id=1, source_target_pairs={{0,1},{1,0},{2,3},{3,2},{4,5},{5,4},{6,7},{7,6},{8,9},{9,8},{10,11... | collective-permute-start | bytes 1572872 | tf_op jit(solution)/shard_map/ppermute | solution.py:330
  8.1 8.5 %collective-permute-start.3 = (bf16[2,2,8320]{2,1,0:T(2,128)(2,1)S(1)}, bf16[2,2,8320]{2,1,0:T(2,128)(2,1)S(1)}, u32[]{:S(2)}, u32[]{:S(2)}) collective-permute-start(bf16[2,2,8320]{2,1,0:T(2,128)(2,1)S(1)} %pad_maximum_fusion.refs_0_), channel_id=1, source_target_pairs={{0,12},{1,13},{2,14},{3,15},{4,8},{5,9},{6,10},{7,11},{8,4},{9,5},... | collective-permute-start | bytes 199688 | tf_op jit(solution)/shard_map/ppermute | solution.py:330
  12.3 5.2 %collective-permute-start.2 = (bf16[2,2,8320]{2,1,0:T(2,128)(2,1)S(1)}, bf16[2,2,8320]{2,1,0:T(2,128)(2,1)S(1)}, u32[]{:S(2)}, u32[]{:S(2)}) collective-permute-start(bf16[2,2,8320]{2,1,0:T(2,128)(2,1)S(1)} %pad_maximum_fusion.refs_0_), channel_id=1, source_target_pairs={{0,8},{1,9},{2,10},{3,11},{4,12},{5,13},{6,14},{7,15},{8,0},{9,1},... | collective-permute-start | bytes 199688 | tf_op jit(solution)/shard_map/ppermute | solution.py:330
  12.3 5.2 %collective-permute-start.1 = (bf16[2,2,8320]{2,1,0:T(2,128)(2,1)S(1)}, bf16[2,2,8320]{2,1,0:T(2,128)(2,1)S(1)}, u32[]{:S(2)}, u32[]{:S(2)}) collective-permute-start(bf16[2,2,8320]{2,1,0:T(2,128)(2,1)S(1)} %pad_maximum_fusion.refs_0_), channel_id=1, source_target_pairs={{0,4},{1,5},{2,6},{3,7},{4,0},{5,1},{6,2},{7,3},{8,12},{9,13},{10,... | collective-permute-start | bytes 199688 | tf_op jit(solution)/shard_map/ppermute | solution.py:330
  13.0 1.0 %copy-start = (bf16[2,16,8192]{2,1,0:T(8,128)(2,1)S(1)}, bf16[2,16,8192]{2,1,0:T(8,128)(2,1)}, u32[]{:S(2)}) copy-start(bf16[2,16,8192]{2,1,0:T(8,128)(2,1)} %param.7) | copy-start | bytes 1572868
  14.0 0.9 %copy-start.1 = (f32[16,4096]{1,0:T(8,128)S(1)}, f32[16,4096]{1,0:T(8,128)}, u32[]{:S(2)}) copy-start(f32[16,4096]{1,0:T(8,128)} %ctf_hbm.1) | copy-start | bytes 786436
  15.0 0.9 %copy-start.2 = (f32[16,4096]{1,0:T(8,128)S(1)}, f32[16,4096]{1,0:T(8,128)}, u32[]{:S(2)}) copy-start(f32[16,4096]{1,0:T(8,128)} %noise_hbm.1) | copy-start | bytes 786436
  20.1 12.0 %collective-permute-start.6 = (bf16[144,8192]{1,0:T(8,128)(2,1)S(1)}, bf16[144,8192]{1,0:T(8,128)(2,1)S(1)}, u32[]{:S(2)}, u32[]{:S(2)}) collective-permute-start(bf16[144,8192]{1,0:T(8,128)(2,1)S(1)} %get-tuple-element.21.weighted_own_ref), channel_id=1, source_target_pairs={{0,1},{1,0},{2,3},{3,2},{4,5},{5,4},{6,7},{7,6},{8,9},{9,8},{10,11... | collective-permute-start | bytes 7077896 | tf_op jit(solution)/shard_map/ppermute | solution.py:330
  20.2 11.9 %collective-permute-start.5 = (f32[1,32,144]{2,1,0:T(8,128)S(1)}, f32[1,32,144]{2,1,0:T(8,128)S(1)}, u32[]{:S(2)}, u32[]{:S(2)}) collective-permute-start(f32[1,32,144]{2,1,0:T(8,128)S(1)} %get-tuple-element.20), channel_id=1, source_target_pairs={{0,1},{1,0},{2,3},{3,2},{4,5},{5,4},{6,7},{7,6},{8,9},{9,8},{10,11... | collective-permute-start | bytes 55304 | tf_op jit(solution)/shard_map/ppermute | solution.py:330

commit v4 on v3

--- a/solution.py
+++ b/solution.py
@@ -50,18 +50,30 @@
     return high, (value - high.astype(jnp.float32)).astype(jnp.bfloat16)
 
 
-def pack_kernel(images_hbm, group_hbm, limit_hbm, offsets_hbm, packed_ref, group, limit, offsets, sems):
+def pack_kernel(
+    images_hbm,
+    group_hbm,
+    limit_hbm,
+    offsets_hbm,
+    packed_hbm,
+    numbers_ref,
+    group,
+    limit,
+    offsets,
+    sems,
+):
     per_device, full = images_hbm.shape
     shifts = offsets_hbm.shape[2]
     copies = [
-        pltpu.make_async_copy(images_hbm, packed_ref.at[0, :, pl.ds(0, full)], sems.at[0]),
-        pltpu.make_async_copy(group_hbm, group, sems.at[1]),
-        pltpu.make_async_copy(limit_hbm, limit, sems.at[2]),
-        pltpu.make_async_copy(offsets_hbm, offsets, sems.at[3]),
+        pltpu.make_async_copy(group_hbm, group, sems.at[0]),
+        pltpu.make_async_copy(limit_hbm, limit, sems.at[1]),
+        pltpu.make_async_copy(offsets_hbm, offsets, sems.at[2]),
+        pltpu.make_async_copy(images_hbm, packed_hbm.at[0, :, pl.ds(0, full)], sems.at[3]),
+        pltpu.make_async_copy(numbers_ref, packed_hbm.at[0, :, pl.ds(full, LANES)], sems.at[4]),
     ]
-    for copy in copies:
+    for copy in copies[:4]:
         copy.start()
-    for copy in copies[1:]:
+    for copy in copies[:3]:
         copy.wait()
     row = lax.broadcasted_iota(jnp.int32, (per_device, LANES), 0)
     lane = lax.broadcasted_iota(jnp.int32, (per_device, LANES), 1)
@@ -74,8 +86,10 @@
             line = jnp.where(lane == X_AT + shift, offsets[particle, 0, shift], line)
             line = jnp.where(lane == Y_AT + shift, offsets[particle, 1, shift], line)
         numbers = jnp.where(row == particle, line, numbers)
-    packed_ref[0, :, pl.ds(full, LANES)] = numbers.astype(jnp.float32).astype(jnp.bfloat16)
-    copies[0].wait()
+    numbers_ref[...] = numbers.astype(jnp.float32).astype(jnp.bfloat16)
+    copies[4].start()
+    copies[3].wait()
+    copies[4].wait()
 
 
 def split_thirds(value):
@@ -85,41 +99,22 @@
     return high, middle, (rest - middle.astype(jnp.float32)).astype(jnp.bfloat16)
 
 
-def power_kernel(
-    own_hbm,
-    other_ref,
-    ctf_hbm,
-    noise_hbm,
-    both_ref,
-    high_ref,
-    low_ref,
-    table_ref,
-    ctf_ref,
-    noise_ref,
-    sems,
-):
-    rows, full = other_ref.shape
+def power_kernel(own_ref, other_ref, both_ref, high_ref, low_ref):
+    rows, full = own_ref.shape
     half = full // 2
-    groups = ctf_ref.shape[0]
-    copies = [
-        pltpu.make_async_copy(own_hbm, both_ref.at[pl.ds(0, rows)], sems.at[0]),
-        pltpu.make_async_copy(ctf_hbm, ctf_ref, sems.at[1]),
-        pltpu.make_async_copy(noise_hbm, noise_ref, sems.at[2]),
-    ]
-    for copy in copies:
-        copy.start()
-    both_ref[pl.ds(rows, rows), :] = other_ref[...]
-    for place in (1, 0):
+    for place, ref in enumerate((own_ref, other_ref)):
         at = pl.ds(place * rows, rows)
-        if place == 0:
-            copies[0].wait()
-        real = both_ref[at, :half].astype(jnp.float32)
-        imag = both_ref[at, half:].astype(jnp.float32)
+        both_ref[at, :] = ref[...]
+        real = ref[:, :half].astype(jnp.float32)
+        imag = ref[:, half:].astype(jnp.float32)
         high, low = split_halves(real * real + imag * imag)
         high_ref[at, :] = high
         low_ref[at, :] = low
+
+
+def table_kernel(ctf_ref, noise_ref, table_ref):
+    groups, half = ctf_ref.shape
     for place, ref in enumerate((ctf_ref, noise_ref)):
-        copies[1 + place].wait()
         for third, part in enumerate(split_thirds(ref[...])):
             table_ref[pl.ds(third * groups, groups), pl.ds(place * half, half)] = part
 
@@ -231,78 +226,90 @@
     lax.fori_loop(0, particles // ROWS, block, 0)
 
 
-def slice_kernel(
+def multiply_slices(scale, posterior_ref, weighted_ref, out_ref):
+    blocks, rows, block_rows = posterior_ref.shape
+    width = 1024
+    for start in range(0, weighted_ref.shape[1], width):
+        at = pl.ds(start, width)
+        summed = functools.reduce(
+            jnp.add,
+            [
+                jnp.dot(
+                    posterior_ref[block],
+                    weighted_ref[pl.ds(block * block_rows, block_rows), at],
+                    preferred_element_type=jnp.float32,
+                )
+                for block in range(blocks)
+            ],
+        )
+        out_ref[:, at] = (summed * scale).astype(out_ref.dtype)
+
+
+def send_kernel(
     scale,
     stats_ref,
     exps_own_ref,
     exps_other_ref,
-    weighted_own_ref,
-    weighted_other_ref,
-    out_hbm,
+    weighted_ref,
+    send_ref,
+    posterior_ref,
     best_hbm,
     log_hbm,
+    posterior_other_ref,
     best_ref,
     log_ref,
-    posterior_ref,
-    summed_ref,
     sems,
-    number_sems,
 ):
     blocks, rows, block_rows = exps_own_ref.shape
     chips = stats_ref.shape[0]
     per_device = best_ref.shape[0]
-    full = out_hbm.shape[1]
-    index = lax.axis_index("blk")
-    chip = index >> 1
+    chip = lax.axis_index("blk") >> 1
     lane = lax.broadcasted_iota(jnp.int32, (1, LANES), 1)
-    for side, exps_ref in enumerate((exps_own_ref, exps_other_ref)):
-        core = (index & 1) ^ side
-        for block in range(blocks):
-            at = pl.ds(block, 1)
-            lines = [stats_ref[source, core, at, :] for source in range(chips)]
-            top = functools.reduce(jnp.maximum, lines)
-            total = functools.reduce(
-                jnp.add,
-                [pltpu.roll(line, LANES - ROWS, 1) * jnp.exp(line - top) for line in lines],
-            )
-            log_total = top + jnp.log(total)
-            factor = jnp.exp(stats_ref[chip, core, at, :] - log_total)
-            factor = jnp.where(lane < ROWS, factor, 0.0)
-            filled = ROWS
-            while filled < LANES:
-                factor = factor + pltpu.roll(factor, filled, 1)
-                filled *= 2
-            factor = jnp.concatenate([factor] * -(-block_rows // LANES), axis=1)[:, :block_rows]
-            posterior_ref[side, block] = (exps_ref[block] * factor).astype(jnp.bfloat16)
-            if side == 0:
-                best = jnp.exp(top - log_total)
-                for row in range(per_device):
-                    particle = chip * per_device + row
-
-                    @pl.when(particle // ROWS == block)
-                    def _():
-                        chosen = lane == particle % ROWS
-                        best_ref[row] = jnp.sum(jnp.where(chosen, best, 0.0))
-                        log_ref[row] = jnp.sum(jnp.where(chosen, log_total, 0.0))
-
-    width = 1024
+    for block in range(blocks):
+        at = pl.ds(block, 1)
+        lines = [stats_ref[source, at, :] for source in range(chips)]
+        top = functools.reduce(jnp.maximum, lines)
+        total = functools.reduce(
+            jnp.add,
+            [pltpu.roll(line, LANES - ROWS, 1) * jnp.exp(line - top) for line in lines],
+        )
+        log_total = top + jnp.log(total)
+        factor = jnp.exp(stats_ref[chip, at, :] - log_total)
+        factor = jnp.where(lane < ROWS, factor, 0.0)
+        filled = ROWS
+        while filled < LANES:
+            factor = factor + pltpu.roll(factor, filled, 1)
+            filled *= 2
+        factor = jnp.concatenate([factor] * -(-block_rows // LANES), axis=1)[:, :block_rows]
+        posterior_other_ref[block] = (exps_other_ref[block] * factor).astype(jnp.bfloat16)
+        posterior_ref[block] = (exps_own_ref[block] * factor).astype(jnp.bfloat16)
+        best = jnp.exp(top - log_total)
+        for row in range(per_device):
+            particle = chip * per_device + row
+
+            @pl.when(particle // ROWS == block)
+            def _():
+                chosen = lane == particle % ROWS
+                best_ref[row] = jnp.sum(jnp.where(chosen, best, 0.0))
+                log_ref[row] = jnp.sum(jnp.where(chosen, log_total, 0.0))
+
     copies = [
-        pltpu.make_async_copy(best_ref, best_hbm, number_sems.at[0]),
-        pltpu.make_async_copy(log_ref, log_hbm, number_sems.at[1]),
+        pltpu.make_async_copy(best_ref, best_hbm, sems.at[0]),
+        pltpu.make_async_copy(log_ref, log_hbm, sems.at[1]),
     ]
     for copy in copies:
         copy.start()
-    for number, start in enumerate(range(0, full, width)):
-        at = pl.ds(start, width)
-        summed = jnp.zeros((rows, width), jnp.float32)
-        for side, weighted_ref in enumerate((weighted_own_ref, weighted_other_ref)):
-            for block in range(blocks):
-                summed = summed + jnp.dot(
-                    posterior_ref[side, block],
-                    weighted_ref[pl.ds(block * block_rows, block_rows), at],
-                    preferred_element_type=jnp.float32,
-                )
-        summed_ref[:, at] = summed * scale
+    multiply_slices(scale, posterior_other_ref, weighted_ref, send_ref)
+    for copy in copies:
+        copy.wait()
+
+
+def add_kernel(keep_ref, received_ref, out_hbm, summed_ref, sems):
+    width = summed_ref.shape[1] // sems.shape[0]
+    copies = []
+    for number in range(sems.shape[0]):
+        at = pl.ds(number * width, width)
+        summed_ref[:, at] = keep_ref[:, at] + received_ref[:, at].astype(jnp.float32)
         copy = pltpu.make_async_copy(summed_ref.at[:, at], out_hbm.at[:, at], sems.at[number])
         copy.start()
         copies.append(copy)
@@ -333,50 +340,61 @@
         pack_kernel,
         out_shape=jax.ShapeDtypeStruct((1, per_device, full + LANES), jnp.bfloat16),
         in_specs=[HBM] * 4,
-        out_specs=VMEM,
+        out_specs=HBM,
         scratch_shapes=[
+            pltpu.VMEM((per_device, LANES), jnp.bfloat16),
             pltpu.SMEM((per_device,), jnp.int32),
             pltpu.SMEM((per_device,), jnp.int32),
             pltpu.SMEM((per_device, 2, shifts), jnp.int32),
-            pltpu.SemaphoreType.DMA((4,)),
+            pltpu.SemaphoreType.DMA((5,)),
         ],
         compiler_params=pltpu.CompilerParams(vmem_limit_bytes=60 * 2**20),
         name="pack",
     )(images, ctf_group, shell_limit, shift_offsets.transpose(0, 2, 1))
-    by_distance = chips <= 8
-    if by_distance:
-        pair = jnp.concatenate([packed, swap(packed, 2)], axis=0) if chips > 1 else packed
-        pieces = [pair] + [swap(pair, mask) for mask in range(4, axis_size, 4)]
-    else:
-        same_core = [[2 * c + core for c in range(chips)] for core in range(2)]
-        pieces = [
-            lax.all_gather(packed, "blk", axis=0, tiled=True, axis_index_groups=same_core)
-        ]
-
+    received = swap(packed, 2) if 1 < chips <= 8 else packed
     flat = projections.reshape(own_rows, full)
     other = swap(flat, 1)
     groups = ctf_table.shape[0]
-    both, high, low, tables = pl.pallas_call(
+    both, high, low = pl.pallas_call(
         power_kernel,
         out_shape=(
             jax.ShapeDtypeStruct((candidates, full), jnp.bfloat16),
             jax.ShapeDtypeStruct((candidates, half), jnp.bfloat16),
             jax.ShapeDtypeStruct((candidates, half), jnp.bfloat16),
-            jax.ShapeDtypeStruct((3 * groups, full), jnp.bfloat16),
-        ),
-        in_specs=[HBM, VMEM, HBM, HBM],
-        out_specs=(VMEM,) * 4,
-        scratch_shapes=[
-            pltpu.VMEM((groups, half), jnp.float32),
-            pltpu.VMEM((groups, half), jnp.float32),
-            pltpu.SemaphoreType.DMA((3,)),
-        ],
+        ),
+        in_specs=[VMEM] * 2,
+        out_specs=(VMEM,) * 3,
         compiler_params=params,
         cost_estimate=pl.CostEstimate(
             flops=8 * candidates * full, bytes_accessed=4 * candidates * full, transcendentals=0
         ),
         name="power",
-    )(flat, other, ctf_table, noise_weight)
+    )(flat, other)
+    tables = pl.pallas_call(
+        table_kernel,
+        out_shape=jax.ShapeDtypeStruct((3 * groups, full), jnp.bfloat16),
+        in_specs=[VMEM] * 2,
+        out_specs=VMEM,
+        compiler_params=params,
+        cost_estimate=pl.CostEstimate(
+            flops=6 * groups * full, bytes_accessed=10 * groups * full, transcendentals=0
+        ),
+        name="tables",
+    )(ctf_table, noise_weight)
+    by_distance = 1 < chips <= 8
+    same_core = [[2 * c + core for c in range(chips)] for core in range(2)]
+    if by_distance:
+        pair = jnp.zeros((2,) + packed.shape[1:], packed.dtype)
+        pair = lax.dynamic_update_slice(pair, packed, (0, 0, 0))
+        pair, received, both, high, low = lax.optimization_barrier(
+            (pair, received, both, high, low)
+        )
+        pair = lax.dynamic_update_slice(pair, received, (1, 0, 0))
+        pieces = [pair] + [swap(pair, mask) for mask in range(4, axis_size, 4)]
+    else:
+        pieces = [
+            lax.all_gather(packed, "blk", axis=0, tiled=True, axis_index_groups=same_core)
+        ]
 
     weighted, exps, exps_other, stats = pl.pallas_call(
         functools.partial(score_kernel, len(pieces), shifts, by_distance),
@@ -384,7 +402,7 @@
             jax.ShapeDtypeStruct((blocks * block_rows, full), jnp.bfloat16),
             jax.ShapeDtypeStruct((blocks, own_rows, block_rows), jnp.float32),
             jax.ShapeDtypeStruct((blocks, own_rows, block_rows), jnp.float32),
-            jax.ShapeDtypeStruct((axis_size, blocks, LANES), jnp.float32),
+            jax.ShapeDtypeStruct((chips, blocks, LANES), jnp.float32),
         ),
         in_specs=[VMEM] * (len(pieces) + 4),
         out_specs=(VMEM,) * 4,
@@ -399,31 +417,54 @@
         name="scores",
     )(*pieces, both, high, low, tables)
 
-    weighted_other = swap(weighted, 1)
-    exps_in = swap(exps_other, 1)
-    gathered = lax.all_to_all(stats, "blk", 0, 0)
-    gathered = gathered.reshape((chips, 2) + gathered.shape[1:])
-
-    slices, best_posterior, log_total = pl.pallas_call(
-        functools.partial(slice_kernel, own_rows / per_device),
+    gathered = lax.all_to_all(stats, "blk", 0, 0, axis_index_groups=same_core)
+
+    scale = own_rows / per_device
+    send, posterior, best_posterior, log_total = pl.pallas_call(
+        functools.partial(send_kernel, scale),
         out_shape=(
-            jax.ShapeDtypeStruct((own_rows, full), jnp.float32),
+            jax.ShapeDtypeStruct((own_rows, full), jnp.bfloat16),
+            jax.ShapeDtypeStruct((blocks, own_rows, block_rows), jnp.bfloat16),
             jax.ShapeDtypeStruct((per_device,), jnp.float32),
             jax.ShapeDtypeStruct((per_device,), jnp.float32),
         ),
-        in_specs=[VMEM] * 5,
-        out_specs=(HBM, HBM, HBM),
+        in_specs=[VMEM] * 4,
+        out_specs=(VMEM, VMEM, HBM, HBM),
         scratch_shapes=[
+            pltpu.VMEM((blocks, own_rows, block_rows), jnp.bfloat16),
             pltpu.SMEM((per_device,), jnp.float32),
             pltpu.SMEM((per_device,), jnp.float32),
-            pltpu.VMEM((2, blocks, own_rows, block_rows), jnp.bfloat16),
-            pltpu.VMEM((own_rows, full), jnp.float32),
-            pltpu.SemaphoreType.DMA((full // 1024,)),
             pltpu.SemaphoreType.DMA((2,)),
         ],
         compiler_params=params,
-        name="slices",
-    )(gathered, exps, exps_in, weighted, weighted_other)
+        name="send",
+    )(gathered, exps, exps_other, weighted)
+    received = swap(send, 1)
+    keep = pl.pallas_call(
+        functools.partial(multiply_slices, scale),
+        out_shape=jax.ShapeDtypeStruct((own_rows, full), jnp.float32),
+        in_specs=[VMEM] * 2,
+        out_specs=VMEM,
+        compiler_params=params,
+        cost_estimate=pl.CostEstimate(
+            flops=2 * own_rows * full * blocks * block_rows,
+            bytes_accessed=4 * own_rows * full,
+            transcendentals=0,
+        ),
+        name="keep",
+    )(posterior, weighted)
+    slices = pl.pallas_call(
+        add_kernel,
+        out_shape=jax.ShapeDtypeStruct((own_rows, full), jnp.float32),
+        in_specs=[VMEM] * 2,
+        out_specs=HBM,
+        scratch_shapes=[
+            pltpu.VMEM((own_rows, full), jnp.float32),
+            pltpu.SemaphoreType.DMA((8,)),
+        ],
+        compiler_params=params,
+        name="add",
+    )(keep, received)
     return (slices.reshape(batch_count, orient_dev, full), best_posterior, log_total)
 
 

time: 34.8 us -> 35.7 us (1.026)
  waiting for transfers between devices: 3.04 us -> 4.48 us
  other arithmetic: 0.86 us -> 0 us
  local copies, waits for them, and re-layouts: 2.94 us -> 3.8 us
  blocking collectives: 11.4 us -> 10.7 us
  Pallas kernels: 7.1 us -> 7.79 us
  starting transfers between devices: 8.41 us -> 7.84 us
    ppermute x7 -> x6, waiting for transfers between devices: 3.04 us -> 4.48 us  [swap(): return lax.ppermute(value, 'blk', [(i, i ^ mask) for i in range(axis_size)])]
    dynamic_update_slice x0 -> x2, local copies, waits for them, and re-layouts: none -> 0.87 us  [the longest x1 0.83 us: local(): pair = lax.dynamic_update_slice(pair, packed, (0, 0, 0))]
    concatenate x1 -> x0, other arithmetic: 0.86 us -> none  [local(): jnp.concatenate([packed, swap(packed, 2)], axis=0)]
    all_to_all x1, blocking collectives: 11.4 us -> 10.7 us  [local(): gathered = lax.all_to_all(stats, 'blk', 0, 0, axis_index_groups=same_core)]
    pallas_call x1, Pallas kernels: 1.51 us -> 2.14 us  [local(): pl.pallas_call(pack_kernel, out_shape=jax.ShapeDtypeStruct((1, per_device...]
    ppermute x7 -> x6, starting transfers between devices: 8.41 us -> 7.84 us  [swap(): return lax.ppermute(value, 'blk', [(i, i ^ mask) for i in range(axis_size)])]
    pallas_call x1 -> x4, Pallas kernels: 2.36 us -> 2.73 us  [the longest x1 1.1 us: local(): pl.pallas_call(functools.partial(send_kernel, scale), out_shape=(jax.Shap...]
    pallas_call x1, Pallas kernels: 0.69 us -> 0.33 us  [local(): pl.pallas_call(power_kernel, out_shape=(jax.ShapeDtypeStruct((candidates,...]
  transfers between devices with their start and end apart: 7 -> 6, of which waited for: 2 -> 2; matrix products, arithmetic and copies ran while one was open for 2% -> 2% of each run, Pallas kernels for 2% -> 9%
where the time goes in v4:
time: 35.7 us; the launch traced here: 35.3 us
  blocking collectives  10.7 us (30%)
  starting transfers between devices  7.84 us (22%)
  Pallas kernels  7.79 us (22%)
  waiting for transfers between devices  4.48 us (13%)
  local copies, waits for them, and re-layouts  3.8 us (11%)
  between operations  0.71 us (2%)
    all_to_all x1, blocking collectives, local(): gathered = lax.all_to_all(stats, 'blk', 0, 0, axis_index_groups=same_core)  10.7 us
    ppermute x6, starting transfers between devices, swap(): return lax.ppermute(value, 'blk', [(i, i ^ mask) for i in range(axis_size)])  7.84 us
    ppermute x6, waiting for transfers between devices, swap(): return lax.ppermute(value, 'blk', [(i, i ^ mask) for i in range(axis_size)])  4.48 us
    unnamed x6, local copies, waits for them, and re-layouts  2.94 us
    pallas_call x1, Pallas kernels, local(): pl.pallas_call(functools.partial(score_kernel, len(pieces), shifts, by_di...  2.6 us
    pallas_call x1, Pallas kernels, local(): pl.pallas_call(pack_kernel, out_shape=jax.ShapeDtypeStruct((1, per_device...  2.14 us
    pallas_call x1, Pallas kernels, local(): pl.pallas_call(functools.partial(send_kernel, scale), out_shape=(jax.Shap...  1.1 us
    pallas_call x1, Pallas kernels, local(): pl.pallas_call(add_kernel, out_shape=jax.ShapeDtypeStruct((own_rows, full...  1.04 us
  transfers between devices with their start and end apart: 6, of which 2 were waited for; matrix products, arithmetic and copies ran while one was open for 2% of the time, Pallas kernels for 9%

profile of v4, /device:TPU:0, one launch (start us, length us, event | category | flops | bytes accessed | tf_op | source)
XLA Modules:
  0.0 35.3 jit_solution(4134859338600138350)
XLA Ops:
  0.6 0.5 %collective-permute-start.1 = (bf16[32,8192]{1,0:T(8,128)(2,1)}, bf16[32,8192]{1,0:T(8,128)(2,1)S(1)}, u32[]{:S(2)}, u32[]{:S(2)}) collective-permute-start(bf16[32,8192]{1,0:T(8,128)(2,1)} %bitcast.3), channel_id=1, source_target_pairs={{0,1},{1,0},{2,3},{3,2},{4,5},{5,4},{6,7},{7,6},{8,9},{9,8},{10,11... | collective-permute-start | bytes 1572872 | tf_op jit(solution)/shard_map/ppermute | solution.py:337
  1.1 2.1 %pack.1 = bf16[1,2,8320]{2,1,0:T(2,128)(2,1)} custom-call(bf16[2,8192]{1,0:T(2,128)(2,1)} %images_hbm.1, s32[2]{0:T(128)} %group_hbm.1, s32[2]{0:T(128)} %limit_hbm.1, s32[2,2,9]{2,1,0:T(2,128)} %bitcast.6), custom_call_target="tpu_custom_call" | custom-call | tf_op jit(solution)/shard_map/pack/pallas_call | solution.py:339
  3.3 2.6 %collective-permute-start = (bf16[1,2,8320]{2,1,0:T(2,128)(2,1)}, bf16[1,2,8320]{2,1,0:T(2,128)(2,1)S(1)}, u32[]{:S(2)}, u32[]{:S(2)}) collective-permute-start(bf16[1,2,8320]{2,1,0:T(2,128)(2,1)} %pack.1), channel_id=1, source_target_pairs={{0,2},{1,3},{2,0},{3,1},{4,6},{5,7},{6,4},{7,5},{8,10},{9,11},{10,... | collective-permute-start | bytes 99848 | tf_op jit(solution)/shard_map/ppermute | solution.py:337
  5.9 0.8 %dynamic_update_slice.6 = bf16[2,2,8320]{2,1,0:T(2,128)(2,1)S(1)} pad(bf16[1,2,8320]{2,1,0:T(2,128)(2,1)} %pack.1, bf16[]{:T(256)} %constant.0.clone.1), padding=0_1x0_0x0_0 | pad | bytes 99842 | tf_op jit(solution)/shard_map/dynamic_update_slice | solution.py:388
  6.7 0.0 collective-permute-done.1.other_ref
  6.7 0.0 copy-start
  6.8 1.0 %copy-done = bf16[2,16,8192]{2,1,0:T(8,128)(2,1)S(1)} copy-done((bf16[2,16,8192]{2,1,0:T(8,128)(2,1)S(1)}, bf16[2,16,8192]{2,1,0:T(8,128)(2,1)}, u32[]{:S(2)}) %copy-start) | copy-done | bytes 524312
  7.8 0.3 power.1
  8.1 0.0 collective-permute-done
  8.2 4.0 %collective-permute-start.4 = (bf16[2,2,8320]{2,1,0:T(2,128)(2,1)S(1)}, bf16[2,2,8320]{2,1,0:T(2,128)(2,1)S(1)}, u32[]{:S(2)}, u32[]{:S(2)}) collective-permute-start(bf16[2,2,8320]{2,1,0:T(2,128)(2,1)S(1)} %constant_dynamic-update-slice_fusion.refs_0_), channel_id=1, source_target_pairs={{0,12},{1,13},{2,14},{3,15},{4,8},{5,9},{6,10},{7,11},{8,4},{9,5},... | collective-permute-start | bytes 199688 | tf_op jit(solution)/shard_map/ppermute | solution.py:337
  12.2 0.0 collective-permute-start.3
  12.2 0.6 %collective-permute-start.2 = (bf16[2,2,8320]{2,1,0:T(2,128)(2,1)S(1)}, bf16[2,2,8320]{2,1,0:T(2,128)(2,1)S(1)}, u32[]{:S(2)}, u32[]{:S(2)}) collective-permute-start(bf16[2,2,8320]{2,1,0:T(2,128)(2,1)S(1)} %constant_dynamic-update-slice_fusion.refs_0_), channel_id=1, source_target_pairs={{0,4},{1,5},{2,6},{3,7},{4,0},{5,1},{6,2},{7,3},{8,12},{9,13},{10,... | collective-permute-start | bytes 199688 | tf_op jit(solution)/shard_map/ppermute | solution.py:337
  12.8 0.0 copy-start.1
  12.9 0.9 %copy-done.1 = f32[16,4096]{1,0:T(8,128)S(1)} copy-done((f32[16,4096]{1,0:T(8,128)S(1)}, f32[16,4096]{1,0:T(8,128)}, u32[]{:S(2)}) %copy-start.1) | copy-done | bytes 262168
  13.8 0.0 copy-start.2
  13.8 0.9 %copy-done.2 = f32[16,4096]{1,0:T(8,128)S(1)} copy-done((f32[16,4096]{1,0:T(8,128)S(1)}, f32[16,4096]{1,0:T(8,128)}, u32[]{:S(2)}) %copy-start.2) | copy-done | bytes 262168
  14.8 0.1 tables.1.refs_7_
  14.9 0.0 collective-permute-done.4.refs_3_
  14.9 3.0 %collective-permute-done.3.refs_2_ = bf16[2,2,8320]{2,1,0:T(2,128)(2,1)S(1)} collective-permute-done((bf16[2,2,8320]{2,1,0:T(2,128)(2,1)S(1)}, bf16[2,2,8320]{2,1,0:T(2,128)(2,1)S(1)}, u32[]{:S(2)}, u32[]{:S(2)}) %collective-permute-start.3) | collective-permute-done | bytes 66592 | tf_op jit(solution)/shard_map/ppermute | solution.py:337
  17.9 0.0 collective-permute-done.2.refs_1_
  17.9 2.6 %scores.1 = (bf16[144,8192]{1,0:T(8,128)(2,1)S(1)}, f32[1,32,144]{2,1,0:T(8,128)S(1)}, f32[1,32,144]{2,1,0:T(8,128)S(1)}, f32[8,1,128]{2,1,0:T(1,128)S(1)}) custom-call(bf16[2,2,8320]{2,1,0:T(2,128)(2,1)S(1)} %constant_dynamic-update-slice_fusion.refs_0_, bf16[2,2,8320]{2,1,0:T(2,128)(2,1)S(1)} %collective-permute-done.2.refs_1_, ...), custom_call_target="tpu_custom_call" | custom-call | tf_op jit(solution)/shard_map/scores/pallas_call | solution.py:399
  20.5 10.7 %all_to_all.5.stats_ref = f32[8,1,128]{2,1,0:T(1,128)S(1)} all-to-all(f32[8,1,128]{2,1,0:T(1,128)S(1)} %get-tuple-element.27), channel_id=1, replica_groups={{0,2,4,6,8,10,12,14},{1,3,5,7,9,11,13,15},{16,18,20,22,24,26,28,30},{17..., dimensions={0} | all-to-all | bytes 8192 | tf_op jit(solution)/shard_map/all_to_all | solution.py:420
  31.2 1.1 %send.1 = (bf16[32,8192]{1,0:T(8,128)(2,1)S(1)}, bf16[1,32,144]{2,1,0:T(8,128)(2,1)S(1)}, f32[2]{0:T(128)}, f32[2]{0:T(128)}) custom-call(f32[8,1,128]{2,1,0:T(1,128)S(1)} %all_to_all.5.stats_ref, f32[1,32,144]{2,1,0:T(8,128)S(1)} %get-tuple-element.28.exps_own_ref, f32[1,32,144]{2,1,0:T(8,128)S(1)} %get-tuple-element.29.exps_other_ref, ...), custom_call_target="tpu_custom_call" | custom-call | tf_op jit(solution)/shard_map/send/pallas_call | solution.py:423
  32.3 0.1 collective-permute-start.5
  32.4 0.5 %keep.1.keep_ref = f32[32,8192]{1,0:T(8,128)S(1)} custom-call(bf16[1,32,144]{2,1,0:T(8,128)(2,1)S(1)} %get-tuple-element.31.posterior_ref, bf16[144,8192]{1,0:T(8,128)(2,1)S(1)} %get-tuple-element.30.weighted_ref), custom_call_target="tpu_custom_call" | custom-call | flops 75497472 | bytes 1048576 | tf_op jit(solution)/shard_map/keep/pallas_call | solution.py:443
  32.9 1.4 %collective-permute-done.5.received_ref = bf16[32,8192]{1,0:T(8,128)(2,1)S(1)} collective-permute-done((bf16[32,8192]{1,0:T(8,128)(2,1)S(1)}, bf16[32,8192]{1,0:T(8,128)(2,1)S(1)}, u32[]{:S(2)}, u32[]{:S(2)}) %collective-permute-start.5) | collective-permute-done | bytes 524320 | tf_op jit(solution)/shard_map/ppermute | solution.py:337
  34.3 1.0 %add.3 = f32[32,8192]{1,0:T(8,128)} custom-call(f32[32,8192]{1,0:T(8,128)S(1)} %keep.1.keep_ref, bf16[32,8192]{1,0:T(8,128)(2,1)S(1)} %collective-permute-done.5.received_ref), custom_call_target="tpu_custom_call" | custom-call | tf_op jit(solution)/shard_map/add/pallas_call | solution.py:456
  (1 shorter events, 0.0 us)
Async XLA Ops:
  0.6 6.1 %collective-permute-start.1 = (bf16[32,8192]{1,0:T(8,128)(2,1)}, bf16[32,8192]{1,0:T(8,128)(2,1)S(1)}, u32[]{:S(2)}, u32[]{:S(2)}) collective-permute-start(bf16[32,8192]{1,0:T(8,128)(2,1)} %bitcast.3), channel_id=1, source_target_pairs={{0,1},{1,0},{2,3},{3,2},{4,5},{5,4},{6,7},{7,6},{8,9},{9,8},{10,11... | collective-permute-start | bytes 1572872 | tf_op jit(solution)/shard_map/ppermute | solution.py:337
  3.3 4.9 %collective-permute-start = (bf16[1,2,8320]{2,1,0:T(2,128)(2,1)}, bf16[1,2,8320]{2,1,0:T(2,128)(2,1)S(1)}, u32[]{:S(2)}, u32[]{:S(2)}) collective-permute-start(bf16[1,2,8320]{2,1,0:T(2,128)(2,1)} %pack.1), channel_id=1, source_target_pairs={{0,2},{1,3},{2,0},{3,1},{4,6},{5,7},{6,4},{7,5},{8,10},{9,11},{10,... | collective-permute-start | bytes 99848 | tf_op jit(solution)/shard_map/ppermute | solution.py:337
  6.7 1.0 %copy-start = (bf16[2,16,8192]{2,1,0:T(8,128)(2,1)S(1)}, bf16[2,16,8192]{2,1,0:T(8,128)(2,1)}, u32[]{:S(2)}) copy-start(bf16[2,16,8192]{2,1,0:T(8,128)(2,1)} %param.7) | copy-start | bytes 1572868
  8.2 6.7 %collective-permute-start.4 = (bf16[2,2,8320]{2,1,0:T(2,128)(2,1)S(1)}, bf16[2,2,8320]{2,1,0:T(2,128)(2,1)S(1)}, u32[]{:S(2)}, u32[]{:S(2)}) collective-permute-start(bf16[2,2,8320]{2,1,0:T(2,128)(2,1)S(1)} %constant_dynamic-update-slice_fusion.refs_0_), channel_id=1, source_target_pairs={{0,12},{1,13},{2,14},{3,15},{4,8},{5,9},{6,10},{7,11},{8,4},{9,5},... | collective-permute-start | bytes 199688 | tf_op jit(solution)/shard_map/ppermute | solution.py:337
  12.2 5.7 %collective-permute-start.3 = (bf16[2,2,8320]{2,1,0:T(2,128)(2,1)S(1)}, bf16[2,2,8320]{2,1,0:T(2,128)(2,1)S(1)}, u32[]{:S(2)}, u32[]{:S(2)}) collective-permute-start(bf16[2,2,8320]{2,1,0:T(2,128)(2,1)S(1)} %constant_dynamic-update-slice_fusion.refs_0_), channel_id=1, source_target_pairs={{0,8},{1,9},{2,10},{3,11},{4,12},{5,13},{6,14},{7,15},{8,0},{9,1},... | collective-permute-start | bytes 199688 | tf_op jit(solution)/shard_map/ppermute | solution.py:337
  12.2 5.7 %collective-permute-start.2 = (bf16[2,2,8320]{2,1,0:T(2,128)(2,1)S(1)}, bf16[2,2,8320]{2,1,0:T(2,128)(2,1)S(1)}, u32[]{:S(2)}, u32[]{:S(2)}) collective-permute-start(bf16[2,2,8320]{2,1,0:T(2,128)(2,1)S(1)} %constant_dynamic-update-slice_fusion.refs_0_), channel_id=1, source_target_pairs={{0,4},{1,5},{2,6},{3,7},{4,0},{5,1},{6,2},{7,3},{8,12},{9,13},{10,... | collective-permute-start | bytes 199688 | tf_op jit(solution)/shard_map/ppermute | solution.py:337
  12.8 0.9 %copy-start.1 = (f32[16,4096]{1,0:T(8,128)S(1)}, f32[16,4096]{1,0:T(8,128)}, u32[]{:S(2)}) copy-start(f32[16,4096]{1,0:T(8,128)} %ctf_ref.1) | copy-start | bytes 786436
  13.8 0.9 %copy-start.2 = (f32[16,4096]{1,0:T(8,128)S(1)}, f32[16,4096]{1,0:T(8,128)}, u32[]{:S(2)}) copy-start(f32[16,4096]{1,0:T(8,128)} %noise_ref.1) | copy-start | bytes 786436
  32.3 2.0 %collective-permute-start.5 = (bf16[32,8192]{1,0:T(8,128)(2,1)S(1)}, bf16[32,8192]{1,0:T(8,128)(2,1)S(1)}, u32[]{:S(2)}, u32[]{:S(2)}) collective-permute-start(bf16[32,8192]{1,0:T(8,128)(2,1)S(1)} %get-tuple-element.32), channel_id=1, source_target_pairs={{0,1},{1,0},{2,3},{3,2},{4,5},{5,4},{6,7},{7,6},{8,9},{9,8},{10,11... | collective-permute-start | bytes 1572872 | tf_op jit(solution)/shard_map/ppermute | solution.py:337

commit v5 on v3

v5 whole, which is shorter than its diff:
```python
import functools
import math

import jax
import jax.numpy as jnp
from jax import lax
from jax.experimental import pallas as pl
from jax.experimental.pallas import tpu as pltpu
from jax.sharding import PartitionSpec as P

KY = 64
IMG = 256
LANES = 128
ROWS = 8
NEAR = 4
LIMIT_AT = 1
X_AT = 16
Y_AT = 48

VMEM = pl.BlockSpec(memory_space=pltpu.VMEM)
HBM = pl.BlockSpec(memory_space=pltpu.HBM)
NT = (((1,), (1,)), ((), ()))


def sin_cos(turns):
    quarter = IMG // 4
    wrapped = (turns + quarter // 2) & (IMG - 1)
    quadrant = wrapped >> int(math.log2(quarter))
    angle = (wrapped - quadrant * quarter - quarter // 2).astype(jnp.float32) * (
        2.0 * math.pi / IMG
    )
    square = angle * angle
    even = 1.0 + square * (
        -1.0 / 2 + square * (1.0 / 24 + square * (-1.0 / 720 + square * (1.0 / 40320)))
    )
    odd = angle * (
        1.0
        + square
        * (-1.0 / 6 + square * (1.0 / 120 + square * (-1.0 / 5040 + square * (1.0 / 362880))))
    )
    swapped = (quadrant & 1) == 1
    cosine = jnp.where(swapped, odd, even)
    sine = jnp.where(swapped, even, odd)
    cosine = jnp.where((quadrant == 1) | (quadrant == 2), -cosine, cosine)
    sine = jnp.where(quadrant >= 2, -sine, sine)
    return cosine, sine


def split_halves(value):
    high = value.astype(jnp.bfloat16)
    return high, (value - high.astype(jnp.float32)).astype(jnp.bfloat16)


def pack_kernel(images_hbm, group_hbm, limit_hbm, offsets_hbm, packed_ref, group, limit, offsets, sems):
    per_device, full = images_hbm.shape
    shifts = offsets_hbm.shape[2]
    copies = [
        pltpu.make_async_copy(images_hbm, packed_ref.at[0, :, pl.ds(0, full)], sems.at[0]),
        pltpu.make_async_copy(group_hbm, group, sems.at[1]),
        pltpu.make_async_copy(limit_hbm, limit, sems.at[2]),
        pltpu.make_async_copy(offsets_hbm, offsets, sems.at[3]),
    ]
    for copy in copies:
        copy.start()
    for copy in copies[1:]:
        copy.wait()
    row = lax.broadcasted_iota(jnp.int32, (per_device, LANES), 0)
    lane = lax.broadcasted_iota(jnp.int32, (per_device, LANES), 1)
    numbers = jnp.zeros((per_device, LANES), jnp.int32)
    for particle in range(per_device):
        line = jnp.zeros((per_device, LANES), jnp.int32)
        line = jnp.where(lane == 0, group[particle], line)
        line = jnp.where(lane == LIMIT_AT, limit[particle], line)
        for shift in range(shifts):
            line = jnp.where(lane == X_AT + shift, offsets[particle, 0, shift], line)
            line = jnp.where(lane == Y_AT + shift, offsets[particle, 1, shift], line)
        numbers = jnp.where(row == particle, line, numbers)
    packed_ref[0, :, pl.ds(full, LANES)] = numbers.astype(jnp.float32).astype(jnp.bfloat16)
    copies[0].wait()


def split_thirds(value):
    high = value.astype(jnp.bfloat16)
    rest = value - high.astype(jnp.float32)
    middle = rest.astype(jnp.bfloat16)
    return high, middle, (rest - middle.astype(jnp.float32)).astype(jnp.bfloat16)


def power_kernel(own_ref, other_ref, both_ref, high_ref, low_ref):
    rows, full = own_ref.shape
    half = full // 2
    for place, ref in enumerate((own_ref, other_ref)):
        at = pl.ds(place * rows, rows)
        both_ref[at, :] = ref[...]
        real = ref[:, :half].astype(jnp.float32)
        imag = ref[:, half:].astype(jnp.float32)
        high, low = split_halves(real * real + imag * imag)
        high_ref[at, :] = high
        low_ref[at, :] = low


def table_kernel(ctf_ref, noise_ref, table_ref):
    groups, half = ctf_ref.shape
    for place, ref in enumerate((ctf_ref, noise_ref)):
        for third, part in enumerate(split_thirds(ref[...])):
            table_ref[pl.ds(third * groups, groups), pl.ds(place * half, half)] = part


def score_kernel(sources, by_distance, shifts, has_earlier, *refs):
    pieces = refs[: len(sources)]
    refs = refs[len(sources) :]
    both_ref, high_ref, low_ref, table_ref = refs[:4]
    refs = refs[4:]
    if has_earlier:
        earlier_own_ref, earlier_other_ref, earlier_stats_ref = refs[:3]
        refs = refs[3:]
    weighted_ref, exps_ref, exps_other_ref, stats_ref = refs[:4]
    image_ref, real_ref, imag_ref, cross_ref, square_ref = refs[4:]
    full = both_ref.shape[1]
    half = full // 2
    groups = table_ref.shape[0] // 3
    candidates = both_ref.shape[0]
    rows_total = image_ref.shape[0]
    per_device = pieces[0].shape[1]
    scale = 0.5 / math.sqrt(half)
    chip = lax.axis_index("blk") >> 1
    for piece, places in zip(pieces, sources):
        for row, place in enumerate(places):
            if by_distance:
                place = (chip ^ place) & (NEAR - 1)
            values = piece[row].astype(jnp.float32)
            for sub in range(per_device):
                image_ref[pl.ds(place * per_device + sub, 1), :] = values[sub : sub + 1]

    block_rows = shifts * ROWS
    slot = 1 if has_earlier else 0
    if has_earlier:
        exps_ref[0] = earlier_own_ref[0]
        exps_other_ref[0] = earlier_other_ref[0]

    def block(index, carry):
        rows = pl.ds(pl.multiple_of(index * ROWS, ROWS), ROWS)
        first = pl.multiple_of(index * block_rows, ROWS)
        numbers = image_ref[rows, full:]
        column = lax.broadcasted_iota(jnp.int32, (ROWS, 3 * groups), 1) % groups
        one_hot = (numbers[:, :1].astype(jnp.int32) == column).astype(jnp.bfloat16)
        tables = jnp.dot(one_hot, table_ref[...], preferred_element_type=jnp.float32)
        ctf = tables[:, :half]
        noise = tables[:, half:]
        limit = numbers[:, LIMIT_AT : LIMIT_AT + 1].astype(jnp.int32)
        position = lax.broadcasted_iota(jnp.int32, (ROWS, half), 1)
        freq_x = position >> int(math.log2(KY))
        freq_y = (position & (KY - 1)) - KY // 2
        weight = jnp.where(freq_x * freq_x + freq_y * freq_y < limit * limit, noise, 0.0)
        ctf_weight = weight * ctf
        real = image_ref[rows, :half]
        imag = image_ref[rows, half:full]
        norm = jnp.sum(weight * (real * real + imag * imag), axis=1, keepdims=True)
        real_ref[...] = ctf_weight * real
        imag_ref[...] = ctf_weight * imag
        quad_high, quad_low = split_halves(ctf_weight * ctf)
        quad_weight = jnp.concatenate([quad_high, quad_low], axis=0)
        quad = lax.dot_general(
            quad_weight, high_ref[...], NT, preferred_element_type=jnp.float32
        ) + lax.dot_general(quad_weight, low_ref[...], NT, preferred_element_type=jnp.float32)
        quad = quad[:ROWS] + quad[ROWS:]

        numbers_int = numbers.astype(jnp.int32)
        step_cos, step_sin = sin_cos(numbers_int * (LANES // KY))
        for start in range(0, shifts, 2):
            members = range(start, min(start + 2, shifts))

            def stacked(value, base):
                return jnp.concatenate(
                    [value[:, base + shift : base + shift + 1] for shift in members], axis=0
                )

            height = len(members) * ROWS
            lane = lax.broadcasted_iota(jnp.int32, (height, LANES), 1)
            turns = (lane >> int(math.log2(KY))) * stacked(numbers_int, X_AT) + (
                (lane & (KY - 1)) - KY // 2
            ) * stacked(numbers_int, Y_AT)
            cosine, sine = sin_cos(turns)
            turn_cos = stacked(step_cos, X_AT)
            turn_sin = stacked(step_sin, X_AT)
            cosine_before = cosine * turn_cos + sine * turn_sin
            sine_before = sine * turn_cos - cosine * turn_sin
            double = jnp.broadcast_to(2.0 * turn_cos, (height, LANES))
            out_rows = pl.ds(first + start * ROWS, height)
            for chunk in range(half // LANES):
                at = pl.ds(chunk * LANES, LANES)
                real = jnp.concatenate([real_ref[:, at]] * len(members), axis=0)
                imag = jnp.concatenate([imag_ref[:, at]] * len(members), axis=0)
                weighted_ref[out_rows, at] = (real * cosine + imag * sine).astype(jnp.bfloat16)
                weighted_ref[out_rows, pl.ds(half + chunk * LANES, LANES)] = (
                    imag * cosine - real * sine
                ).astype(jnp.bfloat16)
                cosine, cosine_before = double * cosine - cosine_before, cosine
                sine, sine_before = double * sine - sine_before, sine

        cross_ref[...] = lax.dot_general(
            weighted_ref[pl.ds(first, block_rows), :],
            both_ref[...],
            NT,
            preferred_element_type=jnp.float32,
        )
        base = norm + quad
        scores = [
            -(base - 2.0 * cross_ref[pl.ds(shift * ROWS, ROWS), :]) * scale
            for shift in range(shifts)
        ]
        top = jnp.max(functools.reduce(jnp.maximum, scores), axis=1, keepdims=True)
        exps = [jnp.exp(score - top) for score in scores]
        total = jnp.sum(functools.reduce(jnp.add, exps), axis=1, keepdims=True)
        for shift in range(shifts):
            square_ref[pl.ds(shift * ROWS, ROWS), :candidates] = exps[shift]
        turned = square_ref[...].T
        exps_ref[index + slot] = turned[: candidates // 2, :block_rows]
        exps_other_ref[index + slot] = turned[candidates // 2 : candidates, :block_rows]
        row = lax.broadcasted_iota(jnp.int32, (ROWS, LANES), 0)
        lane = lax.broadcasted_iota(jnp.int32, (ROWS, LANES), 1)
        line = jnp.sum(
            jnp.where(lane == row, top, jnp.where(lane == row + LANES // 2, total, 0.0)),
            axis=0,
            keepdims=True,
        )
        if has_earlier:
            first_half = chip // NEAR == 0
            before = earlier_stats_ref[0]
            line = jnp.where(first_half, before, line) + pltpu.roll(
                jnp.where(first_half, line, before), ROWS, 1
            )
        for target in range(stats_ref.shape[0]):
            stats_ref[target, pl.ds(index, 1), :] = line
        return carry

    lax.fori_loop(0, rows_total // ROWS, block, 0)


def slice_kernel(scale, calls, by_distance, *refs):
    stats_ref, exps_own_ref, exps_other_ref = refs[:3]
    weighted_refs = (refs[3 : 3 + calls], refs[3 + calls : 3 + 2 * calls])
    out_hbm, best_hbm, log_hbm = refs[3 + 2 * calls : 6 + 2 * calls]
    best_ref, log_ref, posterior_ref, summed_ref, sems, number_sems = refs[6 + 2 * calls :]
    blocks, rows, block_rows = exps_own_ref.shape
    chips = stats_ref.shape[0]
    per_device = best_ref.shape[0]
    full = out_hbm.shape[1]
    index = lax.axis_index("blk")
    chip = index >> 1
    lane = lax.broadcasted_iota(jnp.int32, (1, LANES), 1)

    def combined(core, row):
        lines = [stats_ref[source, core, pl.ds(row, 1), :] for source in range(chips)]
        top = functools.reduce(jnp.maximum, lines)
        total = functools.reduce(
            jnp.add,
            [pltpu.roll(line, LANES // 2, 1) * jnp.exp(line - top) for line in lines],
        )
        log_total = top + jnp.log(total)
        return top, log_total, stats_ref[chip, core, pl.ds(row, 1), :]

    for side, exps_ref in enumerate((exps_own_ref, exps_other_ref)):
        core = (index & 1) ^ side
        for block in range(blocks):
            if block == 0 or not by_distance:
                top, log_total, mine = combined(core, block)
                line = jnp.exp(mine - log_total)
            factor = line
            if by_distance:
                first_half = chip // NEAR == block
                factor = jnp.where(first_half, line, pltpu.roll(line, LANES - ROWS, 1))
            factor = jnp.where(lane < ROWS, factor, 0.0)
            filled = ROWS
            while filled < LANES:
                factor = factor + pltpu.roll(factor, filled, 1)
                filled *= 2
            posterior_ref[side, block] = (exps_ref[block] * factor[:, :block_rows]).astype(
                jnp.bfloat16
            )

    width = 1024
    copies = []
    for number, start in enumerate(range(0, full, width)):
        at = pl.ds(start, width)
        products = []
        for side in range(2):
            for block in range(blocks):
                call, place = divmod(block, blocks // calls)
                products.append(
                    jnp.dot(
                        posterior_ref[side, block],
                        weighted_refs[side][call][pl.ds(place * block_rows, block_rows), at],
                        preferred_element_type=jnp.float32,
                    )
                )
        summed_ref[:, at] = functools.reduce(jnp.add, products) * scale
        copy = pltpu.make_async_copy(summed_ref.at[:, at], out_hbm.at[:, at], sems.at[number])
        copy.start()
        copies.append(copy)
        if number == 0:
            for row in range(per_device):
                particle = chip * per_device + row
                if by_distance:
                    top, log_total, mine = combined(index & 1, 0)
                    chosen = lane == particle
                else:
                    top, log_total, mine = combined(index & 1, particle // ROWS)
                    chosen = lane == particle % ROWS
                best_ref[row] = jnp.sum(jnp.where(chosen, jnp.exp(top - log_total), 0.0))
                log_ref[row] = jnp.sum(jnp.where(chosen, log_total, 0.0))
            copies.append(pltpu.make_async_copy(best_ref, best_hbm, number_sems.at[0]))
            copies.append(pltpu.make_async_copy(log_ref, log_hbm, number_sems.at[1]))
            copies[-2].start()
            copies[-1].start()
    for copy in copies:
        copy.wait()


def local(
    axis_size, projections, images, ctf_group, shift_offsets, shell_limit, ctf_table, noise_weight
):
    batch_count, orient_dev, full = projections.shape
    half = full // 2
    own_rows = batch_count * orient_dev
    candidates = 2 * own_rows
    per_device = images.shape[0]
    shifts = shift_offsets.shape[1]
    chips = axis_size // 2
    particles = chips * per_device
    blocks = particles // ROWS
    block_rows = shifts * ROWS
    megabytes = 12 + -(-2 * blocks * block_rows * full * 2 // 2**20)
    params = pltpu.CompilerParams(vmem_limit_bytes=megabytes * 2**20)

    def swap(value, mask):
        return lax.ppermute(value, "blk", [(i, i ^ mask) for i in range(axis_size)])

    packed = pl.pallas_call(
        pack_kernel,
        out_shape=jax.ShapeDtypeStruct((1, per_device, full + LANES), jnp.bfloat16),
        in_specs=[HBM] * 4,
        out_specs=VMEM,
        scratch_shapes=[
            pltpu.SMEM((per_device,), jnp.int32),
            pltpu.SMEM((per_device,), jnp.int32),
            pltpu.SMEM((per_device, 2, shifts), jnp.int32),
            pltpu.SemaphoreType.DMA((4,)),
        ],
        compiler_params=pltpu.CompilerParams(vmem_limit_bytes=60 * 2**20),
        name="pack",
    )(images, ctf_group, shell_limit, shift_offsets.transpose(0, 2, 1))
    by_distance = chips == 2 * NEAR and per_device * NEAR == ROWS
    received = swap(packed, 2) if by_distance else packed
    flat = projections.reshape(own_rows, full)
    other = swap(flat, 1)
    groups = ctf_table.shape[0]
    both, high, low = pl.pallas_call(
        power_kernel,
        out_shape=(
            jax.ShapeDtypeStruct((candidates, full), jnp.bfloat16),
            jax.ShapeDtypeStruct((candidates, half), jnp.bfloat16),
            jax.ShapeDtypeStruct((candidates, half), jnp.bfloat16),
        ),
        in_specs=[VMEM] * 2,
        out_specs=(VMEM,) * 3,
        compiler_params=params,
        cost_estimate=pl.CostEstimate(
            flops=8 * candidates * full, bytes_accessed=4 * candidates * full, transcendentals=0
        ),
        name="power",
    )(flat, other)
    tables = pl.pallas_call(
        table_kernel,
        out_shape=jax.ShapeDtypeStruct((3 * groups, full), jnp.bfloat16),
        in_specs=[VMEM] * 2,
        out_specs=VMEM,
        compiler_params=params,
        cost_estimate=pl.CostEstimate(
            flops=6 * groups * full, bytes_accessed=10 * groups * full, transcendentals=0
        ),
        name="tables",
    )(ctf_table, noise_weight)
    if by_distance:
        pair = jnp.zeros((2,) + packed.shape[1:], packed.dtype)
        pair = lax.dynamic_update_slice(pair, packed, (0, 0, 0))
        pair, received, both, high, low = lax.optimization_barrier(
            (pair, received, both, high, low)
        )
        pair = lax.dynamic_update_slice(pair, received, (1, 0, 0))
        pieces = [pair] + [swap(pair, mask) for mask in range(4, axis_size, 4)]
        parts = [(pieces[:2], ((0, 1), (2, 3))), (pieces[2:], ((4, 5), (6, 7)))]
    else:
        same_core = [[2 * c + core for c in range(chips)] for core in range(2)]
        gathered = lax.all_gather(
            packed, "blk", axis=0, tiled=True, axis_index_groups=same_core
        )
        parts = [([gathered], (tuple(range(chips)),))]

    all_weighted = []
    earlier = ()
    for pieces, sources in parts:
        last = len(all_weighted) == len(parts) - 1
        own_blocks = blocks // len(parts)
        seen = blocks if last else own_blocks
        weighted, *earlier = pl.pallas_call(
            functools.partial(score_kernel, sources, by_distance, shifts, bool(earlier)),
            out_shape=(
                jax.ShapeDtypeStruct((own_blocks * block_rows, full), jnp.bfloat16),
                jax.ShapeDtypeStruct((seen, own_rows, block_rows), jnp.float32),
                jax.ShapeDtypeStruct((seen, own_rows, block_rows), jnp.float32),
                jax.ShapeDtypeStruct(
                    (axis_size if last else 1, 1 if by_distance else blocks, LANES), jnp.float32
                ),
            ),
            in_specs=[VMEM] * (len(pieces) + 4 + len(earlier)),
            out_specs=(VMEM,) * 4,
            scratch_shapes=[
                pltpu.VMEM((own_blocks * ROWS, full + LANES), jnp.float32),
                pltpu.VMEM((ROWS, half), jnp.float32),
                pltpu.VMEM((ROWS, half), jnp.float32),
                pltpu.VMEM((block_rows, candidates), jnp.float32),
                pltpu.VMEM((-(-block_rows // LANES) * LANES, LANES), jnp.float32),
            ],
            compiler_params=params,
            cost_estimate=pl.CostEstimate(
                flops=2 * own_blocks * block_rows * full * (candidates + 8),
                bytes_accessed=2 * own_blocks * block_rows * full,
                transcendentals=0,
            ),
            name="scores",
        )(*pieces, both, high, low, tables, *earlier)
        all_weighted.append(weighted)
    exps, exps_other, stats = earlier

    exchanged = [swap(weighted, 1) for weighted in all_weighted]
    exps_in = swap(exps_other, 1)
    gathered = lax.all_to_all(stats, "blk", 0, 0)
    gathered = gathered.reshape((chips, 2) + gathered.shape[1:])

    slices, best_posterior, log_total = pl.pallas_call(
        functools.partial(
            slice_kernel, own_rows / per_device, len(all_weighted), by_distance
        ),
        out_shape=(
            jax.ShapeDtypeStruct((own_rows, full), jnp.float32),
            jax.ShapeDtypeStruct((per_device,), jnp.float32),
            jax.ShapeDtypeStruct((per_device,), jnp.float32),
        ),
        in_specs=[VMEM] * (3 + 2 * len(all_weighted)),
        out_specs=(HBM, HBM, HBM),
        scratch_shapes=[
            pltpu.SMEM((per_device,), jnp.float32),
            pltpu.SMEM((per_device,), jnp.float32),
            pltpu.VMEM((2, blocks, own_rows, block_rows), jnp.bfloat16),
            pltpu.VMEM((own_rows, full), jnp.float32),
            pltpu.SemaphoreType.DMA((full // 1024,)),
            pltpu.SemaphoreType.DMA((2,)),
        ],
        compiler_params=params,
        name="slices",
    )(gathered, exps, exps_in, *all_weighted, *exchanged)
    return (slices.reshape(batch_count, orient_dev, full), best_posterior, log_total)


def solution(mesh):
    in_specs = (
        P(None, ("groups", "blk"), None),
        P(("groups", "blk"), None),
        P(("groups", "blk")),
        P(("groups", "blk"), None, None),
        P(("groups", "blk")),
        P("groups", None),
        P("groups", None),
    )
    out_specs = (P(None, ("groups", "blk"), None), P(("groups", "blk")), P(("groups", "blk")))
    return jax.shard_map(
        functools.partial(local, mesh.shape["blk"]),
        mesh=mesh,
        in_specs=in_specs,
        out_specs=out_specs,
        check_vma=False,
    )
```

time: 34.8 us -> 33.7 us (0.968)
  waiting for transfers between devices: 3.04 us -> 4.8 us
  local copies, waits for them, and re-layouts: 2.94 us -> 1.91 us
  other arithmetic: 0.86 us -> 0 us
  blocking collectives: 11.4 us -> 10.6 us
    unnamed x6, local copies, waits for them, and re-layouts: 2.94 us -> 1.04 us
    ppermute x7 -> x8, waiting for transfers between devices: 3.04 us -> 4.8 us  [swap(): return lax.ppermute(value, 'blk', [(i, i ^ mask) for i in range(axis_size)])]
    dynamic_update_slice x0 -> x2, local copies, waits for them, and re-layouts: none -> 0.87 us  [the longest x1 0.83 us: local(): pair = lax.dynamic_update_slice(pair, packed, (0, 0, 0))]
    concatenate x1 -> x0, other arithmetic: 0.86 us -> none  [local(): jnp.concatenate([packed, swap(packed, 2)], axis=0)]
    all_to_all x1, blocking collectives: 11.4 us -> 10.6 us  [local(): gathered = lax.all_to_all(stats, 'blk', 0, 0)]
    pallas_call x2 -> x4, Pallas kernels: 4.9 us -> 5.26 us  [the longest x2 3.08 us: local(): pl.pallas_call(functools.partial(score_kernel, sources, by_distance, shif...]
    pallas_call x1, Pallas kernels: 0.69 us -> 0.33 us  [local(): pl.pallas_call(power_kernel, out_shape=(jax.ShapeDtypeStruct((candidates,...]
    ppermute x7 -> x8, starting transfers between devices: 8.41 us -> 8.28 us  [swap(): return lax.ppermute(value, 'blk', [(i, i ^ mask) for i in range(axis_size)])]
  transfers between devices with their start and end apart: 7 -> 8, of which waited for: 2 -> 2; matrix products, arithmetic and copies ran while one was open for 2% -> 2% of each run, Pallas kernels for 2% -> 10%
where the time goes in v5:
time: 33.7 us; the launch traced here: 33.3 us
  blocking collectives  10.6 us (31%)
  starting transfers between devices  8.28 us (25%)
  Pallas kernels  7.1 us (21%)
  waiting for transfers between devices  4.8 us (14%)
  local copies, waits for them, and re-layouts  1.91 us (6%)
  between operations  0.7 us (2%)
    all_to_all x1, blocking collectives, local(): gathered = lax.all_to_all(stats, 'blk', 0, 0)  10.6 us
    ppermute x8, starting transfers between devices, swap(): return lax.ppermute(value, 'blk', [(i, i ^ mask) for i in range(axis_size)])  8.28 us
    ppermute x8, waiting for transfers between devices, swap(): return lax.ppermute(value, 'blk', [(i, i ^ mask) for i in range(axis_size)])  4.8 us
    pallas_call x2, Pallas kernels, local(): pl.pallas_call(functools.partial(score_kernel, sources, by_distance, shif...  3.08 us
    pallas_call x1, Pallas kernels, local(): pl.pallas_call(functools.partial(slice_kernel, own_rows / per_device, len...  2.04 us
    pallas_call x1, Pallas kernels, local(): pl.pallas_call(pack_kernel, out_shape=jax.ShapeDtypeStruct((1, per_device...  1.51 us
    unnamed x6, local copies, waits for them, and re-layouts  1.04 us
    dynamic_update_slice x1, local copies, waits for them, and re-layouts, local(): pair = lax.dynamic_update_slice(pair, packed, (0, 0, 0))  0.83 us
  transfers between devices with their start and end apart: 8, of which 2 were waited for; matrix products, arithmetic and copies ran while one was open for 2% of the time, Pallas kernels for 10%

profile of v5, /device:TPU:0, one launch (start us, length us, event | category | flops | bytes accessed | tf_op | source)
XLA Modules:
  0.0 33.3 jit_solution(12066647717106058133)
XLA Ops:
  0.6 0.5 %collective-permute-start.1 = (bf16[32,8192]{1,0:T(8,128)(2,1)}, bf16[32,8192]{1,0:T(8,128)(2,1)S(1)}, u32[]{:S(2)}, u32[]{:S(2)}) collective-permute-start(bf16[32,8192]{1,0:T(8,128)(2,1)} %bitcast.4), channel_id=1, source_target_pairs={{0,1},{1,0},{2,3},{3,2},{4,5},{5,4},{6,7},{7,6},{8,9},{9,8},{10,11... | collective-permute-start | bytes 1572872 | tf_op jit(solution)/shard_map/ppermute | solution.py:337
  1.1 1.5 %pack.1 = bf16[1,2,8320]{2,1,0:T(2,128)(2,1)} custom-call(bf16[2,8192]{1,0:T(2,128)(2,1)} %images_hbm.1, s32[2]{0:T(128)} %group_hbm.1, s32[2]{0:T(128)} %limit_hbm.1, s32[2,2,9]{2,1,0:T(2,128)} %bitcast.7), custom_call_target="tpu_custom_call" | custom-call | tf_op jit(solution)/shard_map/pack/pallas_call | solution.py:339
  2.7 2.6 %collective-permute-start = (bf16[1,2,8320]{2,1,0:T(2,128)(2,1)}, bf16[1,2,8320]{2,1,0:T(2,128)(2,1)S(1)}, u32[]{:S(2)}, u32[]{:S(2)}) collective-permute-start(bf16[1,2,8320]{2,1,0:T(2,128)(2,1)} %pack.1), channel_id=1, source_target_pairs={{0,2},{1,3},{2,0},{3,1},{4,6},{5,7},{6,4},{7,5},{8,10},{9,11},{10,... | collective-permute-start | bytes 99848 | tf_op jit(solution)/shard_map/ppermute | solution.py:337
  5.3 0.8 %dynamic_update_slice.6 = bf16[2,2,8320]{2,1,0:T(2,128)(2,1)S(1)} pad(bf16[1,2,8320]{2,1,0:T(2,128)(2,1)} %pack.1, bf16[]{:T(256)} %constant.0.clone.1), padding=0_1x0_0x0_0 | pad | bytes 99842 | tf_op jit(solution)/shard_map/dynamic_update_slice | solution.py:386
  6.1 0.0 collective-permute-done.1.other_ref
  6.1 0.0 copy-start
  6.1 1.0 %copy-done = bf16[2,16,8192]{2,1,0:T(8,128)(2,1)S(1)} copy-done((bf16[2,16,8192]{2,1,0:T(8,128)(2,1)S(1)}, bf16[2,16,8192]{2,1,0:T(8,128)(2,1)}, u32[]{:S(2)}) %copy-start) | copy-done | bytes 524312
  7.2 0.0 copy-start.1
  7.2 0.0 copy-start.2
  7.2 0.3 power.1
  7.5 0.0 collective-permute-done
  7.6 2.0 %collective-permute-start.4 = (bf16[2,2,8320]{2,1,0:T(2,128)(2,1)S(1)}, bf16[2,2,8320]{2,1,0:T(2,128)(2,1)S(1)}, u32[]{:S(2)}, u32[]{:S(2)}) collective-permute-start(bf16[2,2,8320]{2,1,0:T(2,128)(2,1)S(1)} %constant_dynamic-update-slice_fusion.refs_0_), channel_id=1, source_target_pairs={{0,4},{1,5},{2,6},{3,7},{4,0},{5,1},{6,2},{7,3},{8,12},{9,13},{10,... | collective-permute-start | bytes 199688 | tf_op jit(solution)/shard_map/ppermute | solution.py:337
  9.5 2.5 %collective-permute-start.3 = (bf16[2,2,8320]{2,1,0:T(2,128)(2,1)S(1)}, bf16[2,2,8320]{2,1,0:T(2,128)(2,1)S(1)}, u32[]{:S(2)}, u32[]{:S(2)}) collective-permute-start(bf16[2,2,8320]{2,1,0:T(2,128)(2,1)S(1)} %constant_dynamic-update-slice_fusion.refs_0_), channel_id=1, source_target_pairs={{0,12},{1,13},{2,14},{3,15},{4,8},{5,9},{6,10},{7,11},{8,4},{9,5},... | collective-permute-start | bytes 199688 | tf_op jit(solution)/shard_map/ppermute | solution.py:337
  12.0 0.1 collective-permute-start.2
  12.1 0.0 copy-done.1
  12.1 0.0 copy-done.2
  12.1 0.1 tables.1.refs_5_
  12.3 0.0 collective-permute-done.4.refs_1_
  12.3 1.5 %scores.2 = (bf16[72,8192]{1,0:T(8,128)(2,1)S(1)}, f32[1,32,72]{2,1,0:T(8,128)S(1)}, f32[1,32,72]{2,1,0:T(8,128)S(1)}, f32[1,1,128]{2,1,0:T(1,128)S(1)}) custom-call(bf16[2,2,8320]{2,1,0:T(2,128)(2,1)S(1)} %constant_dynamic-update-slice_fusion.refs_0_, bf16[2,2,8320]{2,1,0:T(2,128)(2,1)S(1)} %collective-permute-done.4.refs_1_, ...), custom_call_target="tpu_custom_call" | custom-call | flops 84934656 | bytes 1179648 | tf_op jit(solution)/shard_map/scores/pallas_call | solution.py:406
  13.8 2.6 %collective-permute-done.3.refs_1_ = bf16[2,2,8320]{2,1,0:T(2,128)(2,1)S(1)} collective-permute-done((bf16[2,2,8320]{2,1,0:T(2,128)(2,1)S(1)}, bf16[2,2,8320]{2,1,0:T(2,128)(2,1)S(1)}, u32[]{:S(2)}, u32[]{:S(2)}) %collective-permute-start.3) | collective-permute-done | bytes 66592 | tf_op jit(solution)/shard_map/ppermute | solution.py:337
  16.4 2.1 %collective-permute-done.2.refs_0_ = bf16[2,2,8320]{2,1,0:T(2,128)(2,1)S(1)} collective-permute-done((bf16[2,2,8320]{2,1,0:T(2,128)(2,1)S(1)}, bf16[2,2,8320]{2,1,0:T(2,128)(2,1)S(1)}, u32[]{:S(2)}, u32[]{:S(2)}) %collective-permute-start.2) | collective-permute-done | bytes 66592 | tf_op jit(solution)/shard_map/ppermute | solution.py:337
  18.6 1.6 %scores.3 = (bf16[72,8192]{1,0:T(8,128)(2,1)S(1)}, f32[2,32,72]{2,1,0:T(8,128)S(1)}, f32[2,32,72]{2,1,0:T(8,128)S(1)}, f32[16,1,128]{2,1,0:T(1,128)S(1)}) custom-call(bf16[2,2,8320]{2,1,0:T(2,128)(2,1)S(1)} %collective-permute-done.2.refs_0_, bf16[2,2,8320]{2,1,0:T(2,128)(2,1)S(1)} %collective-permute-done.3.refs_1_, ...), custom_call_target="tpu_custom_call" | custom-call | flops 84934656 | bytes 1179648 | tf_op jit(solution)/shard_map/scores/pallas_call | solution.py:406
  20.1 0.0 collective-permute-start.7
  20.2 0.5 %collective-permute-start.6 = (bf16[72,8192]{1,0:T(8,128)(2,1)S(1)}, bf16[72,8192]{1,0:T(8,128)(2,1)S(1)}, u32[]{:S(2)}, u32[]{:S(2)}) collective-permute-start(bf16[72,8192]{1,0:T(8,128)(2,1)S(1)} %get-tuple-element.36.refs_3_), channel_id=1, source_target_pairs={{0,1},{1,0},{2,3},{3,2},{4,5},{5,4},{6,7},{7,6},{8,9},{9,8},{10,11... | collective-permute-start | bytes 3538952 | tf_op jit(solution)/shard_map/ppermute | solution.py:337
  20.7 0.1 collective-permute-start.5
  20.7 10.6 %all_to_all.5 = f32[16,1,128]{2,1,0:T(1,128)S(1)} all-to-all(f32[16,1,128]{2,1,0:T(1,128)S(1)} %get-tuple-element.33), channel_id=1, replica_groups=mesh['groups'=2,'blk'=16] {'blk'}, dimensions={0} | all-to-all | bytes 16384 | tf_op jit(solution)/shard_map/all_to_all | solution.py:438
  31.3 0.0 collective-permute-done.5.refs_2_
  31.3 0.0 collective-permute-done.7.refs_6_
  31.3 0.0 collective-permute-done.6.refs_5_
  31.3 2.0 %slices.1 = (f32[32,8192]{1,0:T(8,128)}, f32[2]{0:T(128)}, f32[2]{0:T(128)}) custom-call(f32[8,2,1,128]{3,2,1,0:T(1,128)S(1)} %bitcast.6, f32[2,32,72]{2,1,0:T(8,128)S(1)} %get-tuple-element.34.refs_1_, f32[2,32,72]{2,1,0:T(8,128)S(1)} %collective-permute-done.5.refs_2_, bf16[72,8192]{1,0:T(8,128)(2,1)S(1)} %get-tuple-element.36.refs_3_, ...), custom_call_target="tpu_custom_call" | custom-call | tf_op jit(solution)/shard_map/slices/pallas_call | solution.py:441
  (1 shorter events, 0.0 us)
Async XLA Ops:
  0.6 5.5 %collective-permute-start.1 = (bf16[32,8192]{1,0:T(8,128)(2,1)}, bf16[32,8192]{1,0:T(8,128)(2,1)S(1)}, u32[]{:S(2)}, u32[]{:S(2)}) collective-permute-start(bf16[32,8192]{1,0:T(8,128)(2,1)} %bitcast.4), channel_id=1, source_target_pairs={{0,1},{1,0},{2,3},{3,2},{4,5},{5,4},{6,7},{7,6},{8,9},{9,8},{10,11... | collective-permute-start | bytes 1572872 | tf_op jit(solution)/shard_map/ppermute | solution.py:337
  2.7 4.9 %collective-permute-start = (bf16[1,2,8320]{2,1,0:T(2,128)(2,1)}, bf16[1,2,8320]{2,1,0:T(2,128)(2,1)S(1)}, u32[]{:S(2)}, u32[]{:S(2)}) collective-permute-start(bf16[1,2,8320]{2,1,0:T(2,128)(2,1)} %pack.1), channel_id=1, source_target_pairs={{0,2},{1,3},{2,0},{3,1},{4,6},{5,7},{6,4},{7,5},{8,10},{9,11},{10,... | collective-permute-start | bytes 99848 | tf_op jit(solution)/shard_map/ppermute | solution.py:337
  6.1 1.0 %copy-start = (bf16[2,16,8192]{2,1,0:T(8,128)(2,1)S(1)}, bf16[2,16,8192]{2,1,0:T(8,128)(2,1)}, u32[]{:S(2)}) copy-start(bf16[2,16,8192]{2,1,0:T(8,128)(2,1)} %param.7) | copy-start | bytes 1572868
  7.2 5.0 %copy-start.1 = (f32[16,4096]{1,0:T(8,128)S(1)}, f32[16,4096]{1,0:T(8,128)}, u32[]{:S(2)}) copy-start(f32[16,4096]{1,0:T(8,128)} %ctf_ref.1) | copy-start | bytes 786436
  7.2 5.0 %copy-start.2 = (f32[16,4096]{1,0:T(8,128)S(1)}, f32[16,4096]{1,0:T(8,128)}, u32[]{:S(2)}) copy-start(f32[16,4096]{1,0:T(8,128)} %noise_ref.1) | copy-start | bytes 786436
  7.6 4.7 %collective-permute-start.4 = (bf16[2,2,8320]{2,1,0:T(2,128)(2,1)S(1)}, bf16[2,2,8320]{2,1,0:T(2,128)(2,1)S(1)}, u32[]{:S(2)}, u32[]{:S(2)}) collective-permute-start(bf16[2,2,8320]{2,1,0:T(2,128)(2,1)S(1)} %constant_dynamic-update-slice_fusion.refs_0_), channel_id=1, source_target_pairs={{0,4},{1,5},{2,6},{3,7},{4,0},{5,1},{6,2},{7,3},{8,12},{9,13},{10,... | collective-permute-start | bytes 199688 | tf_op jit(solution)/shard_map/ppermute | solution.py:337
  9.5 6.9 %collective-permute-start.3 = (bf16[2,2,8320]{2,1,0:T(2,128)(2,1)S(1)}, bf16[2,2,8320]{2,1,0:T(2,128)(2,1)S(1)}, u32[]{:S(2)}, u32[]{:S(2)}) collective-permute-start(bf16[2,2,8320]{2,1,0:T(2,128)(2,1)S(1)} %constant_dynamic-update-slice_fusion.refs_0_), channel_id=1, source_target_pairs={{0,12},{1,13},{2,14},{3,15},{4,8},{5,9},{6,10},{7,11},{8,4},{9,5},... | collective-permute-start | bytes 199688 | tf_op jit(solution)/shard_map/ppermute | solution.py:337
  12.0 6.5 %collective-permute-start.2 = (bf16[2,2,8320]{2,1,0:T(2,128)(2,1)S(1)}, bf16[2,2,8320]{2,1,0:T(2,128)(2,1)S(1)}, u32[]{:S(2)}, u32[]{:S(2)}) collective-permute-start(bf16[2,2,8320]{2,1,0:T(2,128)(2,1)S(1)} %constant_dynamic-update-slice_fusion.refs_0_), channel_id=1, source_target_pairs={{0,8},{1,9},{2,10},{3,11},{4,12},{5,13},{6,14},{7,15},{8,0},{9,1},... | collective-permute-start | bytes 199688 | tf_op jit(solution)/shard_map/ppermute | solution.py:337
  20.1 11.2 %collective-permute-start.7 = (bf16[72,8192]{1,0:T(8,128)(2,1)S(1)}, bf16[72,8192]{1,0:T(8,128)(2,1)S(1)}, u32[]{:S(2)}, u32[]{:S(2)}) collective-permute-start(bf16[72,8192]{1,0:T(8,128)(2,1)S(1)} %get-tuple-element.37.refs_4_), channel_id=1, source_target_pairs={{0,1},{1,0},{2,3},{3,2},{4,5},{5,4},{6,7},{7,6},{8,9},{9,8},{10,11... | collective-permute-start | bytes 3538952 | tf_op jit(solution)/shard_map/ppermute | solution.py:337
  20.2 11.1 %collective-permute-start.6 = (bf16[72,8192]{1,0:T(8,128)(2,1)S(1)}, bf16[72,8192]{1,0:T(8,128)(2,1)S(1)}, u32[]{:S(2)}, u32[]{:S(2)}) collective-permute-start(bf16[72,8192]{1,0:T(8,128)(2,1)S(1)} %get-tuple-element.36.refs_3_), channel_id=1, source_target_pairs={{0,1},{1,0},{2,3},{3,2},{4,5},{5,4},{6,7},{7,6},{8,9},{9,8},{10,11... | collective-permute-start | bytes 3538952 | tf_op jit(solution)/shard_map/ppermute | solution.py:337
  20.7 10.6 %collective-permute-start.5 = (f32[2,32,72]{2,1,0:T(8,128)S(1)}, f32[2,32,72]{2,1,0:T(8,128)S(1)}, u32[]{:S(2)}, u32[]{:S(2)}) collective-permute-start(f32[2,32,72]{2,1,0:T(8,128)S(1)} %get-tuple-element.35), channel_id=1, source_target_pairs={{0,1},{1,0},{2,3},{3,2},{4,5},{5,4},{6,7},{7,6},{8,9},{9,8},{10,11... | collective-permute-start | bytes 55304 | tf_op jit(solution)/shard_map/ppermute | solution.py:337

commit v6 on v5

--- a/solution.py
+++ b/solution.py
@@ -13,6 +13,7 @@
 LANES = 128
 ROWS = 8
 NEAR = 4
+GROUP = 1024
 LIMIT_AT = 1
 X_AT = 16
 Y_AT = 48
@@ -167,6 +168,7 @@
 
         numbers_int = numbers.astype(jnp.int32)
         step_cos, step_sin = sin_cos(numbers_int * (LANES // KY))
+        phases = []
         for start in range(0, shifts, 2):
             members = range(start, min(start + 2, shifts))
 
@@ -186,24 +188,36 @@
             cosine_before = cosine * turn_cos + sine * turn_sin
             sine_before = sine * turn_cos - cosine * turn_sin
             double = jnp.broadcast_to(2.0 * turn_cos, (height, LANES))
-            out_rows = pl.ds(first + start * ROWS, height)
-            for chunk in range(half // LANES):
-                at = pl.ds(chunk * LANES, LANES)
-                real = jnp.concatenate([real_ref[:, at]] * len(members), axis=0)
-                imag = jnp.concatenate([imag_ref[:, at]] * len(members), axis=0)
-                weighted_ref[out_rows, at] = (real * cosine + imag * sine).astype(jnp.bfloat16)
-                weighted_ref[out_rows, pl.ds(half + chunk * LANES, LANES)] = (
-                    imag * cosine - real * sine
-                ).astype(jnp.bfloat16)
-                cosine, cosine_before = double * cosine - cosine_before, cosine
-                sine, sine_before = double * sine - sine_before, sine
-
-        cross_ref[...] = lax.dot_general(
-            weighted_ref[pl.ds(first, block_rows), :],
-            both_ref[...],
-            NT,
-            preferred_element_type=jnp.float32,
-        )
+            phases.append((cosine, cosine_before, sine, sine_before, double))
+
+        cross = jnp.zeros(cross_ref.shape, jnp.float32)
+        for group in range(0, half, GROUP):
+            for number, phase in enumerate(phases):
+                cosine, cosine_before, sine, sine_before, double = phase
+                height = double.shape[0]
+                out_rows = pl.ds(first + 2 * number * ROWS, height)
+                for start in range(group, group + GROUP, LANES):
+                    at = pl.ds(start, LANES)
+                    real = jnp.concatenate([real_ref[:, at]] * (height // ROWS), axis=0)
+                    imag = jnp.concatenate([imag_ref[:, at]] * (height // ROWS), axis=0)
+                    weighted_ref[out_rows, at] = (real * cosine + imag * sine).astype(
+                        jnp.bfloat16
+                    )
+                    weighted_ref[out_rows, pl.ds(half + start, LANES)] = (
+                        imag * cosine - real * sine
+                    ).astype(jnp.bfloat16)
+                    cosine, cosine_before = double * cosine - cosine_before, cosine
+                    sine, sine_before = double * sine - sine_before, sine
+                phases[number] = (cosine, cosine_before, sine, sine_before, double)
+            for base in (group, half + group):
+                at = pl.ds(base, GROUP)
+                cross = cross + lax.dot_general(
+                    weighted_ref[pl.ds(first, block_rows), at],
+                    both_ref[:, at],
+                    NT,
+                    preferred_element_type=jnp.float32,
+                )
+        cross_ref[...] = cross
         base = norm + quad
         scores = [
             -(base - 2.0 * cross_ref[pl.ds(shift * ROWS, ROWS), :]) * scale
@@ -219,17 +233,15 @@
         exps_other_ref[index + slot] = turned[candidates // 2 : candidates, :block_rows]
         row = lax.broadcasted_iota(jnp.int32, (ROWS, LANES), 0)
         lane = lax.broadcasted_iota(jnp.int32, (ROWS, LANES), 1)
+        half_at = chip // NEAR ^ slot if by_distance else 0
+        here = (lane & (2 * ROWS - 1)) == row + half_at * ROWS
         line = jnp.sum(
-            jnp.where(lane == row, top, jnp.where(lane == row + LANES // 2, total, 0.0)),
+            jnp.where(here, jnp.where(lane < LANES // 2, top, total), 0.0),
             axis=0,
             keepdims=True,
         )
         if has_earlier:
-            first_half = chip // NEAR == 0
-            before = earlier_stats_ref[0]
-            line = jnp.where(first_half, before, line) + pltpu.roll(
-                jnp.where(first_half, line, before), ROWS, 1
-            )
+            line = line + earlier_stats_ref[0]
         for target in range(stats_ref.shape[0]):
             stats_ref[target, pl.ds(index, 1), :] = line
         return carry
@@ -251,30 +263,29 @@
     lane = lax.broadcasted_iota(jnp.int32, (1, LANES), 1)
 
     def combined(core, row):
-        lines = [stats_ref[source, core, pl.ds(row, 1), :] for source in range(chips)]
-        top = functools.reduce(jnp.maximum, lines)
+        at = pl.ds(row, 1)
+        lower = lane < LANES // 2
+        lines = [stats_ref[source, core, at, :] for source in range(chips)]
+        lines.append(stats_ref[chip, core, at, :])
+        turned = [pltpu.roll(line, LANES // 2, 1) for line in lines]
+        tops = [jnp.where(lower, one, two) for one, two in zip(lines, turned)]
+        totals = [jnp.where(lower, two, one) for one, two in zip(lines, turned)]
+        top = functools.reduce(jnp.maximum, tops)
         total = functools.reduce(
-            jnp.add,
-            [pltpu.roll(line, LANES // 2, 1) * jnp.exp(line - top) for line in lines],
+            jnp.add, [part * jnp.exp(high - top) for high, part in zip(tops[:-1], totals)]
         )
-        log_total = top + jnp.log(total)
-        return top, log_total, stats_ref[chip, core, pl.ds(row, 1), :]
-
+        return top, top + jnp.log(total), tops[-1]
+
+    upper = (lane & ROWS) != 0
     for side, exps_ref in enumerate((exps_own_ref, exps_other_ref)):
         core = (index & 1) ^ side
         for block in range(blocks):
             if block == 0 or not by_distance:
                 top, log_total, mine = combined(core, block)
                 line = jnp.exp(mine - log_total)
-            factor = line
-            if by_distance:
-                first_half = chip // NEAR == block
-                factor = jnp.where(first_half, line, pltpu.roll(line, LANES - ROWS, 1))
-            factor = jnp.where(lane < ROWS, factor, 0.0)
-            filled = ROWS
-            while filled < LANES:
-                factor = factor + pltpu.roll(factor, filled, 1)
-                filled *= 2
+                crossed = pltpu.roll(line, ROWS, 1)
+            wanted = (chip // NEAR ^ block) != 0 if by_distance else False
+            factor = jnp.where(upper == wanted, line, crossed)
             posterior_ref[side, block] = (exps_ref[block] * factor[:, :block_rows]).astype(
                 jnp.bfloat16
             )

time: 33.7 us -> 33.4 us (level)
  Pallas kernels: 7.1 us -> 6.75 us
  transfers between devices with their start and end apart: 8 -> 8, of which waited for: 2 -> 2; matrix products, arithmetic and copies ran while one was open for 2% -> 3% of each run, Pallas kernels for 10% -> 10%
where the time goes in v6:
time: 33.4 us; the launch traced here: 33.1 us
  blocking collectives  10.6 us (32%)
  starting transfers between devices  8.33 us (25%)
  Pallas kernels  6.75 us (20%)
  waiting for transfers between devices  4.82 us (14%)
  local copies, waits for them, and re-layouts  1.91 us (6%)
  between operations  0.71 us (2%)
    all_to_all x1, blocking collectives, local(): gathered = lax.all_to_all(stats, 'blk', 0, 0)  10.6 us
    ppermute x8, starting transfers between devices, swap(): return lax.ppermute(value, 'blk', [(i, i ^ mask) for i in range(axis_size)])  8.33 us
    ppermute x8, waiting for transfers between devices, swap(): return lax.ppermute(value, 'blk', [(i, i ^ mask) for i in range(axis_size)])  4.82 us
    pallas_call x2, Pallas kernels, local(): pl.pallas_call(functools.partial(score_kernel, sources, by_distance, shif...  2.98 us
    pallas_call x1, Pallas kernels, local(): pl.pallas_call(functools.partial(slice_kernel, own_rows / per_device, len...  1.8 us
    pallas_call x1, Pallas kernels, local(): pl.pallas_call(pack_kernel, out_shape=jax.ShapeDtypeStruct((1, per_device...  1.51 us
    unnamed x6, local copies, waits for them, and re-layouts  1.04 us
    dynamic_update_slice x1, local copies, waits for them, and re-layouts, local(): pair = lax.dynamic_update_slice(pair, packed, (0, 0, 0))  0.83 us
  transfers between devices with their start and end apart: 8, of which 2 were waited for; matrix products, arithmetic and copies ran while one was open for 3% of the time, Pallas kernels for 10%

profile of v6, /device:TPU:0, one launch (start us, length us, event | category | flops | bytes accessed | tf_op | source)
XLA Modules:
  0.0 33.1 jit_solution(14310356330418632543)
XLA Ops:
  0.6 0.5 %collective-permute-start.1 = (bf16[32,8192]{1,0:T(8,128)(2,1)}, bf16[32,8192]{1,0:T(8,128)(2,1)S(1)}, u32[]{:S(2)}, u32[]{:S(2)}) collective-permute-start(bf16[32,8192]{1,0:T(8,128)(2,1)} %bitcast.4), channel_id=1, source_target_pairs={{0,1},{1,0},{2,3},{3,2},{4,5},{5,4},{6,7},{7,6},{8,9},{9,8},{10,11... | collective-permute-start | bytes 1572872 | tf_op jit(solution)/shard_map/ppermute | solution.py:348
  1.1 1.5 %pack.1 = bf16[1,2,8320]{2,1,0:T(2,128)(2,1)} custom-call(bf16[2,8192]{1,0:T(2,128)(2,1)} %images_hbm.1, s32[2]{0:T(128)} %group_hbm.1, s32[2]{0:T(128)} %limit_hbm.1, s32[2,2,9]{2,1,0:T(2,128)} %bitcast.7), custom_call_target="tpu_custom_call" | custom-call | tf_op jit(solution)/shard_map/pack/pallas_call | solution.py:350
  2.7 2.6 %collective-permute-start = (bf16[1,2,8320]{2,1,0:T(2,128)(2,1)}, bf16[1,2,8320]{2,1,0:T(2,128)(2,1)S(1)}, u32[]{:S(2)}, u32[]{:S(2)}) collective-permute-start(bf16[1,2,8320]{2,1,0:T(2,128)(2,1)} %pack.1), channel_id=1, source_target_pairs={{0,2},{1,3},{2,0},{3,1},{4,6},{5,7},{6,4},{7,5},{8,10},{9,11},{10,... | collective-permute-start | bytes 99848 | tf_op jit(solution)/shard_map/ppermute | solution.py:348
  5.3 0.8 %dynamic_update_slice.6 = bf16[2,2,8320]{2,1,0:T(2,128)(2,1)S(1)} pad(bf16[1,2,8320]{2,1,0:T(2,128)(2,1)} %pack.1, bf16[]{:T(256)} %constant.0.clone.1), padding=0_1x0_0x0_0 | pad | bytes 99842 | tf_op jit(solution)/shard_map/dynamic_update_slice | solution.py:397
  6.1 0.0 collective-permute-done.1.other_ref
  6.1 0.0 copy-start
  6.1 1.0 %copy-done = bf16[2,16,8192]{2,1,0:T(8,128)(2,1)S(1)} copy-done((bf16[2,16,8192]{2,1,0:T(8,128)(2,1)S(1)}, bf16[2,16,8192]{2,1,0:T(8,128)(2,1)}, u32[]{:S(2)}) %copy-start) | copy-done | bytes 524312
  7.2 0.0 copy-start.1
  7.2 0.0 copy-start.2
  7.2 0.3 power.1
  7.5 0.0 collective-permute-done
  7.6 2.0 %collective-permute-start.4 = (bf16[2,2,8320]{2,1,0:T(2,128)(2,1)S(1)}, bf16[2,2,8320]{2,1,0:T(2,128)(2,1)S(1)}, u32[]{:S(2)}, u32[]{:S(2)}) collective-permute-start(bf16[2,2,8320]{2,1,0:T(2,128)(2,1)S(1)} %constant_dynamic-update-slice_fusion.refs_0_), channel_id=1, source_target_pairs={{0,4},{1,5},{2,6},{3,7},{4,0},{5,1},{6,2},{7,3},{8,12},{9,13},{10,... | collective-permute-start | bytes 199688 | tf_op jit(solution)/shard_map/ppermute | solution.py:348
  9.5 2.5 %collective-permute-start.3 = (bf16[2,2,8320]{2,1,0:T(2,128)(2,1)S(1)}, bf16[2,2,8320]{2,1,0:T(2,128)(2,1)S(1)}, u32[]{:S(2)}, u32[]{:S(2)}) collective-permute-start(bf16[2,2,8320]{2,1,0:T(2,128)(2,1)S(1)} %constant_dynamic-update-slice_fusion.refs_0_), channel_id=1, source_target_pairs={{0,12},{1,13},{2,14},{3,15},{4,8},{5,9},{6,10},{7,11},{8,4},{9,5},... | collective-permute-start | bytes 199688 | tf_op jit(solution)/shard_map/ppermute | solution.py:348
  12.0 0.1 collective-permute-start.2
  12.1 0.0 copy-done.1
  12.1 0.0 copy-done.2
  12.1 0.1 tables.1.refs_5_
  12.3 0.0 collective-permute-done.4.refs_1_
  12.3 1.5 %scores.2 = (bf16[72,8192]{1,0:T(8,128)(2,1)S(1)}, f32[1,32,72]{2,1,0:T(8,128)S(1)}, f32[1,32,72]{2,1,0:T(8,128)S(1)}, f32[1,1,128]{2,1,0:T(1,128)S(1)}) custom-call(bf16[2,2,8320]{2,1,0:T(2,128)(2,1)S(1)} %constant_dynamic-update-slice_fusion.refs_0_, bf16[2,2,8320]{2,1,0:T(2,128)(2,1)S(1)} %collective-permute-done.4.refs_1_, ...), custom_call_target="tpu_custom_call" | custom-call | flops 84934656 | bytes 1179648 | tf_op jit(solution)/shard_map/scores/pallas_call | solution.py:417
  13.8 2.6 %collective-permute-done.3.refs_1_ = bf16[2,2,8320]{2,1,0:T(2,128)(2,1)S(1)} collective-permute-done((bf16[2,2,8320]{2,1,0:T(2,128)(2,1)S(1)}, bf16[2,2,8320]{2,1,0:T(2,128)(2,1)S(1)}, u32[]{:S(2)}, u32[]{:S(2)}) %collective-permute-start.3) | collective-permute-done | bytes 66592 | tf_op jit(solution)/shard_map/ppermute | solution.py:348
  16.4 2.1 %collective-permute-done.2.refs_0_ = bf16[2,2,8320]{2,1,0:T(2,128)(2,1)S(1)} collective-permute-done((bf16[2,2,8320]{2,1,0:T(2,128)(2,1)S(1)}, bf16[2,2,8320]{2,1,0:T(2,128)(2,1)S(1)}, u32[]{:S(2)}, u32[]{:S(2)}) %collective-permute-start.2) | collective-permute-done | bytes 66592 | tf_op jit(solution)/shard_map/ppermute | solution.py:348
  18.6 1.5 %scores.3 = (bf16[72,8192]{1,0:T(8,128)(2,1)S(1)}, f32[2,32,72]{2,1,0:T(8,128)S(1)}, f32[2,32,72]{2,1,0:T(8,128)S(1)}, f32[16,1,128]{2,1,0:T(1,128)S(1)}) custom-call(bf16[2,2,8320]{2,1,0:T(2,128)(2,1)S(1)} %collective-permute-done.2.refs_0_, bf16[2,2,8320]{2,1,0:T(2,128)(2,1)S(1)} %collective-permute-done.3.refs_1_, ...), custom_call_target="tpu_custom_call" | custom-call | flops 84934656 | bytes 1179648 | tf_op jit(solution)/shard_map/scores/pallas_call | solution.py:417
  20.1 0.1 collective-permute-start.7
  20.1 0.5 %collective-permute-start.6 = (bf16[72,8192]{1,0:T(8,128)(2,1)S(1)}, bf16[72,8192]{1,0:T(8,128)(2,1)S(1)}, u32[]{:S(2)}, u32[]{:S(2)}) collective-permute-start(bf16[72,8192]{1,0:T(8,128)(2,1)S(1)} %get-tuple-element.36.refs_3_), channel_id=1, source_target_pairs={{0,1},{1,0},{2,3},{3,2},{4,5},{5,4},{6,7},{7,6},{8,9},{9,8},{10,11... | collective-permute-start | bytes 3538952 | tf_op jit(solution)/shard_map/ppermute | solution.py:348
  20.6 0.1 collective-permute-start.5
  20.7 10.6 %all_to_all.5 = f32[16,1,128]{2,1,0:T(1,128)S(1)} all-to-all(f32[16,1,128]{2,1,0:T(1,128)S(1)} %get-tuple-element.33), channel_id=1, replica_groups=mesh['groups'=2,'blk'=16] {'blk'}, dimensions={0} | all-to-all | bytes 16384 | tf_op jit(solution)/shard_map/all_to_all | solution.py:449
  31.3 0.0 collective-permute-done.5.refs_2_
  31.3 0.0 collective-permute-done.7.refs_6_
  31.3 0.0 collective-permute-done.6.refs_5_
  31.3 1.8 %slices.1 = (f32[32,8192]{1,0:T(8,128)}, f32[2]{0:T(128)}, f32[2]{0:T(128)}) custom-call(f32[8,2,1,128]{3,2,1,0:T(1,128)S(1)} %bitcast.6, f32[2,32,72]{2,1,0:T(8,128)S(1)} %get-tuple-element.34.refs_1_, f32[2,32,72]{2,1,0:T(8,128)S(1)} %collective-permute-done.5.refs_2_, bf16[72,8192]{1,0:T(8,128)(2,1)S(1)} %get-tuple-element.36.refs_3_, ...), custom_call_target="tpu_custom_call" | custom-call | tf_op jit(solution)/shard_map/slices/pallas_call | solution.py:452
  (1 shorter events, 0.0 us)
Async XLA Ops:
  0.6 5.5 %collective-permute-start.1 = (bf16[32,8192]{1,0:T(8,128)(2,1)}, bf16[32,8192]{1,0:T(8,128)(2,1)S(1)}, u32[]{:S(2)}, u32[]{:S(2)}) collective-permute-start(bf16[32,8192]{1,0:T(8,128)(2,1)} %bitcast.4), channel_id=1, source_target_pairs={{0,1},{1,0},{2,3},{3,2},{4,5},{5,4},{6,7},{7,6},{8,9},{9,8},{10,11... | collective-permute-start | bytes 1572872 | tf_op jit(solution)/shard_map/ppermute | solution.py:348
  2.7 4.9 %collective-permute-start = (bf16[1,2,8320]{2,1,0:T(2,128)(2,1)}, bf16[1,2,8320]{2,1,0:T(2,128)(2,1)S(1)}, u32[]{:S(2)}, u32[]{:S(2)}) collective-permute-start(bf16[1,2,8320]{2,1,0:T(2,128)(2,1)} %pack.1), channel_id=1, source_target_pairs={{0,2},{1,3},{2,0},{3,1},{4,6},{5,7},{6,4},{7,5},{8,10},{9,11},{10,... | collective-permute-start | bytes 99848 | tf_op jit(solution)/shard_map/ppermute | solution.py:348
  6.1 1.0 %copy-start = (bf16[2,16,8192]{2,1,0:T(8,128)(2,1)S(1)}, bf16[2,16,8192]{2,1,0:T(8,128)(2,1)}, u32[]{:S(2)}) copy-start(bf16[2,16,8192]{2,1,0:T(8,128)(2,1)} %param.7) | copy-start | bytes 1572868
  7.2 5.0 %copy-start.1 = (f32[16,4096]{1,0:T(8,128)S(1)}, f32[16,4096]{1,0:T(8,128)}, u32[]{:S(2)}) copy-start(f32[16,4096]{1,0:T(8,128)} %ctf_ref.1) | copy-start | bytes 786436
  7.2 5.0 %copy-start.2 = (f32[16,4096]{1,0:T(8,128)S(1)}, f32[16,4096]{1,0:T(8,128)}, u32[]{:S(2)}) copy-start(f32[16,4096]{1,0:T(8,128)} %noise_ref.1) | copy-start | bytes 786436
  7.6 4.7 %collective-permute-start.4 = (bf16[2,2,8320]{2,1,0:T(2,128)(2,1)S(1)}, bf16[2,2,8320]{2,1,0:T(2,128)(2,1)S(1)}, u32[]{:S(2)}, u32[]{:S(2)}) collective-permute-start(bf16[2,2,8320]{2,1,0:T(2,128)(2,1)S(1)} %constant_dynamic-update-slice_fusion.refs_0_), channel_id=1, source_target_pairs={{0,4},{1,5},{2,6},{3,7},{4,0},{5,1},{6,2},{7,3},{8,12},{9,13},{10,... | collective-permute-start | bytes 199688 | tf_op jit(solution)/shard_map/ppermute | solution.py:348
  9.5 6.9 %collective-permute-start.3 = (bf16[2,2,8320]{2,1,0:T(2,128)(2,1)S(1)}, bf16[2,2,8320]{2,1,0:T(2,128)(2,1)S(1)}, u32[]{:S(2)}, u32[]{:S(2)}) collective-permute-start(bf16[2,2,8320]{2,1,0:T(2,128)(2,1)S(1)} %constant_dynamic-update-slice_fusion.refs_0_), channel_id=1, source_target_pairs={{0,12},{1,13},{2,14},{3,15},{4,8},{5,9},{6,10},{7,11},{8,4},{9,5},... | collective-permute-start | bytes 199688 | tf_op jit(solution)/shard_map/ppermute | solution.py:348
  12.0 6.5 %collective-permute-start.2 = (bf16[2,2,8320]{2,1,0:T(2,128)(2,1)S(1)}, bf16[2,2,8320]{2,1,0:T(2,128)(2,1)S(1)}, u32[]{:S(2)}, u32[]{:S(2)}) collective-permute-start(bf16[2,2,8320]{2,1,0:T(2,128)(2,1)S(1)} %constant_dynamic-update-slice_fusion.refs_0_), channel_id=1, source_target_pairs={{0,8},{1,9},{2,10},{3,11},{4,12},{5,13},{6,14},{7,15},{8,0},{9,1},... | collective-permute-start | bytes 199688 | tf_op jit(solution)/shard_map/ppermute | solution.py:348
  20.1 11.2 %collective-permute-start.7 = (bf16[72,8192]{1,0:T(8,128)(2,1)S(1)}, bf16[72,8192]{1,0:T(8,128)(2,1)S(1)}, u32[]{:S(2)}, u32[]{:S(2)}) collective-permute-start(bf16[72,8192]{1,0:T(8,128)(2,1)S(1)} %get-tuple-element.37.refs_4_), channel_id=1, source_target_pairs={{0,1},{1,0},{2,3},{3,2},{4,5},{5,4},{6,7},{7,6},{8,9},{9,8},{10,11... | collective-permute-start | bytes 3538952 | tf_op jit(solution)/shard_map/ppermute | solution.py:348
  20.1 11.1 %collective-permute-start.6 = (bf16[72,8192]{1,0:T(8,128)(2,1)S(1)}, bf16[72,8192]{1,0:T(8,128)(2,1)S(1)}, u32[]{:S(2)}, u32[]{:S(2)}) collective-permute-start(bf16[72,8192]{1,0:T(8,128)(2,1)S(1)} %get-tuple-element.36.refs_3_), channel_id=1, source_target_pairs={{0,1},{1,0},{2,3},{3,2},{4,5},{5,4},{6,7},{7,6},{8,9},{9,8},{10,11... | collective-permute-start | bytes 3538952 | tf_op jit(solution)/shard_map/ppermute | solution.py:348
  20.6 10.6 %collective-permute-start.5 = (f32[2,32,72]{2,1,0:T(8,128)S(1)}, f32[2,32,72]{2,1,0:T(8,128)S(1)}, u32[]{:S(2)}, u32[]{:S(2)}) collective-permute-start(f32[2,32,72]{2,1,0:T(8,128)S(1)} %get-tuple-element.35), channel_id=1, source_target_pairs={{0,1},{1,0},{2,3},{3,2},{4,5},{5,4},{6,7},{7,6},{8,9},{9,8},{10,11... | collective-permute-start | bytes 55304 | tf_op jit(solution)/shard_map/ppermute | solution.py:348

commit v7 on v6

--- a/solution.py
+++ b/solution.py
@@ -52,18 +52,16 @@
     return high, (value - high.astype(jnp.float32)).astype(jnp.bfloat16)
 
 
-def pack_kernel(images_hbm, group_hbm, limit_hbm, offsets_hbm, packed_ref, group, limit, offsets, sems):
-    per_device, full = images_hbm.shape
-    shifts = offsets_hbm.shape[2]
+def pack_kernel(group_hbm, limit_hbm, offsets_hbm, packed_ref, group, limit, offsets, sems):
+    per_device, _, shifts = offsets_hbm.shape
     copies = [
-        pltpu.make_async_copy(images_hbm, packed_ref.at[0, :, pl.ds(0, full)], sems.at[0]),
-        pltpu.make_async_copy(group_hbm, group, sems.at[1]),
-        pltpu.make_async_copy(limit_hbm, limit, sems.at[2]),
-        pltpu.make_async_copy(offsets_hbm, offsets, sems.at[3]),
+        pltpu.make_async_copy(group_hbm, group, sems.at[0]),
+        pltpu.make_async_copy(limit_hbm, limit, sems.at[1]),
+        pltpu.make_async_copy(offsets_hbm, offsets, sems.at[2]),
     ]
     for copy in copies:
         copy.start()
-    for copy in copies[1:]:
+    for copy in copies:
         copy.wait()
     row = lax.broadcasted_iota(jnp.int32, (per_device, LANES), 0)
     lane = lax.broadcasted_iota(jnp.int32, (per_device, LANES), 1)
@@ -76,8 +74,7 @@
             line = jnp.where(lane == X_AT + shift, offsets[particle, 0, shift], line)
             line = jnp.where(lane == Y_AT + shift, offsets[particle, 1, shift], line)
         numbers = jnp.where(row == particle, line, numbers)
-    packed_ref[0, :, pl.ds(full, LANES)] = numbers.astype(jnp.float32).astype(jnp.bfloat16)
-    copies[0].wait()
+    packed_ref[0] = numbers.astype(jnp.float32).astype(jnp.bfloat16)
 
 
 def split_thirds(value):
@@ -347,24 +344,30 @@
     def swap(value, mask):
         return lax.ppermute(value, "blk", [(i, i ^ mask) for i in range(axis_size)])
 
-    packed = pl.pallas_call(
+    numbers = pl.pallas_call(
         pack_kernel,
-        out_shape=jax.ShapeDtypeStruct((1, per_device, full + LANES), jnp.bfloat16),
-        in_specs=[HBM] * 4,
+        out_shape=jax.ShapeDtypeStruct((1, per_device, LANES), jnp.bfloat16),
+        in_specs=[HBM] * 3,
         out_specs=VMEM,
         scratch_shapes=[
             pltpu.SMEM((per_device,), jnp.int32),
             pltpu.SMEM((per_device,), jnp.int32),
             pltpu.SMEM((per_device, 2, shifts), jnp.int32),
-            pltpu.SemaphoreType.DMA((4,)),
+            pltpu.SemaphoreType.DMA((3,)),
         ],
         compiler_params=pltpu.CompilerParams(vmem_limit_bytes=60 * 2**20),
         name="pack",
-    )(images, ctf_group, shell_limit, shift_offsets.transpose(0, 2, 1))
+    )(ctf_group, shell_limit, shift_offsets.transpose(0, 2, 1))
     by_distance = chips == 2 * NEAR and per_device * NEAR == ROWS
-    received = swap(packed, 2) if by_distance else packed
+    rows = images[None]
+    if by_distance:
+        received = swap(rows, 2)
+
     flat = projections.reshape(own_rows, full)
     other = swap(flat, 1)
+    if by_distance:
+        rows, numbers, other = lax.optimization_barrier((rows, numbers, other))
+        received_numbers = swap(numbers, 2)
     groups = ctf_table.shape[0]
     both, high, low = pl.pallas_call(
         power_kernel,
@@ -393,18 +396,20 @@
         name="tables",
     )(ctf_table, noise_weight)
     if by_distance:
-        pair = jnp.zeros((2,) + packed.shape[1:], packed.dtype)
-        pair = lax.dynamic_update_slice(pair, packed, (0, 0, 0))
-        pair, received, both, high, low = lax.optimization_barrier(
-            (pair, received, both, high, low)
+        pair = jnp.zeros((2, per_device, full + LANES), images.dtype)
+        pair = lax.dynamic_update_slice(pair, rows, (0, 0, 0))
+        pair = lax.dynamic_update_slice(pair, numbers, (0, 0, full))
+        pair, received, received_numbers, both, high, low = lax.optimization_barrier(
+            (pair, received, received_numbers, both, high, low)
         )
         pair = lax.dynamic_update_slice(pair, received, (1, 0, 0))
+        pair = lax.dynamic_update_slice(pair, received_numbers, (1, 0, full))
         pieces = [pair] + [swap(pair, mask) for mask in range(4, axis_size, 4)]
         parts = [(pieces[:2], ((0, 1), (2, 3))), (pieces[2:], ((4, 5), (6, 7)))]
     else:
         same_core = [[2 * c + core for c in range(chips)] for core in range(2)]
         gathered = lax.all_gather(
-            packed, "blk", axis=0, tiled=True, axis_index_groups=same_core
+            jnp.concatenate([rows, numbers], axis=2), "blk", axis=0, tiled=True, axis_index_groups=same_core
         )
         parts = [([gathered], (tuple(range(chips)),))]
 

time: 33.4 us -> 34.5 us (1.033)
  local copies, waits for them, and re-layouts: 1.91 us -> 2.55 us
  starting transfers between devices: 8.33 us -> 8.75 us
    dynamic_update_slice x1 -> x3, local copies, waits for them, and re-layouts: 0.83 us -> 1.47 us  [the longest x1 0.8 us: local(): pair = lax.dynamic_update_slice(pair, rows, (0, 0, 0))]
    ppermute x8 -> x9, starting transfers between devices: 8.33 us -> 8.75 us  [swap(): return lax.ppermute(value, 'blk', [(i, i ^ mask) for i in range(axis_size)])]
    ppermute x8 -> x9, waiting for transfers between devices: 4.82 us -> 4.74 us  [swap(): return lax.ppermute(value, 'blk', [(i, i ^ mask) for i in range(axis_size)])]
  transfers between devices with their start and end apart: 8 -> 9, of which waited for: 2 -> 3; matrix products, arithmetic and copies ran while one was open for 3% -> 4% of each run, Pallas kernels for 10% -> 10%
where the time goes in v7:
time: 34.5 us; the launch traced here: 34.2 us
  blocking collectives  10.8 us (31%)
  starting transfers between devices  8.75 us (25%)
  Pallas kernels  6.62 us (19%)
  waiting for transfers between devices  4.74 us (14%)
  local copies, waits for them, and re-layouts  2.55 us (7%)
  between operations  0.71 us (2%)
    all_to_all x1, blocking collectives, local(): gathered = lax.all_to_all(stats, 'blk', 0, 0)  10.8 us
    ppermute x9, starting transfers between devices, swap(): return lax.ppermute(value, 'blk', [(i, i ^ mask) for i in range(axis_size)])  8.75 us
    ppermute x9, waiting for transfers between devices, swap(): return lax.ppermute(value, 'blk', [(i, i ^ mask) for i in range(axis_size)])  4.74 us
    pallas_call x2, Pallas kernels, local(): pl.pallas_call(functools.partial(score_kernel, sources, by_distance, shif...  3.1 us
    pallas_call x1, Pallas kernels, local(): pl.pallas_call(functools.partial(slice_kernel, own_rows / per_device, len...  1.8 us
    pallas_call x1, Pallas kernels, local(): pl.pallas_call(pack_kernel, out_shape=jax.ShapeDtypeStruct((1, per_device...  1.26 us
    unnamed x6, local copies, waits for them, and re-layouts  1.05 us
    dynamic_update_slice x1, local copies, waits for them, and re-layouts, local(): pair = lax.dynamic_update_slice(pair, rows, (0, 0, 0))  0.8 us
  transfers between devices with their start and end apart: 9, of which 3 were waited for; matrix products, arithmetic and copies ran while one was open for 4% of the time, Pallas kernels for 10%

profile of v7, /device:TPU:0, one launch (start us, length us, event | category | flops | bytes accessed | tf_op | source)
XLA Modules:
  0.0 34.2 jit_solution(1006701789651565420)
XLA Ops:
  0.6 0.5 %collective-permute-start = (bf16[32,8192]{1,0:T(8,128)(2,1)}, bf16[32,8192]{1,0:T(8,128)(2,1)S(1)}, u32[]{:S(2)}, u32[]{:S(2)}) collective-permute-start(bf16[32,8192]{1,0:T(8,128)(2,1)} %bitcast.5), channel_id=1, source_target_pairs={{0,1},{1,0},{2,3},{3,2},{4,5},{5,4},{6,7},{7,6},{8,9},{9,8},{10,11... | collective-permute-start | bytes 1572872 | tf_op jit(solution)/shard_map/ppermute | solution.py:345
  1.1 2.6 %collective-permute-start.1 = (bf16[1,2,8192]{2,1,0:T(2,128)(2,1)}, bf16[1,2,8192]{2,1,0:T(2,128)(2,1)S(1)}, u32[]{:S(2)}, u32[]{:S(2)}) collective-permute-start(bf16[1,2,8192]{2,1,0:T(2,128)(2,1)} %bitcast.8), channel_id=1, source_target_pairs={{0,2},{1,3},{2,0},{3,1},{4,6},{5,7},{6,4},{7,5},{8,10},{9,11},{10,... | collective-permute-start | bytes 98312 | tf_op jit(solution)/shard_map/ppermute | solution.py:345
  3.7 1.3 %pack.1 = bf16[1,2,128]{2,1,0:T(2,128)(2,1)} custom-call(s32[2]{0:T(128)} %group_hbm.1, s32[2]{0:T(128)} %limit_hbm.1, s32[2,2,9]{2,1,0:T(2,128)} %bitcast.10), custom_call_target="tpu_custom_call" | custom-call | tf_op jit(solution)/shard_map/pack/pallas_call | solution.py:347
  5.0 0.0 collective-permute-done.other_ref
  5.0 0.8 %collective-permute-start.2 = (bf16[1,2,128]{2,1,0:T(2,128)(2,1)}, bf16[1,2,128]{2,1,0:T(2,128)(2,1)S(1)}, u32[]{:S(2)}, u32[]{:S(2)}) collective-permute-start(bf16[1,2,128]{2,1,0:T(2,128)(2,1)} %pack.1), channel_id=1, source_target_pairs={{0,2},{1,3},{2,0},{3,1},{4,6},{5,7},{6,4},{7,5},{8,10},{9,11},{10,... | collective-permute-start | bytes 1544 | tf_op jit(solution)/shard_map/ppermute | solution.py:345
  5.8 0.8 %dynamic_update_slice.12 = bf16[2,2,8320]{2,1,0:T(2,128)(2,1)S(1)} pad(bf16[1,2,8192]{2,1,0:T(2,128)(2,1)} %bitcast.9, bf16[]{:T(256)} %constant.0.clone.1), padding=0_1x0_0x0_128 | pad | bytes 99330 | tf_op jit(solution)/shard_map/dynamic_update_slice | solution.py:400
  6.6 0.7 %constant_dynamic-update-slice_fusion.2 = bf16[2,2,8320]{2,1,0:T(2,128)(2,1)S(1)} fusion(bf16[2,2,8320]{2,1,0:T(2,128)(2,1)S(1)} %dynamic_update_slice.12, bf16[1,2,128]{2,1,0:T(2,128)(2,1)} %pack.1), kind=kLoop, calls=%fused_computation.2 | loop fusion | bytes 1024 | tf_op jit(solution)/shard_map/dynamic_update_slice | solution.py:401
  7.2 0.0 copy-start
  7.3 1.0 %copy-done = bf16[2,16,8192]{2,1,0:T(8,128)(2,1)S(1)} copy-done((bf16[2,16,8192]{2,1,0:T(8,128)(2,1)S(1)}, bf16[2,16,8192]{2,1,0:T(8,128)(2,1)}, u32[]{:S(2)}) %copy-start) | copy-done | bytes 524312
  8.3 0.0 copy-start.1
  8.3 0.0 copy-start.2
  8.3 0.3 power.1
  8.6 0.0 collective-permute-done.1
  8.6 0.1 collective-permute-done.2
  8.8 1.6 %collective-permute-start.5 = (bf16[2,2,8320]{2,1,0:T(2,128)(2,1)S(1)}, bf16[2,2,8320]{2,1,0:T(2,128)(2,1)S(1)}, u32[]{:S(2)}, u32[]{:S(2)}) collective-permute-start(bf16[2,2,8320]{2,1,0:T(2,128)(2,1)S(1)} %constant_dynamic-update-slice_fusion.refs_0_), channel_id=1, source_target_pairs={{0,4},{1,5},{2,6},{3,7},{4,0},{5,1},{6,2},{7,3},{8,12},{9,13},{10,... | collective-permute-start | bytes 199688 | tf_op jit(solution)/shard_map/ppermute | solution.py:345
  10.5 2.5 %collective-permute-start.4 = (bf16[2,2,8320]{2,1,0:T(2,128)(2,1)S(1)}, bf16[2,2,8320]{2,1,0:T(2,128)(2,1)S(1)}, u32[]{:S(2)}, u32[]{:S(2)}) collective-permute-start(bf16[2,2,8320]{2,1,0:T(2,128)(2,1)S(1)} %constant_dynamic-update-slice_fusion.refs_0_), channel_id=1, source_target_pairs={{0,12},{1,13},{2,14},{3,15},{4,8},{5,9},{6,10},{7,11},{8,4},{9,5},... | collective-permute-start | bytes 199688 | tf_op jit(solution)/shard_map/ppermute | solution.py:345
  12.9 0.1 collective-permute-start.3
  13.0 0.0 copy-done.1
  13.0 0.0 copy-done.2
  13.1 0.1 tables.1.refs_5_
  13.2 0.0 collective-permute-done.5.refs_1_
  13.2 1.5 %scores.2 = (bf16[72,8192]{1,0:T(8,128)(2,1)S(1)}, f32[1,32,72]{2,1,0:T(8,128)S(1)}, f32[1,32,72]{2,1,0:T(8,128)S(1)}, f32[1,1,128]{2,1,0:T(1,128)S(1)}) custom-call(bf16[2,2,8320]{2,1,0:T(2,128)(2,1)S(1)} %constant_dynamic-update-slice_fusion.refs_0_, bf16[2,2,8320]{2,1,0:T(2,128)(2,1)S(1)} %collective-permute-done.5.refs_1_, ...), custom_call_target="tpu_custom_call" | custom-call | flops 84934656 | bytes 1179648 | tf_op jit(solution)/shard_map/scores/pallas_call | solution.py:422
  14.8 2.5 %collective-permute-done.4.refs_1_ = bf16[2,2,8320]{2,1,0:T(2,128)(2,1)S(1)} collective-permute-done((bf16[2,2,8320]{2,1,0:T(2,128)(2,1)S(1)}, bf16[2,2,8320]{2,1,0:T(2,128)(2,1)S(1)}, u32[]{:S(2)}, u32[]{:S(2)}) %collective-permute-start.4) | collective-permute-done | bytes 66592 | tf_op jit(solution)/shard_map/ppermute | solution.py:345
  17.3 2.1 %collective-permute-done.3.refs_0_ = bf16[2,2,8320]{2,1,0:T(2,128)(2,1)S(1)} collective-permute-done((bf16[2,2,8320]{2,1,0:T(2,128)(2,1)S(1)}, bf16[2,2,8320]{2,1,0:T(2,128)(2,1)S(1)}, u32[]{:S(2)}, u32[]{:S(2)}) %collective-permute-start.3) | collective-permute-done | bytes 66592 | tf_op jit(solution)/shard_map/ppermute | solution.py:345
  19.4 1.5 %scores.3 = (bf16[72,8192]{1,0:T(8,128)(2,1)S(1)}, f32[2,32,72]{2,1,0:T(8,128)S(1)}, f32[2,32,72]{2,1,0:T(8,128)S(1)}, f32[16,1,128]{2,1,0:T(1,128)S(1)}) custom-call(bf16[2,2,8320]{2,1,0:T(2,128)(2,1)S(1)} %collective-permute-done.3.refs_0_, bf16[2,2,8320]{2,1,0:T(2,128)(2,1)S(1)} %collective-permute-done.4.refs_1_, ...), custom_call_target="tpu_custom_call" | custom-call | flops 84934656 | bytes 1179648 | tf_op jit(solution)/shard_map/scores/pallas_call | solution.py:422
  20.9 0.1 collective-permute-start.8
  21.0 0.5 %collective-permute-start.7 = (bf16[72,8192]{1,0:T(8,128)(2,1)S(1)}, bf16[72,8192]{1,0:T(8,128)(2,1)S(1)}, u32[]{:S(2)}, u32[]{:S(2)}) collective-permute-start(bf16[72,8192]{1,0:T(8,128)(2,1)S(1)} %get-tuple-element.44.refs_3_), channel_id=1, source_target_pairs={{0,1},{1,0},{2,3},{3,2},{4,5},{5,4},{6,7},{7,6},{8,9},{9,8},{10,11... | collective-permute-start | bytes 3538952 | tf_op jit(solution)/shard_map/ppermute | solution.py:345
  21.5 0.1 collective-permute-start.6
  21.6 10.8 %all_to_all.5 = f32[16,1,128]{2,1,0:T(1,128)S(1)} all-to-all(f32[16,1,128]{2,1,0:T(1,128)S(1)} %get-tuple-element.41), channel_id=1, replica_groups=mesh['groups'=2,'blk'=16] {'blk'}, dimensions={0} | all-to-all | bytes 16384 | tf_op jit(solution)/shard_map/all_to_all | solution.py:454
  32.4 0.0 collective-permute-done.6.refs_2_
  32.4 0.0 collective-permute-done.8.refs_6_
  32.4 0.0 collective-permute-done.7.refs_5_
  32.4 1.8 %slices.1 = (f32[32,8192]{1,0:T(8,128)}, f32[2]{0:T(128)}, f32[2]{0:T(128)}) custom-call(f32[8,2,1,128]{3,2,1,0:T(1,128)S(1)} %bitcast.7, f32[2,32,72]{2,1,0:T(8,128)S(1)} %get-tuple-element.42.refs_1_, f32[2,32,72]{2,1,0:T(8,128)S(1)} %collective-permute-done.6.refs_2_, bf16[72,8192]{1,0:T(8,128)(2,1)S(1)} %get-tuple-element.44.refs_3_, ...), custom_call_target="tpu_custom_call" | custom-call | tf_op jit(solution)/shard_map/slices/pallas_call | solution.py:457
  (2 shorter events, 0.0 us)
Async XLA Ops:
  0.6 4.4 %collective-permute-start = (bf16[32,8192]{1,0:T(8,128)(2,1)}, bf16[32,8192]{1,0:T(8,128)(2,1)S(1)}, u32[]{:S(2)}, u32[]{:S(2)}) collective-permute-start(bf16[32,8192]{1,0:T(8,128)(2,1)} %bitcast.5), channel_id=1, source_target_pairs={{0,1},{1,0},{2,3},{3,2},{4,5},{5,4},{6,7},{7,6},{8,9},{9,8},{10,11... | collective-permute-start | bytes 1572872 | tf_op jit(solution)/shard_map/ppermute | solution.py:345
  1.1 7.5 %collective-permute-start.1 = (bf16[1,2,8192]{2,1,0:T(2,128)(2,1)}, bf16[1,2,8192]{2,1,0:T(2,128)(2,1)S(1)}, u32[]{:S(2)}, u32[]{:S(2)}) collective-permute-start(bf16[1,2,8192]{2,1,0:T(2,128)(2,1)} %bitcast.8), channel_id=1, source_target_pairs={{0,2},{1,3},{2,0},{3,1},{4,6},{5,7},{6,4},{7,5},{8,10},{9,11},{10,... | collective-permute-start | bytes 98312 | tf_op jit(solution)/shard_map/ppermute | solution.py:345
  5.0 3.7 %collective-permute-start.2 = (bf16[1,2,128]{2,1,0:T(2,128)(2,1)}, bf16[1,2,128]{2,1,0:T(2,128)(2,1)S(1)}, u32[]{:S(2)}, u32[]{:S(2)}) collective-permute-start(bf16[1,2,128]{2,1,0:T(2,128)(2,1)} %pack.1), channel_id=1, source_target_pairs={{0,2},{1,3},{2,0},{3,1},{4,6},{5,7},{6,4},{7,5},{8,10},{9,11},{10,... | collective-permute-start | bytes 1544 | tf_op jit(solution)/shard_map/ppermute | solution.py:345
  7.2 1.0 %copy-start = (bf16[2,16,8192]{2,1,0:T(8,128)(2,1)S(1)}, bf16[2,16,8192]{2,1,0:T(8,128)(2,1)}, u32[]{:S(2)}) copy-start(bf16[2,16,8192]{2,1,0:T(8,128)(2,1)} %param.7) | copy-start | bytes 1572868
  8.3 4.8 %copy-start.1 = (f32[16,4096]{1,0:T(8,128)S(1)}, f32[16,4096]{1,0:T(8,128)}, u32[]{:S(2)}) copy-start(f32[16,4096]{1,0:T(8,128)} %ctf_ref.1) | copy-start | bytes 786436
  8.3 4.8 %copy-start.2 = (f32[16,4096]{1,0:T(8,128)S(1)}, f32[16,4096]{1,0:T(8,128)}, u32[]{:S(2)}) copy-start(f32[16,4096]{1,0:T(8,128)} %noise_ref.1) | copy-start | bytes 786436
  8.8 4.4 %collective-permute-start.5 = (bf16[2,2,8320]{2,1,0:T(2,128)(2,1)S(1)}, bf16[2,2,8320]{2,1,0:T(2,128)(2,1)S(1)}, u32[]{:S(2)}, u32[]{:S(2)}) collective-permute-start(bf16[2,2,8320]{2,1,0:T(2,128)(2,1)S(1)} %constant_dynamic-update-slice_fusion.refs_0_), channel_id=1, source_target_pairs={{0,4},{1,5},{2,6},{3,7},{4,0},{5,1},{6,2},{7,3},{8,12},{9,13},{10,... | collective-permute-start | bytes 199688 | tf_op jit(solution)/shard_map/ppermute | solution.py:345
  10.5 6.8 %collective-permute-start.4 = (bf16[2,2,8320]{2,1,0:T(2,128)(2,1)S(1)}, bf16[2,2,8320]{2,1,0:T(2,128)(2,1)S(1)}, u32[]{:S(2)}, u32[]{:S(2)}) collective-permute-start(bf16[2,2,8320]{2,1,0:T(2,128)(2,1)S(1)} %constant_dynamic-update-slice_fusion.refs_0_), channel_id=1, source_target_pairs={{0,12},{1,13},{2,14},{3,15},{4,8},{5,9},{6,10},{7,11},{8,4},{9,5},... | collective-permute-start | bytes 199688 | tf_op jit(solution)/shard_map/ppermute | solution.py:345
  12.9 6.4 %collective-permute-start.3 = (bf16[2,2,8320]{2,1,0:T(2,128)(2,1)S(1)}, bf16[2,2,8320]{2,1,0:T(2,128)(2,1)S(1)}, u32[]{:S(2)}, u32[]{:S(2)}) collective-permute-start(bf16[2,2,8320]{2,1,0:T(2,128)(2,1)S(1)} %constant_dynamic-update-slice_fusion.refs_0_), channel_id=1, source_target_pairs={{0,8},{1,9},{2,10},{3,11},{4,12},{5,13},{6,14},{7,15},{8,0},{9,1},... | collective-permute-start | bytes 199688 | tf_op jit(solution)/shard_map/ppermute | solution.py:345
  20.9 11.5 %collective-permute-start.8 = (bf16[72,8192]{1,0:T(8,128)(2,1)S(1)}, bf16[72,8192]{1,0:T(8,128)(2,1)S(1)}, u32[]{:S(2)}, u32[]{:S(2)}) collective-permute-start(bf16[72,8192]{1,0:T(8,128)(2,1)S(1)} %get-tuple-element.45.refs_4_), channel_id=1, source_target_pairs={{0,1},{1,0},{2,3},{3,2},{4,5},{5,4},{6,7},{7,6},{8,9},{9,8},{10,11... | collective-permute-start | bytes 3538952 | tf_op jit(solution)/shard_map/ppermute | solution.py:345
  21.0 11.4 %collective-permute-start.7 = (bf16[72,8192]{1,0:T(8,128)(2,1)S(1)}, bf16[72,8192]{1,0:T(8,128)(2,1)S(1)}, u32[]{:S(2)}, u32[]{:S(2)}) collective-permute-start(bf16[72,8192]{1,0:T(8,128)(2,1)S(1)} %get-tuple-element.44.refs_3_), channel_id=1, source_target_pairs={{0,1},{1,0},{2,3},{3,2},{4,5},{5,4},{6,7},{7,6},{8,9},{9,8},{10,11... | collective-permute-start | bytes 3538952 | tf_op jit(solution)/shard_map/ppermute | solution.py:345
  21.5 10.9 %collective-permute-start.6 = (f32[2,32,72]{2,1,0:T(8,128)S(1)}, f32[2,32,72]{2,1,0:T(8,128)S(1)}, u32[]{:S(2)}, u32[]{:S(2)}) collective-permute-start(f32[2,32,72]{2,1,0:T(8,128)S(1)} %get-tuple-element.43), channel_id=1, source_target_pairs={{0,1},{1,0},{2,3},{3,2},{4,5},{5,4},{6,7},{7,6},{8,9},{9,8},{10,11... | collective-permute-start | bytes 55304 | tf_op jit(solution)/shard_map/ppermute | solution.py:345

commit v8 on v7

--- a/solution.py
+++ b/solution.py
@@ -399,9 +399,6 @@
         pair = jnp.zeros((2, per_device, full + LANES), images.dtype)
         pair = lax.dynamic_update_slice(pair, rows, (0, 0, 0))
         pair = lax.dynamic_update_slice(pair, numbers, (0, 0, full))
-        pair, received, received_numbers, both, high, low = lax.optimization_barrier(
-            (pair, received, received_numbers, both, high, low)
-        )
         pair = lax.dynamic_update_slice(pair, received, (1, 0, 0))
         pair = lax.dynamic_update_slice(pair, received_numbers, (1, 0, full))
         pieces = [pair] + [swap(pair, mask) for mask in range(4, axis_size, 4)]

time: 34.5 us -> 33.2 us (0.962)
  waiting for transfers between devices: 4.74 us -> 3.35 us
  local copies, waits for them, and re-layouts: 2.55 us -> 3.41 us
  blocking collectives: 10.8 us -> 10.1 us
    ppermute x9, waiting for transfers between devices: 4.74 us -> 3.35 us  [swap(): return lax.ppermute(value, 'blk', [(i, i ^ mask) for i in range(axis_size)])]
    unnamed x6, local copies, waits for them, and re-layouts: 1.05 us -> 1.9 us
    all_to_all x1, blocking collectives: 10.8 us -> 10.1 us  [local(): gathered = lax.all_to_all(stats, 'blk', 0, 0)]
  transfers between devices with their start and end apart: 9 -> 9, of which waited for: 3 -> 2; matrix products, arithmetic and copies ran while one was open for 4% -> 5% of each run, Pallas kernels for 10% -> 10%
where the time goes in v8:
time: 33.2 us; the launch traced here: 32.9 us
  blocking collectives  10.1 us (30%)
  starting transfers between devices  8.69 us (26%)
  Pallas kernels  6.62 us (20%)
  local copies, waits for them, and re-layouts  3.41 us (10%)
  waiting for transfers between devices  3.35 us (10%)
  between operations  0.72 us (2%)
    all_to_all x1, blocking collectives, local(): gathered = lax.all_to_all(stats, 'blk', 0, 0)  10.1 us
    ppermute x9, starting transfers between devices, swap(): return lax.ppermute(value, 'blk', [(i, i ^ mask) for i in range(axis_size)])  8.69 us
    ppermute x9, waiting for transfers between devices, swap(): return lax.ppermute(value, 'blk', [(i, i ^ mask) for i in range(axis_size)])  3.35 us
    pallas_call x2, Pallas kernels, local(): pl.pallas_call(functools.partial(score_kernel, sources, by_distance, shif...  3.1 us
    unnamed x6, local copies, waits for them, and re-layouts  1.9 us
    pallas_call x1, Pallas kernels, local(): pl.pallas_call(functools.partial(slice_kernel, own_rows / per_device, len...  1.8 us
    pallas_call x1, Pallas kernels, local(): pl.pallas_call(pack_kernel, out_shape=jax.ShapeDtypeStruct((1, per_device...  1.26 us
    dynamic_update_slice x1, local copies, waits for them, and re-layouts, local(): pair = lax.dynamic_update_slice(pair, rows, (0, 0, 0))  0.8 us
  transfers between devices with their start and end apart: 9, of which 2 were waited for; matrix products, arithmetic and copies ran while one was open for 5% of the time, Pallas kernels for 10%

profile of v8, /device:TPU:0, one launch (start us, length us, event | category | flops | bytes accessed | tf_op | source)
XLA Modules:
  0.0 32.9 jit_solution(5878105413194316758)
XLA Ops:
  0.6 0.0 copy-start
  0.6 0.5 %collective-permute-start = (bf16[32,8192]{1,0:T(8,128)(2,1)}, bf16[32,8192]{1,0:T(8,128)(2,1)S(1)}, u32[]{:S(2)}, u32[]{:S(2)}) collective-permute-start(bf16[32,8192]{1,0:T(8,128)(2,1)} %bitcast.5), channel_id=1, source_target_pairs={{0,1},{1,0},{2,3},{3,2},{4,5},{5,4},{6,7},{7,6},{8,9},{9,8},{10,11... | collective-permute-start | bytes 1572872 | tf_op jit(solution)/shard_map/ppermute | solution.py:345
  1.2 2.6 %collective-permute-start.1 = (bf16[1,2,8192]{2,1,0:T(2,128)(2,1)}, bf16[1,2,8192]{2,1,0:T(2,128)(2,1)S(1)}, u32[]{:S(2)}, u32[]{:S(2)}) collective-permute-start(bf16[1,2,8192]{2,1,0:T(2,128)(2,1)} %bitcast.8), channel_id=1, source_target_pairs={{0,2},{1,3},{2,0},{3,1},{4,6},{5,7},{6,4},{7,5},{8,10},{9,11},{10,... | collective-permute-start | bytes 98312 | tf_op jit(solution)/shard_map/ppermute | solution.py:345
  3.8 1.3 %pack.1 = bf16[1,2,128]{2,1,0:T(2,128)(2,1)} custom-call(s32[2]{0:T(128)} %group_hbm.1, s32[2]{0:T(128)} %limit_hbm.1, s32[2,2,9]{2,1,0:T(2,128)} %bitcast.10), custom_call_target="tpu_custom_call" | custom-call | tf_op jit(solution)/shard_map/pack/pallas_call | solution.py:347
  5.0 0.0 collective-permute-done.other_ref
  5.0 0.8 %collective-permute-start.2 = (bf16[1,2,128]{2,1,0:T(2,128)(2,1)}, bf16[1,2,128]{2,1,0:T(2,128)(2,1)S(1)}, u32[]{:S(2)}, u32[]{:S(2)}) collective-permute-start(bf16[1,2,128]{2,1,0:T(2,128)(2,1)} %pack.1), channel_id=1, source_target_pairs={{0,2},{1,3},{2,0},{3,1},{4,6},{5,7},{6,4},{7,5},{8,10},{9,11},{10,... | collective-permute-start | bytes 1544 | tf_op jit(solution)/shard_map/ppermute | solution.py:345
  5.8 0.8 %dynamic_update_slice.12 = bf16[2,2,8320]{2,1,0:T(2,128)(2,1)S(1)} pad(bf16[1,2,8192]{2,1,0:T(2,128)(2,1)} %bitcast.9, bf16[]{:T(256)} %constant.0.clone.1), padding=0_1x0_0x0_128 | pad | bytes 99330 | tf_op jit(solution)/shard_map/dynamic_update_slice | solution.py:400
  6.6 0.7 %constant_dynamic-update-slice_fusion.2 = bf16[2,2,8320]{2,1,0:T(2,128)(2,1)S(1)} fusion(bf16[2,2,8320]{2,1,0:T(2,128)(2,1)S(1)} %dynamic_update_slice.12, bf16[1,2,128]{2,1,0:T(2,128)(2,1)} %pack.1), kind=kLoop, calls=%fused_computation.2 | loop fusion | bytes 1024 | tf_op jit(solution)/shard_map/dynamic_update_slice | solution.py:401
  7.3 0.0 collective-permute-done.1
  7.3 1.5 %collective-permute-done.2 = bf16[1,2,128]{2,1,0:T(2,128)(2,1)S(1)} collective-permute-done((bf16[1,2,128]{2,1,0:T(2,128)(2,1)}, bf16[1,2,128]{2,1,0:T(2,128)(2,1)S(1)}, u32[]{:S(2)}, u32[]{:S(2)}) %collective-permute-start.2) | collective-permute-done | bytes 544 | tf_op jit(solution)/shard_map/ppermute | solution.py:345
  8.8 1.6 %collective-permute-start.5 = (bf16[2,2,8320]{2,1,0:T(2,128)(2,1)S(1)}, bf16[2,2,8320]{2,1,0:T(2,128)(2,1)S(1)}, u32[]{:S(2)}, u32[]{:S(2)}) collective-permute-start(bf16[2,2,8320]{2,1,0:T(2,128)(2,1)S(1)} %constant_dynamic-update-slice_fusion.refs_0_), channel_id=1, source_target_pairs={{0,4},{1,5},{2,6},{3,7},{4,0},{5,1},{6,2},{7,3},{8,12},{9,13},{10,... | collective-permute-start | bytes 199688 | tf_op jit(solution)/shard_map/ppermute | solution.py:345
  10.4 2.5 %collective-permute-start.4 = (bf16[2,2,8320]{2,1,0:T(2,128)(2,1)S(1)}, bf16[2,2,8320]{2,1,0:T(2,128)(2,1)S(1)}, u32[]{:S(2)}, u32[]{:S(2)}) collective-permute-start(bf16[2,2,8320]{2,1,0:T(2,128)(2,1)S(1)} %constant_dynamic-update-slice_fusion.refs_0_), channel_id=1, source_target_pairs={{0,12},{1,13},{2,14},{3,15},{4,8},{5,9},{6,10},{7,11},{8,4},{9,5},... | collective-permute-start | bytes 199688 | tf_op jit(solution)/shard_map/ppermute | solution.py:345
  12.8 0.1 collective-permute-start.3
  12.9 0.0 copy-start.1
  13.0 0.9 %copy-done.1 = f32[16,4096]{1,0:T(8,128)S(1)} copy-done((f32[16,4096]{1,0:T(8,128)S(1)}, f32[16,4096]{1,0:T(8,128)}, u32[]{:S(2)}) %copy-start.1) | copy-done | bytes 262168
  13.9 0.0 copy-start.2
  13.9 0.9 %copy-done.2 = f32[16,4096]{1,0:T(8,128)S(1)} copy-done((f32[16,4096]{1,0:T(8,128)S(1)}, f32[16,4096]{1,0:T(8,128)}, u32[]{:S(2)}) %copy-start.2) | copy-done | bytes 262168
  14.9 0.1 tables.1.refs_5_
  15.0 0.0 copy-done
  15.0 0.3 %power.1 = (bf16[64,8192]{1,0:T(8,128)(2,1)S(1)}, bf16[64,4096]{1,0:T(8,128)(2,1)S(1)}, bf16[64,4096]{1,0:T(8,128)(2,1)S(1)}) custom-call(bf16[32,8192]{1,0:T(8,128)(2,1)S(1)} %bitcast.6, bf16[32,8192]{1,0:T(8,128)(2,1)S(1)} %collective-permute-done.other_ref), custom_call_target="tpu_custom_call" | custom-call | flops 4194304 | bytes 2097152 | tf_op jit(solution)/shard_map/power/pallas_call | solution.py:372
  15.3 0.0 collective-permute-done.5.refs_1_
  15.3 1.5 %scores.2 = (bf16[72,8192]{1,0:T(8,128)(2,1)S(1)}, f32[1,32,72]{2,1,0:T(8,128)S(1)}, f32[1,32,72]{2,1,0:T(8,128)S(1)}, f32[1,1,128]{2,1,0:T(1,128)S(1)}) custom-call(bf16[2,2,8320]{2,1,0:T(2,128)(2,1)S(1)} %constant_dynamic-update-slice_fusion.refs_0_, bf16[2,2,8320]{2,1,0:T(2,128)(2,1)S(1)} %collective-permute-done.5.refs_1_, ...), custom_call_target="tpu_custom_call" | custom-call | flops 84934656 | bytes 1179648 | tf_op jit(solution)/shard_map/scores/pallas_call | solution.py:419
  16.9 0.0 collective-permute-done.4.refs_1_
  16.9 1.9 %collective-permute-done.3.refs_0_ = bf16[2,2,8320]{2,1,0:T(2,128)(2,1)S(1)} collective-permute-done((bf16[2,2,8320]{2,1,0:T(2,128)(2,1)S(1)}, bf16[2,2,8320]{2,1,0:T(2,128)(2,1)S(1)}, u32[]{:S(2)}, u32[]{:S(2)}) %collective-permute-start.3) | collective-permute-done | bytes 66592 | tf_op jit(solution)/shard_map/ppermute | solution.py:345
  18.8 1.6 %scores.3 = (bf16[72,8192]{1,0:T(8,128)(2,1)S(1)}, f32[2,32,72]{2,1,0:T(8,128)S(1)}, f32[2,32,72]{2,1,0:T(8,128)S(1)}, f32[16,1,128]{2,1,0:T(1,128)S(1)}) custom-call(bf16[2,2,8320]{2,1,0:T(2,128)(2,1)S(1)} %collective-permute-done.3.refs_0_, bf16[2,2,8320]{2,1,0:T(2,128)(2,1)S(1)} %collective-permute-done.4.refs_1_, ...), custom_call_target="tpu_custom_call" | custom-call | flops 84934656 | bytes 1179648 | tf_op jit(solution)/shard_map/scores/pallas_call | solution.py:419
  20.3 0.1 collective-permute-start.8
  20.4 0.5 %collective-permute-start.7 = (bf16[72,8192]{1,0:T(8,128)(2,1)S(1)}, bf16[72,8192]{1,0:T(8,128)(2,1)S(1)}, u32[]{:S(2)}, u32[]{:S(2)}) collective-permute-start(bf16[72,8192]{1,0:T(8,128)(2,1)S(1)} %get-tuple-element.32.refs_3_), channel_id=1, source_target_pairs={{0,1},{1,0},{2,3},{3,2},{4,5},{5,4},{6,7},{7,6},{8,9},{9,8},{10,11... | collective-permute-start | bytes 3538952 | tf_op jit(solution)/shard_map/ppermute | solution.py:345
  20.9 0.1 collective-permute-start.6
  21.0 10.1 %all_to_all.5 = f32[16,1,128]{2,1,0:T(1,128)S(1)} all-to-all(f32[16,1,128]{2,1,0:T(1,128)S(1)} %get-tuple-element.29), channel_id=1, replica_groups=mesh['groups'=2,'blk'=16] {'blk'}, dimensions={0} | all-to-all | bytes 16384 | tf_op jit(solution)/shard_map/all_to_all | solution.py:451
  31.1 0.0 collective-permute-done.6.refs_2_
  31.1 0.0 collective-permute-done.8.refs_6_
  31.1 0.0 collective-permute-done.7.refs_5_
  31.1 1.8 %slices.1 = (f32[32,8192]{1,0:T(8,128)}, f32[2]{0:T(128)}, f32[2]{0:T(128)}) custom-call(f32[8,2,1,128]{3,2,1,0:T(1,128)S(1)} %bitcast.7, f32[2,32,72]{2,1,0:T(8,128)S(1)} %get-tuple-element.30.refs_1_, f32[2,32,72]{2,1,0:T(8,128)S(1)} %collective-permute-done.6.refs_2_, bf16[72,8192]{1,0:T(8,128)(2,1)S(1)} %get-tuple-element.32.refs_3_, ...), custom_call_target="tpu_custom_call" | custom-call | tf_op jit(solution)/shard_map/slices/pallas_call | solution.py:454
  (2 shorter events, 0.0 us)
Async XLA Ops:
  0.6 14.4 %copy-start = (bf16[2,16,8192]{2,1,0:T(8,128)(2,1)S(1)}, bf16[2,16,8192]{2,1,0:T(8,128)(2,1)}, u32[]{:S(2)}) copy-start(bf16[2,16,8192]{2,1,0:T(8,128)(2,1)} %param.7) | copy-start | bytes 1572868
  0.6 4.4 %collective-permute-start = (bf16[32,8192]{1,0:T(8,128)(2,1)}, bf16[32,8192]{1,0:T(8,128)(2,1)S(1)}, u32[]{:S(2)}, u32[]{:S(2)}) collective-permute-start(bf16[32,8192]{1,0:T(8,128)(2,1)} %bitcast.5), channel_id=1, source_target_pairs={{0,1},{1,0},{2,3},{3,2},{4,5},{5,4},{6,7},{7,6},{8,9},{9,8},{10,11... | collective-permute-start | bytes 1572872 | tf_op jit(solution)/shard_map/ppermute | solution.py:345
  1.2 6.1 %collective-permute-start.1 = (bf16[1,2,8192]{2,1,0:T(2,128)(2,1)}, bf16[1,2,8192]{2,1,0:T(2,128)(2,1)S(1)}, u32[]{:S(2)}, u32[]{:S(2)}) collective-permute-start(bf16[1,2,8192]{2,1,0:T(2,128)(2,1)} %bitcast.8), channel_id=1, source_target_pairs={{0,2},{1,3},{2,0},{3,1},{4,6},{5,7},{6,4},{7,5},{8,10},{9,11},{10,... | collective-permute-start | bytes 98312 | tf_op jit(solution)/shard_map/ppermute | solution.py:345
  5.0 3.7 %collective-permute-start.2 = (bf16[1,2,128]{2,1,0:T(2,128)(2,1)}, bf16[1,2,128]{2,1,0:T(2,128)(2,1)S(1)}, u32[]{:S(2)}, u32[]{:S(2)}) collective-permute-start(bf16[1,2,128]{2,1,0:T(2,128)(2,1)} %pack.1), channel_id=1, source_target_pairs={{0,2},{1,3},{2,0},{3,1},{4,6},{5,7},{6,4},{7,5},{8,10},{9,11},{10,... | collective-permute-start | bytes 1544 | tf_op jit(solution)/shard_map/ppermute | solution.py:345
  8.8 6.6 %collective-permute-start.5 = (bf16[2,2,8320]{2,1,0:T(2,128)(2,1)S(1)}, bf16[2,2,8320]{2,1,0:T(2,128)(2,1)S(1)}, u32[]{:S(2)}, u32[]{:S(2)}) collective-permute-start(bf16[2,2,8320]{2,1,0:T(2,128)(2,1)S(1)} %constant_dynamic-update-slice_fusion.refs_0_), channel_id=1, source_target_pairs={{0,4},{1,5},{2,6},{3,7},{4,0},{5,1},{6,2},{7,3},{8,12},{9,13},{10,... | collective-permute-start | bytes 199688 | tf_op jit(solution)/shard_map/ppermute | solution.py:345
  10.4 6.5 %collective-permute-start.4 = (bf16[2,2,8320]{2,1,0:T(2,128)(2,1)S(1)}, bf16[2,2,8320]{2,1,0:T(2,128)(2,1)S(1)}, u32[]{:S(2)}, u32[]{:S(2)}) collective-permute-start(bf16[2,2,8320]{2,1,0:T(2,128)(2,1)S(1)} %constant_dynamic-update-slice_fusion.refs_0_), channel_id=1, source_target_pairs={{0,12},{1,13},{2,14},{3,15},{4,8},{5,9},{6,10},{7,11},{8,4},{9,5},... | collective-permute-start | bytes 199688 | tf_op jit(solution)/shard_map/ppermute | solution.py:345
  12.8 5.9 %collective-permute-start.3 = (bf16[2,2,8320]{2,1,0:T(2,128)(2,1)S(1)}, bf16[2,2,8320]{2,1,0:T(2,128)(2,1)S(1)}, u32[]{:S(2)}, u32[]{:S(2)}) collective-permute-start(bf16[2,2,8320]{2,1,0:T(2,128)(2,1)S(1)} %constant_dynamic-update-slice_fusion.refs_0_), channel_id=1, source_target_pairs={{0,8},{1,9},{2,10},{3,11},{4,12},{5,13},{6,14},{7,15},{8,0},{9,1},... | collective-permute-start | bytes 199688 | tf_op jit(solution)/shard_map/ppermute | solution.py:345
  12.9 0.9 %copy-start.1 = (f32[16,4096]{1,0:T(8,128)S(1)}, f32[16,4096]{1,0:T(8,128)}, u32[]{:S(2)}) copy-start(f32[16,4096]{1,0:T(8,128)} %ctf_ref.1) | copy-start | bytes 786436
  13.9 0.9 %copy-start.2 = (f32[16,4096]{1,0:T(8,128)S(1)}, f32[16,4096]{1,0:T(8,128)}, u32[]{:S(2)}) copy-start(f32[16,4096]{1,0:T(8,128)} %noise_ref.1) | copy-start | bytes 786436
  20.3 10.8 %collective-permute-start.8 = (bf16[72,8192]{1,0:T(8,128)(2,1)S(1)}, bf16[72,8192]{1,0:T(8,128)(2,1)S(1)}, u32[]{:S(2)}, u32[]{:S(2)}) collective-permute-start(bf16[72,8192]{1,0:T(8,128)(2,1)S(1)} %get-tuple-element.33.refs_4_), channel_id=1, source_target_pairs={{0,1},{1,0},{2,3},{3,2},{4,5},{5,4},{6,7},{7,6},{8,9},{9,8},{10,11... | collective-permute-start | bytes 3538952 | tf_op jit(solution)/shard_map/ppermute | solution.py:345
  20.4 10.7 %collective-permute-start.7 = (bf16[72,8192]{1,0:T(8,128)(2,1)S(1)}, bf16[72,8192]{1,0:T(8,128)(2,1)S(1)}, u32[]{:S(2)}, u32[]{:S(2)}) collective-permute-start(bf16[72,8192]{1,0:T(8,128)(2,1)S(1)} %get-tuple-element.32.refs_3_), channel_id=1, source_target_pairs={{0,1},{1,0},{2,3},{3,2},{4,5},{5,4},{6,7},{7,6},{8,9},{9,8},{10,11... | collective-permute-start | bytes 3538952 | tf_op jit(solution)/shard_map/ppermute | solution.py:345
  20.9 10.2 %collective-permute-start.6 = (f32[2,32,72]{2,1,0:T(8,128)S(1)}, f32[2,32,72]{2,1,0:T(8,128)S(1)}, u32[]{:S(2)}, u32[]{:S(2)}) collective-permute-start(f32[2,32,72]{2,1,0:T(8,128)S(1)} %get-tuple-element.31), channel_id=1, source_target_pairs={{0,1},{1,0},{2,3},{3,2},{4,5},{5,4},{6,7},{7,6},{8,9},{9,8},{10,11... | collective-permute-start | bytes 55304 | tf_op jit(solution)/shard_map/ppermute | solution.py:345

commit v9 on v8

--- a/solution.py
+++ b/solution.py
@@ -112,13 +112,22 @@
     if has_earlier:
         earlier_own_ref, earlier_other_ref, earlier_stats_ref = refs[:3]
         refs = refs[3:]
-    weighted_ref, exps_ref, exps_other_ref, stats_ref = refs[:4]
-    image_ref, real_ref, imag_ref, cross_ref, square_ref = refs[4:]
+    weighted_ref, exps_ref, *exps_other_refs, stats_ref = refs[:-5]
+    image_ref, real_ref, imag_ref, cross_ref, square_ref = refs[-5:]
     full = both_ref.shape[1]
     half = full // 2
     groups = table_ref.shape[0] // 3
     candidates = both_ref.shape[0]
     rows_total = image_ref.shape[0]
+
+    def put_exps(slot, values):
+        for ref in exps_other_refs:
+            ref[slot] = values
+        if has_earlier:
+            for third, part in enumerate(split_thirds(values)):
+                at = pl.ds(full + (3 * slot + third) * LANES, values.shape[1])
+                weighted_ref[pl.ds(0, values.shape[0]), at] = part
+
     per_device = pieces[0].shape[1]
     scale = 0.5 / math.sqrt(half)
     chip = lax.axis_index("blk") >> 1
@@ -134,7 +143,7 @@
     slot = 1 if has_earlier else 0
     if has_earlier:
         exps_ref[0] = earlier_own_ref[0]
-        exps_other_ref[0] = earlier_other_ref[0]
+        put_exps(0, earlier_other_ref[0])
 
     def block(index, carry):
         rows = pl.ds(pl.multiple_of(index * ROWS, ROWS), ROWS)
@@ -227,7 +236,7 @@
             square_ref[pl.ds(shift * ROWS, ROWS), :candidates] = exps[shift]
         turned = square_ref[...].T
         exps_ref[index + slot] = turned[: candidates // 2, :block_rows]
-        exps_other_ref[index + slot] = turned[candidates // 2 : candidates, :block_rows]
+        put_exps(index + slot, turned[candidates // 2 : candidates, :block_rows])
         row = lax.broadcasted_iota(jnp.int32, (ROWS, LANES), 0)
         lane = lax.broadcasted_iota(jnp.int32, (ROWS, LANES), 1)
         half_at = chip // NEAR ^ slot if by_distance else 0
@@ -247,10 +256,13 @@
 
 
 def slice_kernel(scale, calls, by_distance, *refs):
-    stats_ref, exps_own_ref, exps_other_ref = refs[:3]
-    weighted_refs = (refs[3 : 3 + calls], refs[3 + calls : 3 + 2 * calls])
-    out_hbm, best_hbm, log_hbm = refs[3 + 2 * calls : 6 + 2 * calls]
-    best_ref, log_ref, posterior_ref, summed_ref, sems, number_sems = refs[6 + 2 * calls :]
+    stats_ref, exps_own_ref = refs[:2]
+    refs = refs[2:]
+    if not by_distance:
+        exps_other_ref, *refs = refs
+    weighted_refs = (refs[:calls], refs[calls : 2 * calls])
+    out_hbm, best_hbm, log_hbm = refs[2 * calls : 2 * calls + 3]
+    best_ref, log_ref, posterior_ref, summed_ref, sems, number_sems = refs[2 * calls + 3 :]
     blocks, rows, block_rows = exps_own_ref.shape
     chips = stats_ref.shape[0]
     per_device = best_ref.shape[0]
@@ -274,7 +286,20 @@
         return top, top + jnp.log(total), tops[-1]
 
     upper = (lane & ROWS) != 0
-    for side, exps_ref in enumerate((exps_own_ref, exps_other_ref)):
+    def exps_of(side, block):
+        if side == 0:
+            return exps_own_ref[block]
+        if not by_distance:
+            return exps_other_ref[block]
+        parts = [
+            weighted_refs[1][-1][
+                pl.ds(0, rows), pl.ds(full + (3 * block + third) * LANES, block_rows)
+            ].astype(jnp.float32)
+            for third in range(3)
+        ]
+        return parts[0] + (parts[1] + parts[2])
+
+    for side in range(2):
         core = (index & 1) ^ side
         for block in range(blocks):
             if block == 0 or not by_distance:
@@ -283,7 +308,7 @@
                 crossed = pltpu.roll(line, ROWS, 1)
             wanted = (chip // NEAR ^ block) != 0 if by_distance else False
             factor = jnp.where(upper == wanted, line, crossed)
-            posterior_ref[side, block] = (exps_ref[block] * factor[:, :block_rows]).astype(
+            posterior_ref[side, block] = (exps_of(side, block) * factor[:, :block_rows]).astype(
                 jnp.bfloat16
             )
 
@@ -366,7 +391,7 @@
     flat = projections.reshape(own_rows, full)
     other = swap(flat, 1)
     if by_distance:
-        rows, numbers, other = lax.optimization_barrier((rows, numbers, other))
+        rows, numbers = lax.optimization_barrier((rows, numbers))
         received_numbers = swap(numbers, 2)
     groups = ctf_table.shape[0]
     both, high, low = pl.pallas_call(
@@ -416,18 +441,21 @@
         last = len(all_weighted) == len(parts) - 1
         own_blocks = blocks // len(parts)
         seen = blocks if last else own_blocks
+        exps_shape = jax.ShapeDtypeStruct((seen, own_rows, block_rows), jnp.float32)
         weighted, *earlier = pl.pallas_call(
             functools.partial(score_kernel, sources, by_distance, shifts, bool(earlier)),
             out_shape=(
-                jax.ShapeDtypeStruct((own_blocks * block_rows, full), jnp.bfloat16),
-                jax.ShapeDtypeStruct((seen, own_rows, block_rows), jnp.float32),
-                jax.ShapeDtypeStruct((seen, own_rows, block_rows), jnp.float32),
+                jax.ShapeDtypeStruct(
+                    (own_blocks * block_rows, full + (3 * blocks * LANES if earlier else 0)),
+                    jnp.bfloat16,
+                ),
+                *([exps_shape] if earlier else [exps_shape] * 2),
                 jax.ShapeDtypeStruct(
                     (axis_size if last else 1, 1 if by_distance else blocks, LANES), jnp.float32
                 ),
             ),
             in_specs=[VMEM] * (len(pieces) + 4 + len(earlier)),
-            out_specs=(VMEM,) * 4,
+            out_specs=(VMEM,) * (3 if earlier else 4),
             scratch_shapes=[
                 pltpu.VMEM((own_blocks * ROWS, full + LANES), jnp.float32),
                 pltpu.VMEM((ROWS, half), jnp.float32),
@@ -444,10 +472,10 @@
             name="scores",
         )(*pieces, both, high, low, tables, *earlier)
         all_weighted.append(weighted)
-    exps, exps_other, stats = earlier
+    exps, *exps_other, stats = earlier
 
     exchanged = [swap(weighted, 1) for weighted in all_weighted]
-    exps_in = swap(exps_other, 1)
+    exps_in = [swap(part, 1) for part in exps_other]
     gathered = lax.all_to_all(stats, "blk", 0, 0)
     gathered = gathered.reshape((chips, 2) + gathered.shape[1:])
 
@@ -460,7 +488,7 @@
             jax.ShapeDtypeStruct((per_device,), jnp.float32),
             jax.ShapeDtypeStruct((per_device,), jnp.float32),
         ),
-        in_specs=[VMEM] * (3 + 2 * len(all_weighted)),
+        in_specs=[VMEM] * (2 + len(exps_in) + 2 * len(all_weighted)),
         out_specs=(HBM, HBM, HBM),
         scratch_shapes=[
             pltpu.SMEM((per_device,), jnp.float32),
@@ -472,7 +500,7 @@
         ],
         compiler_params=params,
         name="slices",
-    )(gathered, exps, exps_in, *all_weighted, *exchanged)
+    )(gathered, exps, *exps_in, *all_weighted, *exchanged)
     return (slices.reshape(batch_count, orient_dev, full), best_posterior, log_total)
 
 

time: 33.2 us -> 33.5 us (level)
  starting transfers between devices: 8.69 us -> 7.98 us
  blocking collectives: 10.1 us -> 10.6 us
  waiting for transfers between devices: 3.35 us -> 3.85 us
    ppermute x9 -> x8, starting transfers between devices: 8.69 us -> 7.98 us  [swap(): return lax.ppermute(value, 'blk', [(i, i ^ mask) for i in range(axis_size)])]
    all_to_all x1, blocking collectives: 10.1 us -> 10.6 us  [local(): gathered = lax.all_to_all(stats, 'blk', 0, 0)]
    ppermute x9 -> x8, waiting for transfers between devices: 3.35 us -> 3.85 us  [swap(): return lax.ppermute(value, 'blk', [(i, i ^ mask) for i in range(axis_size)])]
  transfers between devices with their start and end apart: 9 -> 8, of which waited for: 2 -> 2; matrix products, arithmetic and copies ran while one was open for 5% -> 5% of each run, Pallas kernels for 10% -> 10%
where the time goes in v9:
time: 33.5 us; the launch traced here: 33.2 us
  blocking collectives  10.6 us (32%)
  starting transfers between devices  7.98 us (24%)
  Pallas kernels  6.63 us (20%)
  waiting for transfers between devices  3.85 us (11%)
  local copies, waits for them, and re-layouts  3.41 us (10%)
  between operations  0.72 us (2%)
    all_to_all x1, blocking collectives, local(): gathered = lax.all_to_all(stats, 'blk', 0, 0)  10.6 us
    ppermute x8, starting transfers between devices, swap(): return lax.ppermute(value, 'blk', [(i, i ^ mask) for i in range(axis_size)])  7.98 us
    ppermute x8, waiting for transfers between devices, swap(): return lax.ppermute(value, 'blk', [(i, i ^ mask) for i in range(axis_size)])  3.85 us
    pallas_call x2, Pallas kernels, local(): pl.pallas_call(functools.partial(score_kernel, sources, by_distance, shif...  3.08 us
    unnamed x6, local copies, waits for them, and re-layouts  1.91 us
    pallas_call x1, Pallas kernels, local(): pl.pallas_call(functools.partial(slice_kernel, own_rows / per_device, len...  1.81 us
    pallas_call x1, Pallas kernels, local(): pl.pallas_call(pack_kernel, out_shape=jax.ShapeDtypeStruct((1, per_device...  1.26 us
    dynamic_update_slice x1, local copies, waits for them, and re-layouts, local(): pair = lax.dynamic_update_slice(pair, rows, (0, 0, 0))  0.8 us
  transfers between devices with their start and end apart: 8, of which 2 were waited for; matrix products, arithmetic and copies ran while one was open for 5% of the time, Pallas kernels for 10%

profile of v9, /device:TPU:0, one launch (start us, length us, event | category | flops | bytes accessed | tf_op | source)
XLA Modules:
  0.0 33.2 jit_solution(13708815907988012613)
XLA Ops:
  0.6 0.0 copy-start
  0.6 3.0 %collective-permute-start = (bf16[1,2,8192]{2,1,0:T(2,128)(2,1)}, bf16[1,2,8192]{2,1,0:T(2,128)(2,1)S(1)}, u32[]{:S(2)}, u32[]{:S(2)}) collective-permute-start(bf16[1,2,8192]{2,1,0:T(2,128)(2,1)} %bitcast.8), channel_id=1, source_target_pairs={{0,2},{1,3},{2,0},{3,1},{4,6},{5,7},{6,4},{7,5},{8,10},{9,11},{10,... | collective-permute-start | bytes 98312 | tf_op jit(solution)/shard_map/ppermute | solution.py:370
  3.7 1.3 %pack.1 = bf16[1,2,128]{2,1,0:T(2,128)(2,1)} custom-call(s32[2]{0:T(128)} %group_hbm.1, s32[2]{0:T(128)} %limit_hbm.1, s32[2,2,9]{2,1,0:T(2,128)} %bitcast.10), custom_call_target="tpu_custom_call" | custom-call | tf_op jit(solution)/shard_map/pack/pallas_call | solution.py:372
  4.9 0.2 collective-permute-start.1
  5.2 0.0 collective-permute-start.4
  5.2 0.8 %dynamic_update_slice.12 = bf16[2,2,8320]{2,1,0:T(2,128)(2,1)S(1)} pad(bf16[1,2,8192]{2,1,0:T(2,128)(2,1)} %bitcast.9, bf16[]{:T(256)} %constant.0.clone.1), padding=0_1x0_0x0_128 | pad | bytes 99330 | tf_op jit(solution)/shard_map/dynamic_update_slice | solution.py:425
  6.0 0.7 %constant_dynamic-update-slice_fusion.2 = bf16[2,2,8320]{2,1,0:T(2,128)(2,1)S(1)} fusion(bf16[2,2,8320]{2,1,0:T(2,128)(2,1)S(1)} %dynamic_update_slice.12, bf16[1,2,128]{2,1,0:T(2,128)(2,1)} %pack.1), kind=kLoop, calls=%fused_computation.2 | loop fusion | bytes 1024 | tf_op jit(solution)/shard_map/dynamic_update_slice | solution.py:426
  6.6 0.0 collective-permute-done
  6.7 2.0 %collective-permute-done.1 = bf16[1,2,128]{2,1,0:T(2,128)(2,1)S(1)} collective-permute-done((bf16[1,2,128]{2,1,0:T(2,128)(2,1)}, bf16[1,2,128]{2,1,0:T(2,128)(2,1)S(1)}, u32[]{:S(2)}, u32[]{:S(2)}) %collective-permute-start.1) | collective-permute-done | bytes 544 | tf_op jit(solution)/shard_map/ppermute | solution.py:370
  8.7 1.6 %collective-permute-start.5 = (bf16[2,2,8320]{2,1,0:T(2,128)(2,1)S(1)}, bf16[2,2,8320]{2,1,0:T(2,128)(2,1)S(1)}, u32[]{:S(2)}, u32[]{:S(2)}) collective-permute-start(bf16[2,2,8320]{2,1,0:T(2,128)(2,1)S(1)} %constant_dynamic-update-slice_fusion.refs_0_), channel_id=1, source_target_pairs={{0,4},{1,5},{2,6},{3,7},{4,0},{5,1},{6,2},{7,3},{8,12},{9,13},{10,... | collective-permute-start | bytes 199688 | tf_op jit(solution)/shard_map/ppermute | solution.py:370
  10.3 2.5 %collective-permute-start.3 = (bf16[2,2,8320]{2,1,0:T(2,128)(2,1)S(1)}, bf16[2,2,8320]{2,1,0:T(2,128)(2,1)S(1)}, u32[]{:S(2)}, u32[]{:S(2)}) collective-permute-start(bf16[2,2,8320]{2,1,0:T(2,128)(2,1)S(1)} %constant_dynamic-update-slice_fusion.refs_0_), channel_id=1, source_target_pairs={{0,12},{1,13},{2,14},{3,15},{4,8},{5,9},{6,10},{7,11},{8,4},{9,5},... | collective-permute-start | bytes 199688 | tf_op jit(solution)/shard_map/ppermute | solution.py:370
  12.7 0.1 collective-permute-start.2
  12.9 0.0 copy-start.1
  12.9 0.9 %copy-done.1 = f32[16,4096]{1,0:T(8,128)S(1)} copy-done((f32[16,4096]{1,0:T(8,128)S(1)}, f32[16,4096]{1,0:T(8,128)}, u32[]{:S(2)}) %copy-start.1) | copy-done | bytes 262168
  13.8 0.0 copy-start.2
  13.8 0.9 %copy-done.2 = f32[16,4096]{1,0:T(8,128)S(1)} copy-done((f32[16,4096]{1,0:T(8,128)S(1)}, f32[16,4096]{1,0:T(8,128)}, u32[]{:S(2)}) %copy-start.2) | copy-done | bytes 262168
  14.8 0.1 tables.1.refs_5_
  14.9 0.0 collective-permute-done.4.other_ref
  14.9 0.0 copy-done
  14.9 0.3 %power.1 = (bf16[64,8192]{1,0:T(8,128)(2,1)S(1)}, bf16[64,4096]{1,0:T(8,128)(2,1)S(1)}, bf16[64,4096]{1,0:T(8,128)(2,1)S(1)}) custom-call(bf16[32,8192]{1,0:T(8,128)(2,1)S(1)} %bitcast.6, bf16[32,8192]{1,0:T(8,128)(2,1)S(1)} %collective-permute-done.4.other_ref), custom_call_target="tpu_custom_call" | custom-call | flops 4194304 | bytes 2097152 | tf_op jit(solution)/shard_map/power/pallas_call | solution.py:397
  15.3 0.0 collective-permute-done.5.refs_1_
  15.3 1.6 %scores.2 = (bf16[72,8192]{1,0:T(8,128)(2,1)S(1)}, f32[1,32,72]{2,1,0:T(8,128)S(1)}, f32[1,32,72]{2,1,0:T(8,128)S(1)}, f32[1,1,128]{2,1,0:T(1,128)S(1)}) custom-call(bf16[2,2,8320]{2,1,0:T(2,128)(2,1)S(1)} %constant_dynamic-update-slice_fusion.refs_0_, bf16[2,2,8320]{2,1,0:T(2,128)(2,1)S(1)} %collective-permute-done.5.refs_1_, ...), custom_call_target="tpu_custom_call" | custom-call | flops 84934656 | bytes 1179648 | tf_op jit(solution)/shard_map/scores/pallas_call | solution.py:445
  16.9 0.0 collective-permute-done.3.refs_1_
  16.9 1.8 %collective-permute-done.2.refs_0_ = bf16[2,2,8320]{2,1,0:T(2,128)(2,1)S(1)} collective-permute-done((bf16[2,2,8320]{2,1,0:T(2,128)(2,1)S(1)}, bf16[2,2,8320]{2,1,0:T(2,128)(2,1)S(1)}, u32[]{:S(2)}, u32[]{:S(2)}) %collective-permute-start.2) | collective-permute-done | bytes 66592 | tf_op jit(solution)/shard_map/ppermute | solution.py:370
  18.7 1.5 %scores.3 = (bf16[72,8960]{1,0:T(8,128)(2,1)S(1)}, f32[2,32,72]{2,1,0:T(8,128)S(1)}, f32[16,1,128]{2,1,0:T(1,128)S(1)}) custom-call(bf16[2,2,8320]{2,1,0:T(2,128)(2,1)S(1)} %collective-permute-done.2.refs_0_, bf16[2,2,8320]{2,1,0:T(2,128)(2,1)S(1)} %collective-permute-done.3.refs_1_, bf16[64,8192]{1,0:T(8,128)(2,1)S(1)} %get-tuple-element.20.refs_2_, ...), custom_call_target="tpu_custom_call" | custom-call | flops 84934656 | bytes 1179648 | tf_op jit(solution)/shard_map/scores/pallas_call | solution.py:445
  20.2 0.1 collective-permute-start.7
  20.3 0.5 %collective-permute-start.6 = (bf16[72,8192]{1,0:T(8,128)(2,1)S(1)}, bf16[72,8192]{1,0:T(8,128)(2,1)S(1)}, u32[]{:S(2)}, u32[]{:S(2)}) collective-permute-start(bf16[72,8192]{1,0:T(8,128)(2,1)S(1)} %get-tuple-element.28.refs_2_), channel_id=1, source_target_pairs={{0,1},{1,0},{2,3},{3,2},{4,5},{5,4},{6,7},{7,6},{8,9},{9,8},{10,11... | collective-permute-start | bytes 3538952 | tf_op jit(solution)/shard_map/ppermute | solution.py:370
  20.8 10.6 %all_to_all.5 = f32[16,1,128]{2,1,0:T(1,128)S(1)} all-to-all(f32[16,1,128]{2,1,0:T(1,128)S(1)} %get-tuple-element.26), channel_id=1, replica_groups=mesh['groups'=2,'blk'=16] {'blk'}, dimensions={0} | all-to-all | bytes 16384 | tf_op jit(solution)/shard_map/all_to_all | solution.py:479
  31.4 0.0 collective-permute-done.6.refs_4_
  31.4 0.0 collective-permute-done.7.refs_5_
  31.4 1.8 %slices.1 = (f32[32,8192]{1,0:T(8,128)}, f32[2]{0:T(128)}, f32[2]{0:T(128)}) custom-call(f32[8,2,1,128]{3,2,1,0:T(1,128)S(1)} %bitcast.7, f32[2,32,72]{2,1,0:T(8,128)S(1)} %get-tuple-element.27.refs_1_, bf16[72,8192]{1,0:T(8,128)(2,1)S(1)} %get-tuple-element.28.refs_2_, bf16[72,8960]{1,0:T(8,128)(2,1)S(1)} %get-tuple-element.29.refs_3_, ...), custom_call_target="tpu_custom_call" | custom-call | tf_op jit(solution)/shard_map/slices/pallas_call | solution.py:482
  (2 shorter events, 0.0 us)
Async XLA Ops:
  0.6 14.3 %copy-start = (bf16[2,16,8192]{2,1,0:T(8,128)(2,1)S(1)}, bf16[2,16,8192]{2,1,0:T(8,128)(2,1)}, u32[]{:S(2)}) copy-start(bf16[2,16,8192]{2,1,0:T(8,128)(2,1)} %param.7) | copy-start | bytes 1572868
  0.6 6.0 %collective-permute-start = (bf16[1,2,8192]{2,1,0:T(2,128)(2,1)}, bf16[1,2,8192]{2,1,0:T(2,128)(2,1)S(1)}, u32[]{:S(2)}, u32[]{:S(2)}) collective-permute-start(bf16[1,2,8192]{2,1,0:T(2,128)(2,1)} %bitcast.8), channel_id=1, source_target_pairs={{0,2},{1,3},{2,0},{3,1},{4,6},{5,7},{6,4},{7,5},{8,10},{9,11},{10,... | collective-permute-start | bytes 98312 | tf_op jit(solution)/shard_map/ppermute | solution.py:370
  4.9 3.7 %collective-permute-start.1 = (bf16[1,2,128]{2,1,0:T(2,128)(2,1)}, bf16[1,2,128]{2,1,0:T(2,128)(2,1)S(1)}, u32[]{:S(2)}, u32[]{:S(2)}) collective-permute-start(bf16[1,2,128]{2,1,0:T(2,128)(2,1)} %pack.1), channel_id=1, source_target_pairs={{0,2},{1,3},{2,0},{3,1},{4,6},{5,7},{6,4},{7,5},{8,10},{9,11},{10,... | collective-permute-start | bytes 1544 | tf_op jit(solution)/shard_map/ppermute | solution.py:370
  5.2 9.7 %collective-permute-start.4 = (bf16[32,8192]{1,0:T(8,128)(2,1)}, bf16[32,8192]{1,0:T(8,128)(2,1)S(1)}, u32[]{:S(2)}, u32[]{:S(2)}) collective-permute-start(bf16[32,8192]{1,0:T(8,128)(2,1)} %bitcast.5), channel_id=1, source_target_pairs={{0,1},{1,0},{2,3},{3,2},{4,5},{5,4},{6,7},{7,6},{8,9},{9,8},{10,11... | collective-permute-start | bytes 1572872 | tf_op jit(solution)/shard_map/ppermute | solution.py:370
  8.7 6.6 %collective-permute-start.5 = (bf16[2,2,8320]{2,1,0:T(2,128)(2,1)S(1)}, bf16[2,2,8320]{2,1,0:T(2,128)(2,1)S(1)}, u32[]{:S(2)}, u32[]{:S(2)}) collective-permute-start(bf16[2,2,8320]{2,1,0:T(2,128)(2,1)S(1)} %constant_dynamic-update-slice_fusion.refs_0_), channel_id=1, source_target_pairs={{0,4},{1,5},{2,6},{3,7},{4,0},{5,1},{6,2},{7,3},{8,12},{9,13},{10,... | collective-permute-start | bytes 199688 | tf_op jit(solution)/shard_map/ppermute | solution.py:370
  10.3 6.6 %collective-permute-start.3 = (bf16[2,2,8320]{2,1,0:T(2,128)(2,1)S(1)}, bf16[2,2,8320]{2,1,0:T(2,128)(2,1)S(1)}, u32[]{:S(2)}, u32[]{:S(2)}) collective-permute-start(bf16[2,2,8320]{2,1,0:T(2,128)(2,1)S(1)} %constant_dynamic-update-slice_fusion.refs_0_), channel_id=1, source_target_pairs={{0,12},{1,13},{2,14},{3,15},{4,8},{5,9},{6,10},{7,11},{8,4},{9,5},... | collective-permute-start | bytes 199688 | tf_op jit(solution)/shard_map/ppermute | solution.py:370
  12.7 5.9 %collective-permute-start.2 = (bf16[2,2,8320]{2,1,0:T(2,128)(2,1)S(1)}, bf16[2,2,8320]{2,1,0:T(2,128)(2,1)S(1)}, u32[]{:S(2)}, u32[]{:S(2)}) collective-permute-start(bf16[2,2,8320]{2,1,0:T(2,128)(2,1)S(1)} %constant_dynamic-update-slice_fusion.refs_0_), channel_id=1, source_target_pairs={{0,8},{1,9},{2,10},{3,11},{4,12},{5,13},{6,14},{7,15},{8,0},{9,1},... | collective-permute-start | bytes 199688 | tf_op jit(solution)/shard_map/ppermute | solution.py:370
  12.9 0.9 %copy-start.1 = (f32[16,4096]{1,0:T(8,128)S(1)}, f32[16,4096]{1,0:T(8,128)}, u32[]{:S(2)}) copy-start(f32[16,4096]{1,0:T(8,128)} %ctf_ref.1) | copy-start | bytes 786436
  13.8 0.9 %copy-start.2 = (f32[16,4096]{1,0:T(8,128)S(1)}, f32[16,4096]{1,0:T(8,128)}, u32[]{:S(2)}) copy-start(f32[16,4096]{1,0:T(8,128)} %noise_ref.1) | copy-start | bytes 786436
  20.2 11.2 %collective-permute-start.7 = (bf16[72,8960]{1,0:T(8,128)(2,1)S(1)}, bf16[72,8960]{1,0:T(8,128)(2,1)S(1)}, u32[]{:S(2)}, u32[]{:S(2)}) collective-permute-start(bf16[72,8960]{1,0:T(8,128)(2,1)S(1)} %get-tuple-element.29.refs_3_), channel_id=1, source_target_pairs={{0,1},{1,0},{2,3},{3,2},{4,5},{5,4},{6,7},{7,6},{8,9},{9,8},{10,11... | collective-permute-start | bytes 3870728 | tf_op jit(solution)/shard_map/ppermute | solution.py:370
  20.3 11.1 %collective-permute-start.6 = (bf16[72,8192]{1,0:T(8,128)(2,1)S(1)}, bf16[72,8192]{1,0:T(8,128)(2,1)S(1)}, u32[]{:S(2)}, u32[]{:S(2)}) collective-permute-start(bf16[72,8192]{1,0:T(8,128)(2,1)S(1)} %get-tuple-element.28.refs_2_), channel_id=1, source_target_pairs={{0,1},{1,0},{2,3},{3,2},{4,5},{5,4},{6,7},{7,6},{8,9},{9,8},{10,11... | collective-permute-start | bytes 3538952 | tf_op jit(solution)/shard_map/ppermute | solution.py:370

commit v10 on v8

--- a/solution.py
+++ b/solution.py
@@ -366,7 +366,7 @@
     flat = projections.reshape(own_rows, full)
     other = swap(flat, 1)
     if by_distance:
-        rows, numbers, other = lax.optimization_barrier((rows, numbers, other))
+        rows, numbers = lax.optimization_barrier((rows, numbers))
         received_numbers = swap(numbers, 2)
     groups = ctf_table.shape[0]
     both, high, low = pl.pallas_call(

time: 33.2 us -> 33.7 us (1.015)
  starting transfers between devices: 8.69 us -> 8.06 us
  blocking collectives: 10.1 us -> 10.7 us
  waiting for transfers between devices: 3.35 us -> 3.88 us
    ppermute x9, starting transfers between devices: 8.69 us -> 8.06 us  [swap(): return lax.ppermute(value, 'blk', [(i, i ^ mask) for i in range(axis_size)])]
    all_to_all x1, blocking collectives: 10.1 us -> 10.7 us  [local(): gathered = lax.all_to_all(stats, 'blk', 0, 0)]
    ppermute x9, waiting for transfers between devices: 3.35 us -> 3.88 us  [swap(): return lax.ppermute(value, 'blk', [(i, i ^ mask) for i in range(axis_size)])]
where the time goes in v10:
time: 33.7 us; the launch traced here: 33.4 us
  blocking collectives  10.7 us (32%)
  starting transfers between devices  8.06 us (24%)
  Pallas kernels  6.64 us (20%)
  waiting for transfers between devices  3.88 us (12%)
  local copies, waits for them, and re-layouts  3.41 us (10%)
  between operations  0.72 us (2%)
    all_to_all x1, blocking collectives, local(): gathered = lax.all_to_all(stats, 'blk', 0, 0)  10.7 us
    ppermute x9, starting transfers between devices, swap(): return lax.ppermute(value, 'blk', [(i, i ^ mask) for i in range(axis_size)])  8.06 us
    ppermute x9, waiting for transfers between devices, swap(): return lax.ppermute(value, 'blk', [(i, i ^ mask) for i in range(axis_size)])  3.88 us
    pallas_call x2, Pallas kernels, local(): pl.pallas_call(functools.partial(score_kernel, sources, by_distance, shif...  3.1 us
    unnamed x6, local copies, waits for them, and re-layouts  1.91 us
    pallas_call x1, Pallas kernels, local(): pl.pallas_call(functools.partial(slice_kernel, own_rows / per_device, len...  1.81 us
    pallas_call x1, Pallas kernels, local(): pl.pallas_call(pack_kernel, out_shape=jax.ShapeDtypeStruct((1, per_device...  1.26 us
    dynamic_update_slice x1, local copies, waits for them, and re-layouts, local(): pair = lax.dynamic_update_slice(pair, rows, (0, 0, 0))  0.8 us
  transfers between devices with their start and end apart: 9, of which 2 were waited for; matrix products, arithmetic and copies ran while one was open for 5% of the time, Pallas kernels for 10%

profile of v10, /device:TPU:0, one launch (start us, length us, event | category | flops | bytes accessed | tf_op | source)
XLA Modules:
  0.0 33.4 jit_solution(7473623037486035252)
XLA Ops:
  0.6 0.0 copy-start
  0.6 3.0 %collective-permute-start = (bf16[1,2,8192]{2,1,0:T(2,128)(2,1)}, bf16[1,2,8192]{2,1,0:T(2,128)(2,1)S(1)}, u32[]{:S(2)}, u32[]{:S(2)}) collective-permute-start(bf16[1,2,8192]{2,1,0:T(2,128)(2,1)} %bitcast.8), channel_id=1, source_target_pairs={{0,2},{1,3},{2,0},{3,1},{4,6},{5,7},{6,4},{7,5},{8,10},{9,11},{10,... | collective-permute-start | bytes 98312 | tf_op jit(solution)/shard_map/ppermute | solution.py:345
  3.7 1.3 %pack.1 = bf16[1,2,128]{2,1,0:T(2,128)(2,1)} custom-call(s32[2]{0:T(128)} %group_hbm.1, s32[2]{0:T(128)} %limit_hbm.1, s32[2,2,9]{2,1,0:T(2,128)} %bitcast.10), custom_call_target="tpu_custom_call" | custom-call | tf_op jit(solution)/shard_map/pack/pallas_call | solution.py:347
  4.9 0.2 collective-permute-start.1
  5.2 0.0 collective-permute-start.4
  5.2 0.8 %dynamic_update_slice.12 = bf16[2,2,8320]{2,1,0:T(2,128)(2,1)S(1)} pad(bf16[1,2,8192]{2,1,0:T(2,128)(2,1)} %bitcast.9, bf16[]{:T(256)} %constant.0.clone.1), padding=0_1x0_0x0_128 | pad | bytes 99330 | tf_op jit(solution)/shard_map/dynamic_update_slice | solution.py:400
  6.0 0.7 %constant_dynamic-update-slice_fusion.2 = bf16[2,2,8320]{2,1,0:T(2,128)(2,1)S(1)} fusion(bf16[2,2,8320]{2,1,0:T(2,128)(2,1)S(1)} %dynamic_update_slice.12, bf16[1,2,128]{2,1,0:T(2,128)(2,1)} %pack.1), kind=kLoop, calls=%fused_computation.2 | loop fusion | bytes 1024 | tf_op jit(solution)/shard_map/dynamic_update_slice | solution.py:401
  6.6 0.0 collective-permute-done
  6.7 2.0 %collective-permute-done.1 = bf16[1,2,128]{2,1,0:T(2,128)(2,1)S(1)} collective-permute-done((bf16[1,2,128]{2,1,0:T(2,128)(2,1)}, bf16[1,2,128]{2,1,0:T(2,128)(2,1)S(1)}, u32[]{:S(2)}, u32[]{:S(2)}) %collective-permute-start.1) | collective-permute-done | bytes 544 | tf_op jit(solution)/shard_map/ppermute | solution.py:345
  8.7 1.6 %collective-permute-start.5 = (bf16[2,2,8320]{2,1,0:T(2,128)(2,1)S(1)}, bf16[2,2,8320]{2,1,0:T(2,128)(2,1)S(1)}, u32[]{:S(2)}, u32[]{:S(2)}) collective-permute-start(bf16[2,2,8320]{2,1,0:T(2,128)(2,1)S(1)} %constant_dynamic-update-slice_fusion.refs_0_), channel_id=1, source_target_pairs={{0,4},{1,5},{2,6},{3,7},{4,0},{5,1},{6,2},{7,3},{8,12},{9,13},{10,... | collective-permute-start | bytes 199688 | tf_op jit(solution)/shard_map/ppermute | solution.py:345
  10.3 2.5 %collective-permute-start.3 = (bf16[2,2,8320]{2,1,0:T(2,128)(2,1)S(1)}, bf16[2,2,8320]{2,1,0:T(2,128)(2,1)S(1)}, u32[]{:S(2)}, u32[]{:S(2)}) collective-permute-start(bf16[2,2,8320]{2,1,0:T(2,128)(2,1)S(1)} %constant_dynamic-update-slice_fusion.refs_0_), channel_id=1, source_target_pairs={{0,12},{1,13},{2,14},{3,15},{4,8},{5,9},{6,10},{7,11},{8,4},{9,5},... | collective-permute-start | bytes 199688 | tf_op jit(solution)/shard_map/ppermute | solution.py:345
  12.7 0.1 collective-permute-start.2
  12.9 0.0 copy-start.1
  12.9 0.9 %copy-done.1 = f32[16,4096]{1,0:T(8,128)S(1)} copy-done((f32[16,4096]{1,0:T(8,128)S(1)}, f32[16,4096]{1,0:T(8,128)}, u32[]{:S(2)}) %copy-start.1) | copy-done | bytes 262168
  13.8 0.0 copy-start.2
  13.8 0.9 %copy-done.2 = f32[16,4096]{1,0:T(8,128)S(1)} copy-done((f32[16,4096]{1,0:T(8,128)S(1)}, f32[16,4096]{1,0:T(8,128)}, u32[]{:S(2)}) %copy-start.2) | copy-done | bytes 262168
  14.8 0.1 tables.1.refs_5_
  14.9 0.0 collective-permute-done.4.other_ref
  14.9 0.0 copy-done
  14.9 0.3 power.1
  15.3 0.0 collective-permute-done.5.refs_1_
  15.3 1.5 %scores.2 = (bf16[72,8192]{1,0:T(8,128)(2,1)S(1)}, f32[1,32,72]{2,1,0:T(8,128)S(1)}, f32[1,32,72]{2,1,0:T(8,128)S(1)}, f32[1,1,128]{2,1,0:T(1,128)S(1)}) custom-call(bf16[2,2,8320]{2,1,0:T(2,128)(2,1)S(1)} %constant_dynamic-update-slice_fusion.refs_0_, bf16[2,2,8320]{2,1,0:T(2,128)(2,1)S(1)} %collective-permute-done.5.refs_1_, ...), custom_call_target="tpu_custom_call" | custom-call | flops 84934656 | bytes 1179648 | tf_op jit(solution)/shard_map/scores/pallas_call | solution.py:419
  16.8 0.0 collective-permute-done.3.refs_1_
  16.8 1.8 %collective-permute-done.2.refs_0_ = bf16[2,2,8320]{2,1,0:T(2,128)(2,1)S(1)} collective-permute-done((bf16[2,2,8320]{2,1,0:T(2,128)(2,1)S(1)}, bf16[2,2,8320]{2,1,0:T(2,128)(2,1)S(1)}, u32[]{:S(2)}, u32[]{:S(2)}) %collective-permute-start.2) | collective-permute-done | bytes 66592 | tf_op jit(solution)/shard_map/ppermute | solution.py:345
  18.7 1.6 %scores.3 = (bf16[72,8192]{1,0:T(8,128)(2,1)S(1)}, f32[2,32,72]{2,1,0:T(8,128)S(1)}, f32[2,32,72]{2,1,0:T(8,128)S(1)}, f32[16,1,128]{2,1,0:T(1,128)S(1)}) custom-call(bf16[2,2,8320]{2,1,0:T(2,128)(2,1)S(1)} %collective-permute-done.2.refs_0_, bf16[2,2,8320]{2,1,0:T(2,128)(2,1)S(1)} %collective-permute-done.3.refs_1_, ...), custom_call_target="tpu_custom_call" | custom-call | flops 84934656 | bytes 1179648 | tf_op jit(solution)/shard_map/scores/pallas_call | solution.py:419
  20.2 0.1 collective-permute-start.8
  20.3 0.5 %collective-permute-start.7 = (bf16[72,8192]{1,0:T(8,128)(2,1)S(1)}, bf16[72,8192]{1,0:T(8,128)(2,1)S(1)}, u32[]{:S(2)}, u32[]{:S(2)}) collective-permute-start(bf16[72,8192]{1,0:T(8,128)(2,1)S(1)} %get-tuple-element.30.refs_3_), channel_id=1, source_target_pairs={{0,1},{1,0},{2,3},{3,2},{4,5},{5,4},{6,7},{7,6},{8,9},{9,8},{10,11... | collective-permute-start | bytes 3538952 | tf_op jit(solution)/shard_map/ppermute | solution.py:345
  20.8 0.1 collective-permute-start.6
  20.9 10.7 %all_to_all.5 = f32[16,1,128]{2,1,0:T(1,128)S(1)} all-to-all(f32[16,1,128]{2,1,0:T(1,128)S(1)} %get-tuple-element.27), channel_id=1, replica_groups=mesh['groups'=2,'blk'=16] {'blk'}, dimensions={0} | all-to-all | bytes 16384 | tf_op jit(solution)/shard_map/all_to_all | solution.py:451
  31.6 0.0 collective-permute-done.6.refs_2_
  31.6 0.0 collective-permute-done.8.refs_6_
  31.6 0.0 collective-permute-done.7.refs_5_
  31.6 1.8 %slices.1 = (f32[32,8192]{1,0:T(8,128)}, f32[2]{0:T(128)}, f32[2]{0:T(128)}) custom-call(f32[8,2,1,128]{3,2,1,0:T(1,128)S(1)} %bitcast.7, f32[2,32,72]{2,1,0:T(8,128)S(1)} %get-tuple-element.28.refs_1_, f32[2,32,72]{2,1,0:T(8,128)S(1)} %collective-permute-done.6.refs_2_, bf16[72,8192]{1,0:T(8,128)(2,1)S(1)} %get-tuple-element.30.refs_3_, ...), custom_call_target="tpu_custom_call" | custom-call | tf_op jit(solution)/shard_map/slices/pallas_call | solution.py:454
  (2 shorter events, 0.0 us)
Async XLA Ops:
  0.6 14.3 %copy-start = (bf16[2,16,8192]{2,1,0:T(8,128)(2,1)S(1)}, bf16[2,16,8192]{2,1,0:T(8,128)(2,1)}, u32[]{:S(2)}) copy-start(bf16[2,16,8192]{2,1,0:T(8,128)(2,1)} %param.7) | copy-start | bytes 1572868
  0.6 6.0 %collective-permute-start = (bf16[1,2,8192]{2,1,0:T(2,128)(2,1)}, bf16[1,2,8192]{2,1,0:T(2,128)(2,1)S(1)}, u32[]{:S(2)}, u32[]{:S(2)}) collective-permute-start(bf16[1,2,8192]{2,1,0:T(2,128)(2,1)} %bitcast.8), channel_id=1, source_target_pairs={{0,2},{1,3},{2,0},{3,1},{4,6},{5,7},{6,4},{7,5},{8,10},{9,11},{10,... | collective-permute-start | bytes 98312 | tf_op jit(solution)/shard_map/ppermute | solution.py:345
  4.9 3.7 %collective-permute-start.1 = (bf16[1,2,128]{2,1,0:T(2,128)(2,1)}, bf16[1,2,128]{2,1,0:T(2,128)(2,1)S(1)}, u32[]{:S(2)}, u32[]{:S(2)}) collective-permute-start(bf16[1,2,128]{2,1,0:T(2,128)(2,1)} %pack.1), channel_id=1, source_target_pairs={{0,2},{1,3},{2,0},{3,1},{4,6},{5,7},{6,4},{7,5},{8,10},{9,11},{10,... | collective-permute-start | bytes 1544 | tf_op jit(solution)/shard_map/ppermute | solution.py:345
  5.2 9.7 %collective-permute-start.4 = (bf16[32,8192]{1,0:T(8,128)(2,1)}, bf16[32,8192]{1,0:T(8,128)(2,1)S(1)}, u32[]{:S(2)}, u32[]{:S(2)}) collective-permute-start(bf16[32,8192]{1,0:T(8,128)(2,1)} %bitcast.5), channel_id=1, source_target_pairs={{0,1},{1,0},{2,3},{3,2},{4,5},{5,4},{6,7},{7,6},{8,9},{9,8},{10,11... | collective-permute-start | bytes 1572872 | tf_op jit(solution)/shard_map/ppermute | solution.py:345
  8.7 6.6 %collective-permute-start.5 = (bf16[2,2,8320]{2,1,0:T(2,128)(2,1)S(1)}, bf16[2,2,8320]{2,1,0:T(2,128)(2,1)S(1)}, u32[]{:S(2)}, u32[]{:S(2)}) collective-permute-start(bf16[2,2,8320]{2,1,0:T(2,128)(2,1)S(1)} %constant_dynamic-update-slice_fusion.refs_0_), channel_id=1, source_target_pairs={{0,4},{1,5},{2,6},{3,7},{4,0},{5,1},{6,2},{7,3},{8,12},{9,13},{10,... | collective-permute-start | bytes 199688 | tf_op jit(solution)/shard_map/ppermute | solution.py:345
  10.3 6.6 %collective-permute-start.3 = (bf16[2,2,8320]{2,1,0:T(2,128)(2,1)S(1)}, bf16[2,2,8320]{2,1,0:T(2,128)(2,1)S(1)}, u32[]{:S(2)}, u32[]{:S(2)}) collective-permute-start(bf16[2,2,8320]{2,1,0:T(2,128)(2,1)S(1)} %constant_dynamic-update-slice_fusion.refs_0_), channel_id=1, source_target_pairs={{0,12},{1,13},{2,14},{3,15},{4,8},{5,9},{6,10},{7,11},{8,4},{9,5},... | collective-permute-start | bytes 199688 | tf_op jit(solution)/shard_map/ppermute | solution.py:345
  12.7 5.9 %collective-permute-start.2 = (bf16[2,2,8320]{2,1,0:T(2,128)(2,1)S(1)}, bf16[2,2,8320]{2,1,0:T(2,128)(2,1)S(1)}, u32[]{:S(2)}, u32[]{:S(2)}) collective-permute-start(bf16[2,2,8320]{2,1,0:T(2,128)(2,1)S(1)} %constant_dynamic-update-slice_fusion.refs_0_), channel_id=1, source_target_pairs={{0,8},{1,9},{2,10},{3,11},{4,12},{5,13},{6,14},{7,15},{8,0},{9,1},... | collective-permute-start | bytes 199688 | tf_op jit(solution)/shard_map/ppermute | solution.py:345
  12.9 0.9 %copy-start.1 = (f32[16,4096]{1,0:T(8,128)S(1)}, f32[16,4096]{1,0:T(8,128)}, u32[]{:S(2)}) copy-start(f32[16,4096]{1,0:T(8,128)} %ctf_ref.1) | copy-start | bytes 786436
  13.8 0.9 %copy-start.2 = (f32[16,4096]{1,0:T(8,128)S(1)}, f32[16,4096]{1,0:T(8,128)}, u32[]{:S(2)}) copy-start(f32[16,4096]{1,0:T(8,128)} %noise_ref.1) | copy-start | bytes 786436
  20.2 11.3 %collective-permute-start.8 = (bf16[72,8192]{1,0:T(8,128)(2,1)S(1)}, bf16[72,8192]{1,0:T(8,128)(2,1)S(1)}, u32[]{:S(2)}, u32[]{:S(2)}) collective-permute-start(bf16[72,8192]{1,0:T(8,128)(2,1)S(1)} %get-tuple-element.31.refs_4_), channel_id=1, source_target_pairs={{0,1},{1,0},{2,3},{3,2},{4,5},{5,4},{6,7},{7,6},{8,9},{9,8},{10,11... | collective-permute-start | bytes 3538952 | tf_op jit(solution)/shard_map/ppermute | solution.py:345
  20.3 11.3 %collective-permute-start.7 = (bf16[72,8192]{1,0:T(8,128)(2,1)S(1)}, bf16[72,8192]{1,0:T(8,128)(2,1)S(1)}, u32[]{:S(2)}, u32[]{:S(2)}) collective-permute-start(bf16[72,8192]{1,0:T(8,128)(2,1)S(1)} %get-tuple-element.30.refs_3_), channel_id=1, source_target_pairs={{0,1},{1,0},{2,3},{3,2},{4,5},{5,4},{6,7},{7,6},{8,9},{9,8},{10,11... | collective-permute-start | bytes 3538952 | tf_op jit(solution)/shard_map/ppermute | solution.py:345
  20.8 10.8 %collective-permute-start.6 = (f32[2,32,72]{2,1,0:T(8,128)S(1)}, f32[2,32,72]{2,1,0:T(8,128)S(1)}, u32[]{:S(2)}, u32[]{:S(2)}) collective-permute-start(f32[2,32,72]{2,1,0:T(8,128)S(1)} %get-tuple-element.29), channel_id=1, source_target_pairs={{0,1},{1,0},{2,3},{3,2},{4,5},{5,4},{6,7},{7,6},{8,9},{9,8},{10,11... | collective-permute-start | bytes 55304 | tf_op jit(solution)/shard_map/ppermute | solution.py:345

commit v11 on v9

--- a/solution.py
+++ b/solution.py
@@ -110,8 +110,8 @@
     both_ref, high_ref, low_ref, table_ref = refs[:4]
     refs = refs[4:]
     if has_earlier:
-        earlier_own_ref, earlier_other_ref, earlier_stats_ref = refs[:3]
-        refs = refs[3:]
+        _, earlier_own_ref, earlier_other_ref, earlier_stats_ref = refs[:4]
+        refs = refs[4:]
     weighted_ref, exps_ref, *exps_other_refs, stats_ref = refs[:-5]
     image_ref, real_ref, imag_ref, cross_ref, square_ref = refs[-5:]
     full = both_ref.shape[1]
@@ -147,7 +147,7 @@
 
     def block(index, carry):
         rows = pl.ds(pl.multiple_of(index * ROWS, ROWS), ROWS)
-        first = pl.multiple_of(index * block_rows, ROWS)
+        first = pl.multiple_of((index + slot) * block_rows, ROWS)
         numbers = image_ref[rows, full:]
         column = lax.broadcasted_iota(jnp.int32, (ROWS, 3 * groups), 1) % groups
         one_hot = (numbers[:, :1].astype(jnp.int32) == column).astype(jnp.bfloat16)
@@ -391,7 +391,7 @@
     flat = projections.reshape(own_rows, full)
     other = swap(flat, 1)
     if by_distance:
-        rows, numbers = lax.optimization_barrier((rows, numbers))
+        rows, numbers, other = lax.optimization_barrier((rows, numbers, other))
         received_numbers = swap(numbers, 2)
     groups = ctf_table.shape[0]
     both, high, low = pl.pallas_call(
@@ -435,18 +435,17 @@
         )
         parts = [([gathered], (tuple(range(chips)),))]
 
-    all_weighted = []
     earlier = ()
-    for pieces, sources in parts:
-        last = len(all_weighted) == len(parts) - 1
+    for number, (pieces, sources) in enumerate(parts):
+        last = number == len(parts) - 1
         own_blocks = blocks // len(parts)
         seen = blocks if last else own_blocks
         exps_shape = jax.ShapeDtypeStruct((seen, own_rows, block_rows), jnp.float32)
-        weighted, *earlier = pl.pallas_call(
+        earlier = pl.pallas_call(
             functools.partial(score_kernel, sources, by_distance, shifts, bool(earlier)),
             out_shape=(
                 jax.ShapeDtypeStruct(
-                    (own_blocks * block_rows, full + (3 * blocks * LANES if earlier else 0)),
+                    (blocks * block_rows, full + (3 * blocks * LANES if by_distance else 0)),
                     jnp.bfloat16,
                 ),
                 *([exps_shape] if earlier else [exps_shape] * 2),
@@ -463,6 +462,7 @@
                 pltpu.VMEM((block_rows, candidates), jnp.float32),
                 pltpu.VMEM((-(-block_rows // LANES) * LANES, LANES), jnp.float32),
             ],
+            input_output_aliases={len(pieces) + 4: 0} if earlier else {},
             compiler_params=params,
             cost_estimate=pl.CostEstimate(
                 flops=2 * own_blocks * block_rows * full * (candidates + 8),
@@ -471,10 +471,10 @@
             ),
             name="scores",
         )(*pieces, both, high, low, tables, *earlier)
-        all_weighted.append(weighted)
-    exps, *exps_other, stats = earlier
-
-    exchanged = [swap(weighted, 1) for weighted in all_weighted]
+    weighted, exps, *exps_other, stats = earlier
+
+    all_weighted = [weighted]
+    exchanged = [swap(weighted, 1)]
     exps_in = [swap(part, 1) for part in exps_other]
     gathered = lax.all_to_all(stats, "blk", 0, 0)
     gathered = gathered.reshape((chips, 2) + gathered.shape[1:])

time: 33.5 us -> 32.6 us (0.973)
  waiting for transfers between devices: 3.85 us -> 2.41 us
  local copies, waits for them, and re-layouts: 3.41 us -> 4.44 us
  blocking collectives: 10.6 us -> 10.1 us
    ppermute x8 -> x7, waiting for transfers between devices: 3.85 us -> 2.41 us  [swap(): return lax.ppermute(value, 'blk', [(i, i ^ mask) for i in range(axis_size)])]
    unnamed x6, local copies, waits for them, and re-layouts: 1.91 us -> 2.94 us
    all_to_all x1, blocking collectives: 10.6 us -> 10.1 us  [local(): gathered = lax.all_to_all(stats, 'blk', 0, 0)]
    ppermute x8 -> x7, starting transfers between devices: 7.98 us -> 8.11 us  [swap(): return lax.ppermute(value, 'blk', [(i, i ^ mask) for i in range(axis_size)])]
  transfers between devices with their start and end apart: 8 -> 7, of which waited for: 2 -> 2; matrix products, arithmetic and copies ran while one was open for 5% -> 5% of each run, Pallas kernels for 10% -> 10%
where the time goes in v11:
time: 32.6 us; the launch traced here: 32.3 us
  blocking collectives  10.1 us (31%)
  starting transfers between devices  8.11 us (25%)
  Pallas kernels  6.44 us (20%)
  local copies, waits for them, and re-layouts  4.44 us (14%)
  waiting for transfers between devices  2.41 us (7%)
  between operations  0.71 us (2%)
    all_to_all x1, blocking collectives, local(): gathered = lax.all_to_all(stats, 'blk', 0, 0)  10.1 us
    ppermute x7, starting transfers between devices, swap(): return lax.ppermute(value, 'blk', [(i, i ^ mask) for i in range(axis_size)])  8.11 us
    unnamed x6, local copies, waits for them, and re-layouts  2.94 us
    pallas_call x2, Pallas kernels, local(): pl.pallas_call(functools.partial(score_kernel, sources, by_distance, shif...  2.92 us
    ppermute x7, waiting for transfers between devices, swap(): return lax.ppermute(value, 'blk', [(i, i ^ mask) for i in range(axis_size)])  2.41 us
    pallas_call x1, Pallas kernels, local(): pl.pallas_call(functools.partial(slice_kernel, own_rows / per_device, len...  1.8 us
    pallas_call x1, Pallas kernels, local(): pl.pallas_call(pack_kernel, out_shape=jax.ShapeDtypeStruct((1, per_device...  1.26 us
    dynamic_update_slice x1, local copies, waits for them, and re-layouts, local(): pair = lax.dynamic_update_slice(pair, rows, (0, 0, 0))  0.8 us
  transfers between devices with their start and end apart: 7, of which 2 were waited for; matrix products, arithmetic and copies ran while one was open for 5% of the time, Pallas kernels for 10%

profile of v11, /device:TPU:0, one launch (start us, length us, event | category | flops | bytes accessed | tf_op | source)
XLA Modules:
  0.0 32.3 jit_solution(1282591841453552414)
XLA Ops:
  0.6 0.5 %collective-permute-start = (bf16[32,8192]{1,0:T(8,128)(2,1)}, bf16[32,8192]{1,0:T(8,128)(2,1)S(1)}, u32[]{:S(2)}, u32[]{:S(2)}) collective-permute-start(bf16[32,8192]{1,0:T(8,128)(2,1)} %bitcast.5), channel_id=1, source_target_pairs={{0,1},{1,0},{2,3},{3,2},{4,5},{5,4},{6,7},{7,6},{8,9},{9,8},{10,11... | collective-permute-start | bytes 1572872 | tf_op jit(solution)/shard_map/ppermute | solution.py:370
  1.1 2.6 %collective-permute-start.1 = (bf16[1,2,8192]{2,1,0:T(2,128)(2,1)}, bf16[1,2,8192]{2,1,0:T(2,128)(2,1)S(1)}, u32[]{:S(2)}, u32[]{:S(2)}) collective-permute-start(bf16[1,2,8192]{2,1,0:T(2,128)(2,1)} %bitcast.8), channel_id=1, source_target_pairs={{0,2},{1,3},{2,0},{3,1},{4,6},{5,7},{6,4},{7,5},{8,10},{9,11},{10,... | collective-permute-start | bytes 98312 | tf_op jit(solution)/shard_map/ppermute | solution.py:370
  3.7 1.3 %pack.1 = bf16[1,2,128]{2,1,0:T(2,128)(2,1)} custom-call(s32[2]{0:T(128)} %group_hbm.1, s32[2]{0:T(128)} %limit_hbm.1, s32[2,2,9]{2,1,0:T(2,128)} %bitcast.10), custom_call_target="tpu_custom_call" | custom-call | tf_op jit(solution)/shard_map/pack/pallas_call | solution.py:372
  5.0 0.0 collective-permute-done.other_ref
  5.0 0.8 %collective-permute-start.2 = (bf16[1,2,128]{2,1,0:T(2,128)(2,1)}, bf16[1,2,128]{2,1,0:T(2,128)(2,1)S(1)}, u32[]{:S(2)}, u32[]{:S(2)}) collective-permute-start(bf16[1,2,128]{2,1,0:T(2,128)(2,1)} %pack.1), channel_id=1, source_target_pairs={{0,2},{1,3},{2,0},{3,1},{4,6},{5,7},{6,4},{7,5},{8,10},{9,11},{10,... | collective-permute-start | bytes 1544 | tf_op jit(solution)/shard_map/ppermute | solution.py:370
  5.8 0.8 %dynamic_update_slice.12 = bf16[2,2,8320]{2,1,0:T(2,128)(2,1)S(1)} pad(bf16[1,2,8192]{2,1,0:T(2,128)(2,1)} %bitcast.9, bf16[]{:T(256)} %constant.0.clone.1), padding=0_1x0_0x0_128 | pad | bytes 99330 | tf_op jit(solution)/shard_map/dynamic_update_slice | solution.py:425
  6.6 0.7 %constant_dynamic-update-slice_fusion.2 = bf16[2,2,8320]{2,1,0:T(2,128)(2,1)S(1)} fusion(bf16[2,2,8320]{2,1,0:T(2,128)(2,1)S(1)} %dynamic_update_slice.12, bf16[1,2,128]{2,1,0:T(2,128)(2,1)} %pack.1), kind=kLoop, calls=%fused_computation.2 | loop fusion | bytes 1024 | tf_op jit(solution)/shard_map/dynamic_update_slice | solution.py:426
  7.2 0.0 collective-permute-done.1
  7.3 1.5 %collective-permute-done.2 = bf16[1,2,128]{2,1,0:T(2,128)(2,1)S(1)} collective-permute-done((bf16[1,2,128]{2,1,0:T(2,128)(2,1)}, bf16[1,2,128]{2,1,0:T(2,128)(2,1)S(1)}, u32[]{:S(2)}, u32[]{:S(2)}) %collective-permute-start.2) | collective-permute-done | bytes 544 | tf_op jit(solution)/shard_map/ppermute | solution.py:370
  8.8 1.6 %collective-permute-start.5 = (bf16[2,2,8320]{2,1,0:T(2,128)(2,1)S(1)}, bf16[2,2,8320]{2,1,0:T(2,128)(2,1)S(1)}, u32[]{:S(2)}, u32[]{:S(2)}) collective-permute-start(bf16[2,2,8320]{2,1,0:T(2,128)(2,1)S(1)} %constant_dynamic-update-slice_fusion.refs_0_), channel_id=1, source_target_pairs={{0,4},{1,5},{2,6},{3,7},{4,0},{5,1},{6,2},{7,3},{8,12},{9,13},{10,... | collective-permute-start | bytes 199688 | tf_op jit(solution)/shard_map/ppermute | solution.py:370
  10.3 2.5 %collective-permute-start.4 = (bf16[2,2,8320]{2,1,0:T(2,128)(2,1)S(1)}, bf16[2,2,8320]{2,1,0:T(2,128)(2,1)S(1)}, u32[]{:S(2)}, u32[]{:S(2)}) collective-permute-start(bf16[2,2,8320]{2,1,0:T(2,128)(2,1)S(1)} %constant_dynamic-update-slice_fusion.refs_0_), channel_id=1, source_target_pairs={{0,12},{1,13},{2,14},{3,15},{4,8},{5,9},{6,10},{7,11},{8,4},{9,5},... | collective-permute-start | bytes 199688 | tf_op jit(solution)/shard_map/ppermute | solution.py:370
  12.8 0.1 collective-permute-start.3
  12.9 0.0 copy-start.1
  12.9 0.9 %copy-done.1 = f32[16,4096]{1,0:T(8,128)S(1)} copy-done((f32[16,4096]{1,0:T(8,128)S(1)}, f32[16,4096]{1,0:T(8,128)}, u32[]{:S(2)}) %copy-start.1) | copy-done | bytes 262168
  13.9 0.0 copy-start.2
  13.9 0.9 %copy-done.2 = f32[16,4096]{1,0:T(8,128)S(1)} copy-done((f32[16,4096]{1,0:T(8,128)S(1)}, f32[16,4096]{1,0:T(8,128)}, u32[]{:S(2)}) %copy-start.2) | copy-done | bytes 262168
  14.8 0.1 tables.1.refs_5_
  15.0 0.0 copy-start
  15.0 1.0 %copy-done = bf16[2,16,8192]{2,1,0:T(8,128)(2,1)S(1)} copy-done((bf16[2,16,8192]{2,1,0:T(8,128)(2,1)S(1)}, bf16[2,16,8192]{2,1,0:T(8,128)(2,1)}, u32[]{:S(2)}) %copy-start) | copy-done | bytes 524312
  16.0 0.3 %power.1 = (bf16[64,8192]{1,0:T(8,128)(2,1)S(1)}, bf16[64,4096]{1,0:T(8,128)(2,1)S(1)}, bf16[64,4096]{1,0:T(8,128)(2,1)S(1)}) custom-call(bf16[32,8192]{1,0:T(8,128)(2,1)S(1)} %bitcast.6, bf16[32,8192]{1,0:T(8,128)(2,1)S(1)} %collective-permute-done.other_ref), custom_call_target="tpu_custom_call" | custom-call | flops 4194304 | bytes 2097152 | tf_op jit(solution)/shard_map/power/pallas_call | solution.py:397
  16.4 0.0 collective-permute-done.5.refs_1_
  16.4 1.4 %scores.2 = (bf16[144,8960]{1,0:T(8,128)(2,1)S(1)}, f32[1,32,72]{2,1,0:T(8,128)S(1)}, f32[1,32,72]{2,1,0:T(8,128)S(1)}, f32[1,1,128]{2,1,0:T(1,128)S(1)}) custom-call(bf16[2,2,8320]{2,1,0:T(2,128)(2,1)S(1)} %constant_dynamic-update-slice_fusion.refs_0_, bf16[2,2,8320]{2,1,0:T(2,128)(2,1)S(1)} %collective-permute-done.5.refs_1_, ...), custom_call_target="tpu_custom_call" | custom-call | flops 84934656 | bytes 1179648 | tf_op jit(solution)/shard_map/scores/pallas_call | solution.py:444
  17.8 0.0 collective-permute-done.4.refs_1_
  17.8 0.9 %collective-permute-done.3.refs_0_ = bf16[2,2,8320]{2,1,0:T(2,128)(2,1)S(1)} collective-permute-done((bf16[2,2,8320]{2,1,0:T(2,128)(2,1)S(1)}, bf16[2,2,8320]{2,1,0:T(2,128)(2,1)S(1)}, u32[]{:S(2)}, u32[]{:S(2)}) %collective-permute-start.3) | collective-permute-done | bytes 66592 | tf_op jit(solution)/shard_map/ppermute | solution.py:370
  18.8 1.5 %scores.3 = (bf16[144,8960]{1,0:T(8,128)(2,1)S(1)}, f32[2,32,72]{2,1,0:T(8,128)S(1)}, f32[16,1,128]{2,1,0:T(1,128)S(1)}) custom-call(bf16[2,2,8320]{2,1,0:T(2,128)(2,1)S(1)} %collective-permute-done.3.refs_0_, bf16[2,2,8320]{2,1,0:T(2,128)(2,1)S(1)} %collective-permute-done.4.refs_1_, ...), custom_call_target="tpu_custom_call", output_to_operand_aliasing={{0}: (6, {})} | custom-call | flops 84934656 | bytes 1179648 | tf_op jit(solution)/shard_map/scores/pallas_call | solution.py:444
  20.2 0.1 collective-permute-start.6
  20.3 10.1 %all_to_all.5 = f32[16,1,128]{2,1,0:T(1,128)S(1)} all-to-all(f32[16,1,128]{2,1,0:T(1,128)S(1)} %get-tuple-element.29), channel_id=1, replica_groups=mesh['groups'=2,'blk'=16] {'blk'}, dimensions={0} | all-to-all | bytes 16384 | tf_op jit(solution)/shard_map/all_to_all | solution.py:479
  30.5 0.0 collective-permute-done.6.refs_3_
  30.5 1.8 %slices.1 = (f32[32,8192]{1,0:T(8,128)}, f32[2]{0:T(128)}, f32[2]{0:T(128)}) custom-call(f32[8,2,1,128]{3,2,1,0:T(1,128)S(1)} %bitcast.7, f32[2,32,72]{2,1,0:T(8,128)S(1)} %get-tuple-element.30.refs_1_, bf16[144,8960]{1,0:T(8,128)(2,1)S(1)} %get-tuple-element.31.refs_2_, bf16[144,8960]{1,0:T(8,128)(2,1)S(1)} %collective-permute-done.6.refs_3_), custom_call_target="tpu_custom_call" | custom-call | tf_op jit(solution)/shard_map/slices/pallas_call | solution.py:482
  (2 shorter events, 0.0 us)
Async XLA Ops:
  0.6 4.4 %collective-permute-start = (bf16[32,8192]{1,0:T(8,128)(2,1)}, bf16[32,8192]{1,0:T(8,128)(2,1)S(1)}, u32[]{:S(2)}, u32[]{:S(2)}) collective-permute-start(bf16[32,8192]{1,0:T(8,128)(2,1)} %bitcast.5), channel_id=1, source_target_pairs={{0,1},{1,0},{2,3},{3,2},{4,5},{5,4},{6,7},{7,6},{8,9},{9,8},{10,11... | collective-permute-start | bytes 1572872 | tf_op jit(solution)/shard_map/ppermute | solution.py:370
  1.1 6.1 %collective-permute-start.1 = (bf16[1,2,8192]{2,1,0:T(2,128)(2,1)}, bf16[1,2,8192]{2,1,0:T(2,128)(2,1)S(1)}, u32[]{:S(2)}, u32[]{:S(2)}) collective-permute-start(bf16[1,2,8192]{2,1,0:T(2,128)(2,1)} %bitcast.8), channel_id=1, source_target_pairs={{0,2},{1,3},{2,0},{3,1},{4,6},{5,7},{6,4},{7,5},{8,10},{9,11},{10,... | collective-permute-start | bytes 98312 | tf_op jit(solution)/shard_map/ppermute | solution.py:370
  5.0 3.7 %collective-permute-start.2 = (bf16[1,2,128]{2,1,0:T(2,128)(2,1)}, bf16[1,2,128]{2,1,0:T(2,128)(2,1)S(1)}, u32[]{:S(2)}, u32[]{:S(2)}) collective-permute-start(bf16[1,2,128]{2,1,0:T(2,128)(2,1)} %pack.1), channel_id=1, source_target_pairs={{0,2},{1,3},{2,0},{3,1},{4,6},{5,7},{6,4},{7,5},{8,10},{9,11},{10,... | collective-permute-start | bytes 1544 | tf_op jit(solution)/shard_map/ppermute | solution.py:370
  8.8 7.6 %collective-permute-start.5 = (bf16[2,2,8320]{2,1,0:T(2,128)(2,1)S(1)}, bf16[2,2,8320]{2,1,0:T(2,128)(2,1)S(1)}, u32[]{:S(2)}, u32[]{:S(2)}) collective-permute-start(bf16[2,2,8320]{2,1,0:T(2,128)(2,1)S(1)} %constant_dynamic-update-slice_fusion.refs_0_), channel_id=1, source_target_pairs={{0,4},{1,5},{2,6},{3,7},{4,0},{5,1},{6,2},{7,3},{8,12},{9,13},{10,... | collective-permute-start | bytes 199688 | tf_op jit(solution)/shard_map/ppermute | solution.py:370
  10.3 7.5 %collective-permute-start.4 = (bf16[2,2,8320]{2,1,0:T(2,128)(2,1)S(1)}, bf16[2,2,8320]{2,1,0:T(2,128)(2,1)S(1)}, u32[]{:S(2)}, u32[]{:S(2)}) collective-permute-start(bf16[2,2,8320]{2,1,0:T(2,128)(2,1)S(1)} %constant_dynamic-update-slice_fusion.refs_0_), channel_id=1, source_target_pairs={{0,12},{1,13},{2,14},{3,15},{4,8},{5,9},{6,10},{7,11},{8,4},{9,5},... | collective-permute-start | bytes 199688 | tf_op jit(solution)/shard_map/ppermute | solution.py:370
  12.8 5.9 %collective-permute-start.3 = (bf16[2,2,8320]{2,1,0:T(2,128)(2,1)S(1)}, bf16[2,2,8320]{2,1,0:T(2,128)(2,1)S(1)}, u32[]{:S(2)}, u32[]{:S(2)}) collective-permute-start(bf16[2,2,8320]{2,1,0:T(2,128)(2,1)S(1)} %constant_dynamic-update-slice_fusion.refs_0_), channel_id=1, source_target_pairs={{0,8},{1,9},{2,10},{3,11},{4,12},{5,13},{6,14},{7,15},{8,0},{9,1},... | collective-permute-start | bytes 199688 | tf_op jit(solution)/shard_map/ppermute | solution.py:370
  12.9 0.9 %copy-start.1 = (f32[16,4096]{1,0:T(8,128)S(1)}, f32[16,4096]{1,0:T(8,128)}, u32[]{:S(2)}) copy-start(f32[16,4096]{1,0:T(8,128)} %ctf_ref.1) | copy-start | bytes 786436
  13.9 0.9 %copy-start.2 = (f32[16,4096]{1,0:T(8,128)S(1)}, f32[16,4096]{1,0:T(8,128)}, u32[]{:S(2)}) copy-start(f32[16,4096]{1,0:T(8,128)} %noise_ref.1) | copy-start | bytes 786436
  15.0 1.0 %copy-start = (bf16[2,16,8192]{2,1,0:T(8,128)(2,1)S(1)}, bf16[2,16,8192]{2,1,0:T(8,128)(2,1)}, u32[]{:S(2)}) copy-start(bf16[2,16,8192]{2,1,0:T(8,128)(2,1)} %param.7) | copy-start | bytes 1572868
  20.2 10.2 %collective-permute-start.6 = (bf16[144,8960]{1,0:T(8,128)(2,1)S(1)}, bf16[144,8960]{1,0:T(8,128)(2,1)S(1)}, u32[]{:S(2)}, u32[]{:S(2)}) collective-permute-start(bf16[144,8960]{1,0:T(8,128)(2,1)S(1)} %get-tuple-element.31.refs_2_), channel_id=1, source_target_pairs={{0,1},{1,0},{2,3},{3,2},{4,5},{5,4},{6,7},{7,6},{8,9},{9,8},{10,11... | collective-permute-start | bytes 7741448 | tf_op jit(solution)/shard_map/ppermute | solution.py:370

commit v12 on v11

--- a/solution.py
+++ b/solution.py
@@ -97,18 +97,17 @@
         low_ref[at, :] = low
 
 
-def table_kernel(ctf_ref, noise_ref, table_ref):
-    groups, half = ctf_ref.shape
-    for place, ref in enumerate((ctf_ref, noise_ref)):
-        for third, part in enumerate(split_thirds(ref[...])):
-            table_ref[pl.ds(third * groups, groups), pl.ds(place * half, half)] = part
+def table_kernel(values_ref, table_ref):
+    groups = values_ref.shape[0]
+    for third, part in enumerate(split_thirds(values_ref[...])):
+        table_ref[pl.ds(third * groups, groups), :] = part
 
 
 def score_kernel(sources, by_distance, shifts, has_earlier, *refs):
     pieces = refs[: len(sources)]
     refs = refs[len(sources) :]
-    both_ref, high_ref, low_ref, table_ref = refs[:4]
-    refs = refs[4:]
+    both_ref, high_ref, low_ref, ctf_ref, noise_ref = refs[:5]
+    refs = refs[5:]
     if has_earlier:
         _, earlier_own_ref, earlier_other_ref, earlier_stats_ref = refs[:4]
         refs = refs[4:]
@@ -116,7 +115,7 @@
     image_ref, real_ref, imag_ref, cross_ref, square_ref = refs[-5:]
     full = both_ref.shape[1]
     half = full // 2
-    groups = table_ref.shape[0] // 3
+    groups = ctf_ref.shape[0] // 3
     candidates = both_ref.shape[0]
     rows_total = image_ref.shape[0]
 
@@ -151,9 +150,8 @@
         numbers = image_ref[rows, full:]
         column = lax.broadcasted_iota(jnp.int32, (ROWS, 3 * groups), 1) % groups
         one_hot = (numbers[:, :1].astype(jnp.int32) == column).astype(jnp.bfloat16)
-        tables = jnp.dot(one_hot, table_ref[...], preferred_element_type=jnp.float32)
-        ctf = tables[:, :half]
-        noise = tables[:, half:]
+        ctf = jnp.dot(one_hot, ctf_ref[...], preferred_element_type=jnp.float32)
+        noise = jnp.dot(one_hot, noise_ref[...], preferred_element_type=jnp.float32)
         limit = numbers[:, LIMIT_AT : LIMIT_AT + 1].astype(jnp.int32)
         position = lax.broadcasted_iota(jnp.int32, (ROWS, half), 1)
         freq_x = position >> int(math.log2(KY))
@@ -409,27 +407,36 @@
         ),
         name="power",
     )(flat, other)
-    tables = pl.pallas_call(
-        table_kernel,
-        out_shape=jax.ShapeDtypeStruct((3 * groups, full), jnp.bfloat16),
-        in_specs=[VMEM] * 2,
-        out_specs=VMEM,
-        compiler_params=params,
-        cost_estimate=pl.CostEstimate(
-            flops=6 * groups * full, bytes_accessed=10 * groups * full, transcendentals=0
-        ),
-        name="tables",
-    )(ctf_table, noise_weight)
+    def in_thirds(values, name):
+        return pl.pallas_call(
+            table_kernel,
+            out_shape=jax.ShapeDtypeStruct((3 * groups, half), jnp.bfloat16),
+            in_specs=[VMEM],
+            out_specs=VMEM,
+            compiler_params=params,
+            cost_estimate=pl.CostEstimate(
+                flops=6 * groups * half, bytes_accessed=10 * groups * half, transcendentals=0
+            ),
+            name=name,
+        )(values)
+
+    noise_thirds = in_thirds(noise_weight, "noise")
     if by_distance:
         pair = jnp.zeros((2, per_device, full + LANES), images.dtype)
         pair = lax.dynamic_update_slice(pair, rows, (0, 0, 0))
         pair = lax.dynamic_update_slice(pair, numbers, (0, 0, full))
+        pair, ctf_late = lax.optimization_barrier((pair, ctf_table))
+        ctf_thirds = in_thirds(ctf_late, "ctf")
         pair = lax.dynamic_update_slice(pair, received, (1, 0, 0))
+        received_numbers, ctf_thirds = lax.optimization_barrier(
+            (received_numbers, ctf_thirds)
+        )
         pair = lax.dynamic_update_slice(pair, received_numbers, (1, 0, full))
         pieces = [pair] + [swap(pair, mask) for mask in range(4, axis_size, 4)]
         parts = [(pieces[:2], ((0, 1), (2, 3))), (pieces[2:], ((4, 5), (6, 7)))]
     else:
         same_core = [[2 * c + core for c in range(chips)] for core in range(2)]
+        ctf_thirds = in_thirds(ctf_table, "ctf")
         gathered = lax.all_gather(
             jnp.concatenate([rows, numbers], axis=2), "blk", axis=0, tiled=True, axis_index_groups=same_core
         )
@@ -453,7 +460,7 @@
                     (axis_size if last else 1, 1 if by_distance else blocks, LANES), jnp.float32
                 ),
             ),
-            in_specs=[VMEM] * (len(pieces) + 4 + len(earlier)),
+            in_specs=[VMEM] * (len(pieces) + 5 + len(earlier)),
             out_specs=(VMEM,) * (3 if earlier else 4),
             scratch_shapes=[
                 pltpu.VMEM((own_blocks * ROWS, full + LANES), jnp.float32),
@@ -462,7 +469,7 @@
                 pltpu.VMEM((block_rows, candidates), jnp.float32),
                 pltpu.VMEM((-(-block_rows // LANES) * LANES, LANES), jnp.float32),
             ],
-            input_output_aliases={len(pieces) + 4: 0} if earlier else {},
+            input_output_aliases={len(pieces) + 5: 0} if earlier else {},
             compiler_params=params,
             cost_estimate=pl.CostEstimate(
                 flops=2 * own_blocks * block_rows * full * (candidates + 8),
@@ -470,7 +477,7 @@
                 transcendentals=0,
             ),
             name="scores",
-        )(*pieces, both, high, low, tables, *earlier)
+        )(*pieces, both, high, low, ctf_thirds, noise_thirds, *earlier)
     weighted, exps, *exps_other, stats = earlier
 
     all_weighted = [weighted]

time: 32.6 us -> 33.6 us (1.031)
  blocking collectives: 10.1 us -> 10.8 us
    all_to_all x1, blocking collectives: 10.1 us -> 10.8 us  [local(): gathered = lax.all_to_all(stats, 'blk', 0, 0)]
  transfers between devices with their start and end apart: 7 -> 7, of which waited for: 2 -> 3; matrix products, arithmetic and copies ran while one was open for 5% -> 5% of each run, Pallas kernels for 10% -> 10%
where the time goes in v12:
time: 33.6 us; the launch traced here: 33.2 us
  blocking collectives  10.8 us (32%)
  starting transfers between devices  8.11 us (24%)
  Pallas kernels  6.42 us (19%)
  local copies, waits for them, and re-layouts  4.43 us (13%)
  waiting for transfers between devices  2.69 us (8%)
  between operations  0.71 us (2%)
    all_to_all x1, blocking collectives, local(): gathered = lax.all_to_all(stats, 'blk', 0, 0)  10.8 us
    ppermute x7, starting transfers between devices, swap(): return lax.ppermute(value, 'blk', [(i, i ^ mask) for i in range(axis_size)])  8.11 us
    unnamed x6, local copies, waits for them, and re-layouts  2.93 us
    pallas_call x2, Pallas kernels, local(): pl.pallas_call(functools.partial(score_kernel, sources, by_distance, shif...  2.92 us
    ppermute x7, waiting for transfers between devices, swap(): return lax.ppermute(value, 'blk', [(i, i ^ mask) for i in range(axis_size)])  2.69 us
    pallas_call x1, Pallas kernels, local(): pl.pallas_call(functools.partial(slice_kernel, own_rows / per_device, len...  1.77 us
    pallas_call x1, Pallas kernels, local(): pl.pallas_call(pack_kernel, out_shape=jax.ShapeDtypeStruct((1, per_device...  1.26 us
    dynamic_update_slice x1, local copies, waits for them, and re-layouts, local(): pair = lax.dynamic_update_slice(pair, rows, (0, 0, 0))  0.8 us
  transfers between devices with their start and end apart: 7, of which 3 were waited for; matrix products, arithmetic and copies ran while one was open for 5% of the time, Pallas kernels for 10%

profile of v12, /device:TPU:0, one launch (start us, length us, event | category | flops | bytes accessed | tf_op | source)
XLA Modules:
  0.0 33.2 jit_solution(12850040995545074239)
XLA Ops:
  0.6 0.5 %collective-permute-start = (bf16[32,8192]{1,0:T(8,128)(2,1)}, bf16[32,8192]{1,0:T(8,128)(2,1)S(1)}, u32[]{:S(2)}, u32[]{:S(2)}) collective-permute-start(bf16[32,8192]{1,0:T(8,128)(2,1)} %bitcast.5), channel_id=1, source_target_pairs={{0,1},{1,0},{2,3},{3,2},{4,5},{5,4},{6,7},{7,6},{8,9},{9,8},{10,11... | collective-permute-start | bytes 1572872 | tf_op jit(solution)/shard_map/ppermute | solution.py:368
  1.1 2.6 %collective-permute-start.1 = (bf16[1,2,8192]{2,1,0:T(2,128)(2,1)}, bf16[1,2,8192]{2,1,0:T(2,128)(2,1)S(1)}, u32[]{:S(2)}, u32[]{:S(2)}) collective-permute-start(bf16[1,2,8192]{2,1,0:T(2,128)(2,1)} %bitcast.8), channel_id=1, source_target_pairs={{0,2},{1,3},{2,0},{3,1},{4,6},{5,7},{6,4},{7,5},{8,10},{9,11},{10,... | collective-permute-start | bytes 98312 | tf_op jit(solution)/shard_map/ppermute | solution.py:368
  3.7 1.3 %pack.1 = bf16[1,2,128]{2,1,0:T(2,128)(2,1)} custom-call(s32[2]{0:T(128)} %group_hbm.1, s32[2]{0:T(128)} %limit_hbm.1, s32[2,2,9]{2,1,0:T(2,128)} %bitcast.10), custom_call_target="tpu_custom_call" | custom-call | tf_op jit(solution)/shard_map/pack/pallas_call | solution.py:370
  5.0 0.0 collective-permute-done.other_ref
  5.0 0.8 %collective-permute-start.2 = (bf16[1,2,128]{2,1,0:T(2,128)(2,1)}, bf16[1,2,128]{2,1,0:T(2,128)(2,1)S(1)}, u32[]{:S(2)}, u32[]{:S(2)}) collective-permute-start(bf16[1,2,128]{2,1,0:T(2,128)(2,1)} %pack.1), channel_id=1, source_target_pairs={{0,2},{1,3},{2,0},{3,1},{4,6},{5,7},{6,4},{7,5},{8,10},{9,11},{10,... | collective-permute-start | bytes 1544 | tf_op jit(solution)/shard_map/ppermute | solution.py:368
  5.8 0.8 %dynamic_update_slice.12 = bf16[2,2,8320]{2,1,0:T(2,128)(2,1)S(1)} pad(bf16[1,2,8192]{2,1,0:T(2,128)(2,1)} %bitcast.9, bf16[]{:T(256)} %constant.0.clone.1), padding=0_1x0_0x0_128 | pad | bytes 99330 | tf_op jit(solution)/shard_map/dynamic_update_slice | solution.py:426
  6.6 0.7 %constant_dynamic-update-slice_fusion.2 = bf16[2,2,8320]{2,1,0:T(2,128)(2,1)S(1)} fusion(bf16[2,2,8320]{2,1,0:T(2,128)(2,1)S(1)} %dynamic_update_slice.12, bf16[1,2,128]{2,1,0:T(2,128)(2,1)} %pack.1), kind=kLoop, calls=%fused_computation.2 | loop fusion | bytes 1024 | tf_op jit(solution)/shard_map/dynamic_update_slice | solution.py:427
  7.2 0.0 collective-permute-done.1
  7.3 0.0 copy-start.1
  7.3 0.9 %copy-done.1 = f32[16,4096]{1,0:T(8,128)S(1)} copy-done((f32[16,4096]{1,0:T(8,128)S(1)}, f32[16,4096]{1,0:T(8,128)}, u32[]{:S(2)}) %copy-start.1) | copy-done | bytes 262168
  8.2 0.1 ctf.1.refs_5_
  8.3 0.5 %collective-permute-done.2 = bf16[1,2,128]{2,1,0:T(2,128)(2,1)S(1)} collective-permute-done((bf16[1,2,128]{2,1,0:T(2,128)(2,1)}, bf16[1,2,128]{2,1,0:T(2,128)(2,1)S(1)}, u32[]{:S(2)}, u32[]{:S(2)}) %collective-permute-start.2) | collective-permute-done | bytes 544 | tf_op jit(solution)/shard_map/ppermute | solution.py:368
  8.8 1.6 %collective-permute-start.5 = (bf16[2,2,8320]{2,1,0:T(2,128)(2,1)S(1)}, bf16[2,2,8320]{2,1,0:T(2,128)(2,1)S(1)}, u32[]{:S(2)}, u32[]{:S(2)}) collective-permute-start(bf16[2,2,8320]{2,1,0:T(2,128)(2,1)S(1)} %constant_dynamic-update-slice_fusion.refs_0_), channel_id=1, source_target_pairs={{0,4},{1,5},{2,6},{3,7},{4,0},{5,1},{6,2},{7,3},{8,12},{9,13},{10,... | collective-permute-start | bytes 199688 | tf_op jit(solution)/shard_map/ppermute | solution.py:368
  10.3 2.5 %collective-permute-start.4 = (bf16[2,2,8320]{2,1,0:T(2,128)(2,1)S(1)}, bf16[2,2,8320]{2,1,0:T(2,128)(2,1)S(1)}, u32[]{:S(2)}, u32[]{:S(2)}) collective-permute-start(bf16[2,2,8320]{2,1,0:T(2,128)(2,1)S(1)} %constant_dynamic-update-slice_fusion.refs_0_), channel_id=1, source_target_pairs={{0,12},{1,13},{2,14},{3,15},{4,8},{5,9},{6,10},{7,11},{8,4},{9,5},... | collective-permute-start | bytes 199688 | tf_op jit(solution)/shard_map/ppermute | solution.py:368
  12.8 0.1 collective-permute-start.3
  12.9 0.0 copy-start.2
  12.9 0.9 %copy-done.2 = f32[16,4096]{1,0:T(8,128)S(1)} copy-done((f32[16,4096]{1,0:T(8,128)S(1)}, f32[16,4096]{1,0:T(8,128)}, u32[]{:S(2)}) %copy-start.2) | copy-done | bytes 262168
  13.9 0.1 noise.1.refs_6_
  14.0 0.0 copy-start
  14.0 1.0 %copy-done = bf16[2,16,8192]{2,1,0:T(8,128)(2,1)S(1)} copy-done((bf16[2,16,8192]{2,1,0:T(8,128)(2,1)S(1)}, bf16[2,16,8192]{2,1,0:T(8,128)(2,1)}, u32[]{:S(2)}) %copy-start) | copy-done | bytes 524312
  15.0 0.3 power.1
  15.3 0.0 collective-permute-done.5.refs_1_
  15.4 1.4 %scores.2 = (bf16[144,8960]{1,0:T(8,128)(2,1)S(1)}, f32[1,32,72]{2,1,0:T(8,128)S(1)}, f32[1,32,72]{2,1,0:T(8,128)S(1)}, f32[1,1,128]{2,1,0:T(1,128)S(1)}) custom-call(bf16[2,2,8320]{2,1,0:T(2,128)(2,1)S(1)} %constant_dynamic-update-slice_fusion.refs_0_, bf16[2,2,8320]{2,1,0:T(2,128)(2,1)S(1)} %collective-permute-done.5.refs_1_, ...), custom_call_target="tpu_custom_call" | custom-call | flops 84934656 | bytes 1179648 | tf_op jit(solution)/shard_map/scores/pallas_call | solution.py:451
  16.8 0.1 collective-permute-done.4.refs_1_
  16.9 2.1 %collective-permute-done.3.refs_0_ = bf16[2,2,8320]{2,1,0:T(2,128)(2,1)S(1)} collective-permute-done((bf16[2,2,8320]{2,1,0:T(2,128)(2,1)S(1)}, bf16[2,2,8320]{2,1,0:T(2,128)(2,1)S(1)}, u32[]{:S(2)}, u32[]{:S(2)}) %collective-permute-start.3) | collective-permute-done | bytes 66592 | tf_op jit(solution)/shard_map/ppermute | solution.py:368
  19.0 1.5 %scores.3 = (bf16[144,8960]{1,0:T(8,128)(2,1)S(1)}, f32[2,32,72]{2,1,0:T(8,128)S(1)}, f32[16,1,128]{2,1,0:T(1,128)S(1)}) custom-call(bf16[2,2,8320]{2,1,0:T(2,128)(2,1)S(1)} %collective-permute-done.3.refs_0_, bf16[2,2,8320]{2,1,0:T(2,128)(2,1)S(1)} %collective-permute-done.4.refs_1_, ...), custom_call_target="tpu_custom_call", output_to_operand_aliasing={{0}: (7, {})} | custom-call | flops 84934656 | bytes 1179648 | tf_op jit(solution)/shard_map/scores/pallas_call | solution.py:451
  20.5 0.1 collective-permute-start.6
  20.6 10.8 %all_to_all.5 = f32[16,1,128]{2,1,0:T(1,128)S(1)} all-to-all(f32[16,1,128]{2,1,0:T(1,128)S(1)} %get-tuple-element.37), channel_id=1, replica_groups=mesh['groups'=2,'blk'=16] {'blk'}, dimensions={0} | all-to-all | bytes 16384 | tf_op jit(solution)/shard_map/all_to_all | solution.py:486
  31.4 0.0 collective-permute-done.6.refs_3_
  31.4 1.8 %slices.1 = (f32[32,8192]{1,0:T(8,128)}, f32[2]{0:T(128)}, f32[2]{0:T(128)}) custom-call(f32[8,2,1,128]{3,2,1,0:T(1,128)S(1)} %bitcast.7, f32[2,32,72]{2,1,0:T(8,128)S(1)} %get-tuple-element.38.refs_1_, bf16[144,8960]{1,0:T(8,128)(2,1)S(1)} %get-tuple-element.39.refs_2_, bf16[144,8960]{1,0:T(8,128)(2,1)S(1)} %collective-permute-done.6.refs_3_), custom_call_target="tpu_custom_call" | custom-call | tf_op jit(solution)/shard_map/slices/pallas_call | solution.py:489
  (2 shorter events, 0.0 us)
Async XLA Ops:
  0.6 4.4 %collective-permute-start = (bf16[32,8192]{1,0:T(8,128)(2,1)}, bf16[32,8192]{1,0:T(8,128)(2,1)S(1)}, u32[]{:S(2)}, u32[]{:S(2)}) collective-permute-start(bf16[32,8192]{1,0:T(8,128)(2,1)} %bitcast.5), channel_id=1, source_target_pairs={{0,1},{1,0},{2,3},{3,2},{4,5},{5,4},{6,7},{7,6},{8,9},{9,8},{10,11... | collective-permute-start | bytes 1572872 | tf_op jit(solution)/shard_map/ppermute | solution.py:368
  1.1 6.1 %collective-permute-start.1 = (bf16[1,2,8192]{2,1,0:T(2,128)(2,1)}, bf16[1,2,8192]{2,1,0:T(2,128)(2,1)S(1)}, u32[]{:S(2)}, u32[]{:S(2)}) collective-permute-start(bf16[1,2,8192]{2,1,0:T(2,128)(2,1)} %bitcast.8), channel_id=1, source_target_pairs={{0,2},{1,3},{2,0},{3,1},{4,6},{5,7},{6,4},{7,5},{8,10},{9,11},{10,... | collective-permute-start | bytes 98312 | tf_op jit(solution)/shard_map/ppermute | solution.py:368
  5.0 3.7 %collective-permute-start.2 = (bf16[1,2,128]{2,1,0:T(2,128)(2,1)}, bf16[1,2,128]{2,1,0:T(2,128)(2,1)S(1)}, u32[]{:S(2)}, u32[]{:S(2)}) collective-permute-start(bf16[1,2,128]{2,1,0:T(2,128)(2,1)} %pack.1), channel_id=1, source_target_pairs={{0,2},{1,3},{2,0},{3,1},{4,6},{5,7},{6,4},{7,5},{8,10},{9,11},{10,... | collective-permute-start | bytes 1544 | tf_op jit(solution)/shard_map/ppermute | solution.py:368
  7.3 1.0 %copy-start.1 = (f32[16,4096]{1,0:T(8,128)S(1)}, f32[16,4096]{1,0:T(8,128)}, u32[]{:S(2)}) copy-start(f32[16,4096]{1,0:T(8,128)} %values_ref.1) | copy-start | bytes 786436
  8.8 6.6 %collective-permute-start.5 = (bf16[2,2,8320]{2,1,0:T(2,128)(2,1)S(1)}, bf16[2,2,8320]{2,1,0:T(2,128)(2,1)S(1)}, u32[]{:S(2)}, u32[]{:S(2)}) collective-permute-start(bf16[2,2,8320]{2,1,0:T(2,128)(2,1)S(1)} %constant_dynamic-update-slice_fusion.refs_0_), channel_id=1, source_target_pairs={{0,4},{1,5},{2,6},{3,7},{4,0},{5,1},{6,2},{7,3},{8,12},{9,13},{10,... | collective-permute-start | bytes 199688 | tf_op jit(solution)/shard_map/ppermute | solution.py:368
  10.3 6.5 %collective-permute-start.4 = (bf16[2,2,8320]{2,1,0:T(2,128)(2,1)S(1)}, bf16[2,2,8320]{2,1,0:T(2,128)(2,1)S(1)}, u32[]{:S(2)}, u32[]{:S(2)}) collective-permute-start(bf16[2,2,8320]{2,1,0:T(2,128)(2,1)S(1)} %constant_dynamic-update-slice_fusion.refs_0_), channel_id=1, source_target_pairs={{0,12},{1,13},{2,14},{3,15},{4,8},{5,9},{6,10},{7,11},{8,4},{9,5},... | collective-permute-start | bytes 199688 | tf_op jit(solution)/shard_map/ppermute | solution.py:368
  12.8 6.2 %collective-permute-start.3 = (bf16[2,2,8320]{2,1,0:T(2,128)(2,1)S(1)}, bf16[2,2,8320]{2,1,0:T(2,128)(2,1)S(1)}, u32[]{:S(2)}, u32[]{:S(2)}) collective-permute-start(bf16[2,2,8320]{2,1,0:T(2,128)(2,1)S(1)} %constant_dynamic-update-slice_fusion.refs_0_), channel_id=1, source_target_pairs={{0,8},{1,9},{2,10},{3,11},{4,12},{5,13},{6,14},{7,15},{8,0},{9,1},... | collective-permute-start | bytes 199688 | tf_op jit(solution)/shard_map/ppermute | solution.py:368
  12.9 0.9 %copy-start.2 = (f32[16,4096]{1,0:T(8,128)S(1)}, f32[16,4096]{1,0:T(8,128)}, u32[]{:S(2)}) copy-start(f32[16,4096]{1,0:T(8,128)} %values_ref.2) | copy-start | bytes 786436
  14.0 1.0 %copy-start = (bf16[2,16,8192]{2,1,0:T(8,128)(2,1)S(1)}, bf16[2,16,8192]{2,1,0:T(8,128)(2,1)}, u32[]{:S(2)}) copy-start(bf16[2,16,8192]{2,1,0:T(8,128)(2,1)} %param.7) | copy-start | bytes 1572868
  20.5 10.9 %collective-permute-start.6 = (bf16[144,8960]{1,0:T(8,128)(2,1)S(1)}, bf16[144,8960]{1,0:T(8,128)(2,1)S(1)}, u32[]{:S(2)}, u32[]{:S(2)}) collective-permute-start(bf16[144,8960]{1,0:T(8,128)(2,1)S(1)} %get-tuple-element.39.refs_2_), channel_id=1, source_target_pairs={{0,1},{1,0},{2,3},{3,2},{4,5},{5,4},{6,7},{7,6},{8,9},{9,8},{10,11... | collective-permute-start | bytes 7741448 | tf_op jit(solution)/shard_map/ppermute | solution.py:368
